TPU v7x, 256 devices: a whole 4x4x8 slice. The times are simulated.
256 devices in a mesh: gx: 8 (over z_hi, core), gy: 4 (over y), gz: 8 (over z_lo, x).
Axes of the slice: x: 4, y: 4, z: 8 (z_hi: 4, z_lo: 2; z = z_hi * 2 + z_lo), core: 2. Of those that a mesh axis runs over, the one named last changes fastest.
Arguments:
- pressure_now: float32 [128, 256, 1024], P('gx', 'gy', 'gz'), may hold values from -6 to 6
- pressure_prev: float32 [128, 256, 1024], P('gx', 'gy', 'gz'), may hold values from -6 to 6
- boundary_mask: int32 [128, 256, 1024], P('gx', 'gy', 'gz'), may hold values 0 or 1
- writer: int32 [8, 4], P('gx', 'gy'), may hold values from 0 to 7
Outputs:
- pressure: float32 [128, 256, 1024], P('gx', 'gy', 'gz')
- collected: float32 [8, 64, 128, 512], P('gz', 'gx', 'gy')
All inputs are finite; a program needn't handle non-finite values. No bound on the sum of `boundary_mask` on one device may be relied on, other than what follows from the above.
Results may differ from a plain program's by a relative error of at most 0.00017.
Values sent between devices are 32-bit elements; how exact they have to be, the bound alone decides.
No kernel may reach another device: no remote copies, remote signals or barrier semaphores. Data moves between devices by JAX's collectives and lax.ppermute only.
A program may use at most 64 MiB of HBM per device.

v0:
```python
import jax
import jax.numpy as jnp
from jax import lax
from jax.sharding import PartitionSpec as P

ITERS = 4


def padded_2(shard, sides, width):
    for axis, dim in sides:
        count, length = (lax.axis_size(axis), shard.shape[dim])
        up = [(i, (i + 1) % count) for i in range(count - 1)]
        down = [(j, i) for i, j in up]
        last = lax.slice_in_dim(shard, length - width, length, axis=dim)
        leading = lax.slice_in_dim(shard, 0, width, axis=dim)
        before = lax.ppermute(last, axis, up)
        after = lax.ppermute(leading, axis, down)
        shard = jnp.concatenate([before, shard, after], axis=dim)
    return shard


def brick_matrix(length):
    rows = jnp.arange(length)[:, None]
    cols = jnp.arange(length // 2)[None, :]
    freq = (cols % 4).astype(jnp.float32)
    place = (rows % 8).astype(jnp.float32)
    scale = jnp.where(
        cols % 4 == 0, jnp.sqrt(jnp.float32(1.0 / 8.0)), jnp.sqrt(jnp.float32(2.0 / 8.0))
    )
    values = scale * jnp.cos(jnp.float32(jnp.pi) * (2.0 * place + 1.0) * freq / 16.0)
    return jnp.where(rows // 8 == cols // 4, values, jnp.float32(0.0))


def neighbours(padded):
    total = padded[2:, 1:-1, 1:-1] + padded[:-2, 1:-1, 1:-1]
    total = total + padded[1:-1, 2:, 1:-1] + padded[1:-1, :-2, 1:-1]
    total = total + padded[1:-1, 1:-1, 2:] + padded[1:-1, 1:-1, :-2]
    return total


def advance(padded, previous, weights):
    return (neighbours(padded) / 3.0 - previous) * (1.0 - 0.5 * weights)


def per_device(pressure_now, pressure_prev, boundary_mask, writer):
    weights = boundary_mask.astype(jnp.float32)
    current, previous = (pressure_now, pressure_prev)
    for turn_index in range(ITERS):
        padded = padded_2(current, (("gx", 0), ("gy", 1), ("gz", 2)), 1)
        following = advance(padded, previous, weights)
        previous = current
        current = following
    size_x, size_y, size_z = current.shape
    highest = lax.Precision.HIGHEST
    coef = jnp.einsum("xyz,zc->xyc", current, brick_matrix(size_z), precision=highest)
    coef = jnp.einsum("xyc,yb->xbc", coef, brick_matrix(size_y), precision=highest)
    coef = jnp.einsum("xbc,xa->abc", coef, brick_matrix(size_x), precision=highest)
    writer_index = writer[0, 0]
    own_index = lax.axis_index("gz")
    gathered = lax.all_gather(coef, "gz", axis=2, tiled=True)
    collected = jnp.where(own_index == writer_index, gathered, jnp.float32(0.0))[None]
    return (current, collected)


def solution(mesh):
    return jax.shard_map(
        per_device,
        mesh=mesh,
        in_specs=(P("gx", "gy", "gz"), P("gx", "gy", "gz"), P("gx", "gy", "gz"), P("gx", "gy")),
        out_specs=(P("gx", "gy", "gz"), P("gz", "gx", "gy", None)),
        check_vma=False,
    )
```

profile of v0, /device:TPU:176, one launch (start us, length us, event | category | flops | bytes accessed | tf_op | source)
XLA Modules:
  0.0 222.3 jit_solution(13542855713082414322)
XLA Ops:
  3.3 5.8 %collective-permute-start = (f32[1,64,128]{2,1,0:T(8,128)S(1)}, f32[1,64,128]{2,1,0:T(8,128)S(1)}, u32[]{:S(2)}, u32[]{:S(2)}) collective-permute-start(f32[1,64,128]{2,1,0:T(8,128)S(1)} %get-tuple-element.37), channel_id=1, source_target_pairs={{32,0},{64,32},{96,64},{128,96},{160,128},{192,160},{224,192},{33,... | collective-permute-start | bytes 98312 | tf_op jit(solution)/shard_map/ppermute | solution.py:17
  10.7 2.5 %pad_maximum_fusion.65 = (f32[16,64,128]{2,1,0:T(8,128)S(1)}, f32[16,64,128]{2,1,0:T(8,128)}, f32[18,64,128]{2,1,0:T(8,128)S(1)}) fusion(f32[16,64,128]{2,1,0:T(8,128)} %param.4, f32[1,64,128]{2,1,0:T(8,128)S(1)} %collective-permute-done.1, f32[1,64,128]{2,1,0:T(8,128)S(1)} %collective-permute-done, f32[18,64,128]{2,1,0:T(8,128)S(1)} %constant_dynamic-update-slice_fusion.2), kind=kLoop, calls=%fused_computation.99 | loop fusion | flops 262144 | bytes 2162688 | tf_op jit(solution)/shard_map/concatenate | solution.py:18
  15.6 3.5 %collective-permute-start.3 = (f32[18,1,128]{2,0,1:T(8,128)S(1)}, f32[18,1,128]{2,0,1:T(8,128)S(1)}, u32[]{:S(2)}, u32[]{:S(2)}) collective-permute-start(f32[18,1,128]{2,0,1:T(8,128)S(1)} %copy.177), channel_id=1, source_target_pairs={{0,8},{8,16},{16,24},{1,9},{9,17},{17,25},{2,10},{10,18},{18,26},{... | collective-permute-start | bytes 27656 | tf_op jit(solution)/shard_map/ppermute | solution.py:16
  23.8 5.1 %collective-permute-start.4 = (f32[18,66,1]{1,0,2:T(8,128)S(1)}, f32[18,66,1]{1,0,2:T(8,128)S(1)}, u32[]{:S(2)}, u32[]{:S(2)}) collective-permute-start(f32[18,66,1]{1,0,2:T(8,128)S(1)} %get-tuple-element.12), channel_id=1, source_target_pairs={{1,0},{2,1},{3,2},{4,3},{5,4},{6,5},{7,6},{9,8},{10,9},{11,10},{12... | collective-permute-start | bytes 14264 | tf_op jit(solution)/shard_map/ppermute | solution.py:17
  36.9 9.3 %fusion.27 = f32[16,64,128]{1,0,2:T(8,128)S(1)} fusion(f32[16,64,128]{1,0,2:T(8,128)S(1)} %copy.145, f32[18,66,1]{1,0,2:T(8,128)S(1)} %collective-permute-done.5, f32[18,1,128]{1,0,2:T(8,128)} %copy-done.4, f32[18,64,128]{1,0,2:T(8,128)} %copy.137, f32[18,1,128]{1,0,2:T(8,128)} %copy.140, f32[18,66,1]{1,0,2:T(8,128)S(1)} %collective-permute-done.4, ...), kind=kLoop, calls=%fused_computation.87 | loop fusion | flops 2490368 | bytes 3239200 | tf_op jit(solution)/shard_map/mul | solution.py:42
  46.3 4.9 %collective-permute-start.6 = (f32[1,64,128]{1,0,2:T(1,128)S(1)}, f32[1,64,128]{1,0,2:T(1,128)S(1)}, u32[]{:S(2)}, u32[]{:S(2)}) collective-permute-start(f32[1,64,128]{1,0,2:T(1,128)S(1)} %get-tuple-element.31), channel_id=1, source_target_pairs={{32,0},{64,32},{96,64},{128,96},{160,128},{192,160},{224,192},{33,... | collective-permute-start | bytes 98312 | tf_op jit(solution)/shard_map/ppermute | solution.py:17
  53.2 5.7 %collective-permute-done.7 = f32[1,64,128]{1,0,2:T(1,128)S(1)} collective-permute-done((f32[1,64,128]{1,0,2:T(1,128)S(1)}, f32[1,64,128]{1,0,2:T(1,128)S(1)}, u32[]{:S(2)}, u32[]{:S(2)}) %collective-permute-start.7) | collective-permute-done | bytes 32800 | tf_op jit(solution)/shard_map/ppermute | solution.py:16
  67.5 3.5 %collective-permute-start.9 = (f32[18,1,128]{2,0,1:T(8,128)S(1)}, f32[18,1,128]{2,0,1:T(8,128)S(1)}, u32[]{:S(2)}, u32[]{:S(2)}) collective-permute-start(f32[18,1,128]{2,0,1:T(8,128)S(1)} %copy.149), channel_id=1, source_target_pairs={{0,8},{8,16},{16,24},{1,9},{9,17},{17,25},{2,10},{10,18},{18,26},{... | collective-permute-start | bytes 27656 | tf_op jit(solution)/shard_map/ppermute | solution.py:16
  75.7 5.8 %collective-permute-start.10 = (f32[18,66,1]{1,0,2:T(8,128)S(1)}, f32[18,66,1]{1,0,2:T(8,128)S(1)}, u32[]{:S(2)}, u32[]{:S(2)}) collective-permute-start(f32[18,66,1]{1,0,2:T(8,128)S(1)} %get-tuple-element.18), channel_id=1, source_target_pairs={{1,0},{2,1},{3,2},{4,3},{5,4},{6,5},{7,6},{9,8},{10,9},{11,10},{12... | collective-permute-start | bytes 14264 | tf_op jit(solution)/shard_map/ppermute | solution.py:17
  84.8 4.4 %collective-permute-done.11 = f32[18,66,1]{1,0,2:T(8,128)S(1)} collective-permute-done((f32[18,66,1]{1,0,2:T(8,128)S(1)}, f32[18,66,1]{1,0,2:T(8,128)S(1)}, u32[]{:S(2)}, u32[]{:S(2)}) %collective-permute-start.11) | collective-permute-done | bytes 4784 | tf_op jit(solution)/shard_map/ppermute | solution.py:16
  89.2 8.7 %fusion.19 = f32[16,64,128]{1,0,2:T(8,128)S(1)} fusion(f32[16,64,128]{1,0,2:T(8,128)} %copy.153, f32[18,66,1]{1,0,2:T(8,128)S(1)} %collective-permute-done.11, f32[18,1,128]{1,0,2:T(8,128)} %copy.148, f32[18,1,128]{1,0,2:T(8,128)} %copy.150, f32[1,64,128]{1,0,2:T(1,128)S(1)} %collective-permute-done.6, f32[16,64,128]{1,0,2:T(8,128)S(1)} %fusion.27, ...), kind=kLoop, calls=%fused_computation.61 | loop fusion | flops 3801088 | bytes 2190624 | tf_op jit(solution)/shard_map/mul | solution.py:42
  99.9 2.6 %collective-permute-start.13 = (f32[1,64,128]{1,0,2:T(1,128)S(1)}, f32[1,64,128]{1,0,2:T(1,128)S(1)}, u32[]{:S(2)}, u32[]{:S(2)}) collective-permute-start(f32[1,64,128]{1,0,2:T(1,128)S(1)} %get-tuple-element.28), channel_id=1, source_target_pairs={{0,32},{32,64},{64,96},{96,128},{128,160},{160,192},{192,224},{1,3... | collective-permute-start | bytes 98312 | tf_op jit(solution)/shard_map/ppermute | solution.py:16
  102.5 5.1 %collective-permute-done.13 = f32[1,64,128]{1,0,2:T(1,128)S(1)} collective-permute-done((f32[1,64,128]{1,0,2:T(1,128)S(1)}, f32[1,64,128]{1,0,2:T(1,128)S(1)}, u32[]{:S(2)}, u32[]{:S(2)}) %collective-permute-start.13) | collective-permute-done | bytes 32800 | tf_op jit(solution)/shard_map/ppermute | solution.py:16
  116.2 3.5 %collective-permute-start.15 = (f32[18,1,128]{2,0,1:T(8,128)S(1)}, f32[18,1,128]{2,0,1:T(8,128)S(1)}, u32[]{:S(2)}, u32[]{:S(2)}) collective-permute-start(f32[18,1,128]{2,0,1:T(8,128)S(1)} %copy.156), channel_id=1, source_target_pairs={{0,8},{8,16},{16,24},{1,9},{9,17},{17,25},{2,10},{10,18},{18,26},{... | collective-permute-start | bytes 27656 | tf_op jit(solution)/shard_map/ppermute | solution.py:16
  126.4 3.9 %collective-permute-start.17 = (f32[18,66,1]{1,0,2:T(8,128)S(1)}, f32[18,66,1]{1,0,2:T(8,128)S(1)}, u32[]{:S(2)}, u32[]{:S(2)}) collective-permute-start(f32[18,66,1]{1,0,2:T(8,128)S(1)} %get-tuple-element.17), channel_id=1, source_target_pairs={{0,1},{1,2},{2,3},{3,4},{4,5},{5,6},{6,7},{8,9},{9,10},{10,11},{11... | collective-permute-start | bytes 14264 | tf_op jit(solution)/shard_map/ppermute | solution.py:16
  130.3 3.7 %collective-permute-done.17 = f32[18,66,1]{1,0,2:T(8,128)S(1)} collective-permute-done((f32[18,66,1]{1,0,2:T(8,128)S(1)}, f32[18,66,1]{1,0,2:T(8,128)S(1)}, u32[]{:S(2)}, u32[]{:S(2)}) %collective-permute-start.17) | collective-permute-done | bytes 4784 | tf_op jit(solution)/shard_map/ppermute | solution.py:16
  134.1 4.5 %fusion.11 = f32[16,64,128]{1,0,2:T(8,128)S(1)} fusion(f32[16,64,128]{1,0,2:T(8,128)S(1)} %fusion.27, f32[18,66,1]{1,0,2:T(8,128)S(1)} %collective-permute-done.17, f32[18,1,128]{1,0,2:T(8,128)S(1)} %copy-done.2, f32[18,1,128]{1,0,2:T(8,128)S(1)} %copy-done.3, f32[1,64,128]{1,0,2:T(1,128)S(1)} %collective-permute-done.12, f32[16,64,128]{1,0,2:T(8,128)S(1)} %fusion.19, ...), kind=kLoop, calls=%fused_computation.35 | loop fusion | flops 3801088 | bytes 2190624 | tf_op jit(solution)/shard_map/mul | solution.py:42
  140.6 2.4 %collective-permute-start.19 = (f32[1,64,128]{1,0,2:T(1,128)S(1)}, f32[1,64,128]{1,0,2:T(1,128)S(1)}, u32[]{:S(2)}, u32[]{:S(2)}) collective-permute-start(f32[1,64,128]{1,0,2:T(1,128)S(1)} %get-tuple-element.26), channel_id=1, source_target_pairs={{0,32},{32,64},{64,96},{96,128},{128,160},{160,192},{192,224},{1,3... | collective-permute-start | bytes 98312 | tf_op jit(solution)/shard_map/ppermute | solution.py:16
  143.1 5.3 %collective-permute-done.19 = f32[1,64,128]{1,0,2:T(1,128)S(1)} collective-permute-done((f32[1,64,128]{1,0,2:T(1,128)S(1)}, f32[1,64,128]{1,0,2:T(1,128)S(1)}, u32[]{:S(2)}, u32[]{:S(2)}) %collective-permute-start.19) | collective-permute-done | bytes 32800 | tf_op jit(solution)/shard_map/ppermute | solution.py:16
  156.5 3.9 %collective-permute-start.21 = (f32[18,1,128]{2,0,1:T(8,128)S(1)}, f32[18,1,128]{2,0,1:T(8,128)S(1)}, u32[]{:S(2)}, u32[]{:S(2)}) collective-permute-start(f32[18,1,128]{2,0,1:T(8,128)S(1)} %copy.162), channel_id=1, source_target_pairs={{0,8},{8,16},{16,24},{1,9},{9,17},{17,25},{2,10},{10,18},{18,26},{... | collective-permute-start | bytes 27656 | tf_op jit(solution)/shard_map/ppermute | solution.py:16
  166.6 4.1 %collective-permute-start.23 = (f32[18,66,1]{1,0,2:T(8,128)S(1)}, f32[18,66,1]{1,0,2:T(8,128)S(1)}, u32[]{:S(2)}, u32[]{:S(2)}) collective-permute-start(f32[18,66,1]{1,0,2:T(8,128)S(1)} %get-tuple-element.15), channel_id=1, source_target_pairs={{0,1},{1,2},{2,3},{3,4},{4,5},{5,6},{6,7},{8,9},{9,10},{10,11},{11... | collective-permute-start | bytes 14264 | tf_op jit(solution)/shard_map/ppermute | solution.py:16
  171.4 2.9 %collective-permute-done.23 = f32[18,66,1]{1,0,2:T(8,128)S(1)} collective-permute-done((f32[18,66,1]{1,0,2:T(8,128)S(1)}, f32[18,66,1]{1,0,2:T(8,128)S(1)}, u32[]{:S(2)}, u32[]{:S(2)}) %collective-permute-start.23) | collective-permute-done | bytes 4784 | tf_op jit(solution)/shard_map/ppermute | solution.py:16
  174.3 9.1 %fusion.3 = f32[16,64,128]{1,0,2:T(8,128)} fusion(f32[16,64,128]{1,0,2:T(8,128)S(1)} %fusion.19, f32[18,66,1]{1,0,2:T(8,128)S(1)} %collective-permute-done.23, f32[18,1,128]{1,0,2:T(8,128)} %copy.161, f32[18,1,128]{1,0,2:T(8,128)} %copy.163, f32[1,64,128]{1,0,2:T(1,128)S(1)} %collective-permute-done.18, f32[16,64,128]{1,0,2:T(8,128)S(1)} %copy-done.1, ...), kind=kLoop, calls=%fused_computation.9 | loop fusion | flops 3801088 | bytes 2190624 | tf_op jit(solution)/shard_map/mul | solution.py:42
  187.1 33.6 %all_gather.3 = f32[8,32,512]{1,0,2:T(8,128)S(1)} all-gather(f32[8,32,64]{1,0,2:T(8,128)S(1)} %fusion.60), channel_id=1, replica_groups=mesh['gx'=8,'gy'=4,'gz'=8] {'gz'}, dimensions={2}, use_global_device_ids=true | all-gather | bytes 589824 | tf_op jit(solution)/shard_map/all_gather | solution.py:60
  (104 shorter events, 76.7 us)
Async XLA Ops:
  1.4 7.7 %collective-permute-start.1 = (f32[1,64,128]{2,1,0:T(8,128)S(1)}, f32[1,64,128]{2,1,0:T(8,128)S(1)}, u32[]{:S(2)}, u32[]{:S(2)}) collective-permute-start(f32[1,64,128]{2,1,0:T(8,128)S(1)} %get-tuple-element.38), channel_id=1, source_target_pairs={{0,32},{32,64},{64,96},{96,128},{128,160},{160,192},{192,224},{1,3... | collective-permute-start | bytes 98312 | tf_op jit(solution)/shard_map/ppermute | solution.py:16
  3.3 7.3 %collective-permute-start = (f32[1,64,128]{2,1,0:T(8,128)S(1)}, f32[1,64,128]{2,1,0:T(8,128)S(1)}, u32[]{:S(2)}, u32[]{:S(2)}) collective-permute-start(f32[1,64,128]{2,1,0:T(8,128)S(1)} %get-tuple-element.37), channel_id=1, source_target_pairs={{32,0},{64,32},{96,64},{128,96},{160,128},{192,160},{224,192},{33,... | collective-permute-start | bytes 98312 | tf_op jit(solution)/shard_map/ppermute | solution.py:17
  13.2 7.5 %collective-permute-start.2 = (f32[18,1,128]{2,0,1:T(8,128)S(1)}, f32[18,1,128]{2,0,1:T(8,128)S(1)}, u32[]{:S(2)}, u32[]{:S(2)}) collective-permute-start(f32[18,1,128]{2,0,1:T(8,128)S(1)} %copy.176), channel_id=1, source_target_pairs={{8,0},{16,8},{24,16},{9,1},{17,9},{25,17},{10,2},{18,10},{26,18},{... | collective-permute-start | bytes 27656 | tf_op jit(solution)/shard_map/ppermute | solution.py:17
  15.6 5.7 %collective-permute-start.3 = (f32[18,1,128]{2,0,1:T(8,128)S(1)}, f32[18,1,128]{2,0,1:T(8,128)S(1)}, u32[]{:S(2)}, u32[]{:S(2)}) collective-permute-start(f32[18,1,128]{2,0,1:T(8,128)S(1)} %copy.177), channel_id=1, source_target_pairs={{0,8},{8,16},{16,24},{1,9},{9,17},{17,25},{2,10},{10,18},{18,26},{... | collective-permute-start | bytes 27656 | tf_op jit(solution)/shard_map/ppermute | solution.py:16
  23.8 13.0 %collective-permute-start.4 = (f32[18,66,1]{1,0,2:T(8,128)S(1)}, f32[18,66,1]{1,0,2:T(8,128)S(1)}, u32[]{:S(2)}, u32[]{:S(2)}) collective-permute-start(f32[18,66,1]{1,0,2:T(8,128)S(1)} %get-tuple-element.12), channel_id=1, source_target_pairs={{1,0},{2,1},{3,2},{4,3},{5,4},{6,5},{7,6},{9,8},{10,9},{11,10},{12... | collective-permute-start | bytes 14264 | tf_op jit(solution)/shard_map/ppermute | solution.py:17
  29.0 7.9 %collective-permute-start.5 = (f32[18,66,1]{1,0,2:T(8,128)S(1)}, f32[18,66,1]{1,0,2:T(8,128)S(1)}, u32[]{:S(2)}, u32[]{:S(2)}) collective-permute-start(f32[18,66,1]{1,0,2:T(8,128)S(1)} %get-tuple-element.13), channel_id=1, source_target_pairs={{0,1},{1,2},{2,3},{3,4},{4,5},{5,6},{6,7},{8,9},{9,10},{10,11},{11... | collective-permute-start | bytes 14264 | tf_op jit(solution)/shard_map/ppermute | solution.py:16
  46.3 6.9 %collective-permute-start.6 = (f32[1,64,128]{1,0,2:T(1,128)S(1)}, f32[1,64,128]{1,0,2:T(1,128)S(1)}, u32[]{:S(2)}, u32[]{:S(2)}) collective-permute-start(f32[1,64,128]{1,0,2:T(1,128)S(1)} %get-tuple-element.31), channel_id=1, source_target_pairs={{32,0},{64,32},{96,64},{128,96},{160,128},{192,160},{224,192},{33,... | collective-permute-start | bytes 98312 | tf_op jit(solution)/shard_map/ppermute | solution.py:17
  51.2 7.7 %collective-permute-start.7 = (f32[1,64,128]{1,0,2:T(1,128)S(1)}, f32[1,64,128]{1,0,2:T(1,128)S(1)}, u32[]{:S(2)}, u32[]{:S(2)}) collective-permute-start(f32[1,64,128]{1,0,2:T(1,128)S(1)} %get-tuple-element.30), channel_id=1, source_target_pairs={{0,32},{32,64},{64,96},{96,128},{128,160},{160,192},{192,224},{1,3... | collective-permute-start | bytes 98312 | tf_op jit(solution)/shard_map/ppermute | solution.py:16
  63.3 7.8 %collective-permute-start.8 = (f32[18,1,128]{2,0,1:T(8,128)S(1)}, f32[18,1,128]{2,0,1:T(8,128)S(1)}, u32[]{:S(2)}, u32[]{:S(2)}) collective-permute-start(f32[18,1,128]{2,0,1:T(8,128)S(1)} %copy.147), channel_id=1, source_target_pairs={{8,0},{16,8},{24,16},{9,1},{17,9},{25,17},{10,2},{18,10},{26,18},{... | collective-permute-start | bytes 27656 | tf_op jit(solution)/shard_map/ppermute | solution.py:17
  67.5 5.6 %collective-permute-start.9 = (f32[18,1,128]{2,0,1:T(8,128)S(1)}, f32[18,1,128]{2,0,1:T(8,128)S(1)}, u32[]{:S(2)}, u32[]{:S(2)}) collective-permute-start(f32[18,1,128]{2,0,1:T(8,128)S(1)} %copy.149), channel_id=1, source_target_pairs={{0,8},{8,16},{16,24},{1,9},{9,17},{17,25},{2,10},{10,18},{18,26},{... | collective-permute-start | bytes 27656 | tf_op jit(solution)/shard_map/ppermute | solution.py:16
  75.7 9.1 %collective-permute-start.10 = (f32[18,66,1]{1,0,2:T(8,128)S(1)}, f32[18,66,1]{1,0,2:T(8,128)S(1)}, u32[]{:S(2)}, u32[]{:S(2)}) collective-permute-start(f32[18,66,1]{1,0,2:T(8,128)S(1)} %get-tuple-element.18), channel_id=1, source_target_pairs={{1,0},{2,1},{3,2},{4,3},{5,4},{6,5},{7,6},{9,8},{10,9},{11,10},{12... | collective-permute-start | bytes 14264 | tf_op jit(solution)/shard_map/ppermute | solution.py:17
  81.5 7.7 %collective-permute-start.11 = (f32[18,66,1]{1,0,2:T(8,128)S(1)}, f32[18,66,1]{1,0,2:T(8,128)S(1)}, u32[]{:S(2)}, u32[]{:S(2)}) collective-permute-start(f32[18,66,1]{1,0,2:T(8,128)S(1)} %get-tuple-element.19), channel_id=1, source_target_pairs={{0,1},{1,2},{2,3},{3,4},{4,5},{5,6},{6,7},{8,9},{9,10},{10,11},{11... | collective-permute-start | bytes 14264 | tf_op jit(solution)/shard_map/ppermute | solution.py:16
  98.0 4.5 %collective-permute-start.12 = (f32[1,64,128]{1,0,2:T(1,128)S(1)}, f32[1,64,128]{1,0,2:T(1,128)S(1)}, u32[]{:S(2)}, u32[]{:S(2)}) collective-permute-start(f32[1,64,128]{1,0,2:T(1,128)S(1)} %get-tuple-element.29), channel_id=1, source_target_pairs={{32,0},{64,32},{96,64},{128,96},{160,128},{192,160},{224,192},{33,... | collective-permute-start | bytes 98312 | tf_op jit(solution)/shard_map/ppermute | solution.py:17
  99.9 7.7 %collective-permute-start.13 = (f32[1,64,128]{1,0,2:T(1,128)S(1)}, f32[1,64,128]{1,0,2:T(1,128)S(1)}, u32[]{:S(2)}, u32[]{:S(2)}) collective-permute-start(f32[1,64,128]{1,0,2:T(1,128)S(1)} %get-tuple-element.28), channel_id=1, source_target_pairs={{0,32},{32,64},{64,96},{96,128},{128,160},{160,192},{192,224},{1,3... | collective-permute-start | bytes 98312 | tf_op jit(solution)/shard_map/ppermute | solution.py:16
  111.9 7.8 %collective-permute-start.14 = (f32[18,1,128]{2,0,1:T(8,128)S(1)}, f32[18,1,128]{2,0,1:T(8,128)S(1)}, u32[]{:S(2)}, u32[]{:S(2)}) collective-permute-start(f32[18,1,128]{2,0,1:T(8,128)S(1)} %copy.154), channel_id=1, source_target_pairs={{8,0},{16,8},{24,16},{9,1},{17,9},{25,17},{10,2},{18,10},{26,18},{... | collective-permute-start | bytes 27656 | tf_op jit(solution)/shard_map/ppermute | solution.py:17
  116.2 5.6 %collective-permute-start.15 = (f32[18,1,128]{2,0,1:T(8,128)S(1)}, f32[18,1,128]{2,0,1:T(8,128)S(1)}, u32[]{:S(2)}, u32[]{:S(2)}) collective-permute-start(f32[18,1,128]{2,0,1:T(8,128)S(1)} %copy.156), channel_id=1, source_target_pairs={{0,8},{8,16},{16,24},{1,9},{9,17},{17,25},{2,10},{10,18},{18,26},{... | collective-permute-start | bytes 27656 | tf_op jit(solution)/shard_map/ppermute | solution.py:16
  124.4 5.9 %collective-permute-start.16 = (f32[18,66,1]{1,0,2:T(8,128)S(1)}, f32[18,66,1]{1,0,2:T(8,128)S(1)}, u32[]{:S(2)}, u32[]{:S(2)}) collective-permute-start(f32[18,66,1]{1,0,2:T(8,128)S(1)} %get-tuple-element.16), channel_id=1, source_target_pairs={{1,0},{2,1},{3,2},{4,3},{5,4},{6,5},{7,6},{9,8},{10,9},{11,10},{12... | collective-permute-start | bytes 14264 | tf_op jit(solution)/shard_map/ppermute | solution.py:17
  126.4 7.7 %collective-permute-start.17 = (f32[18,66,1]{1,0,2:T(8,128)S(1)}, f32[18,66,1]{1,0,2:T(8,128)S(1)}, u32[]{:S(2)}, u32[]{:S(2)}) collective-permute-start(f32[18,66,1]{1,0,2:T(8,128)S(1)} %get-tuple-element.17), channel_id=1, source_target_pairs={{0,1},{1,2},{2,3},{3,4},{4,5},{5,6},{6,7},{8,9},{9,10},{10,11},{11... | collective-permute-start | bytes 14264 | tf_op jit(solution)/shard_map/ppermute | solution.py:16
  138.7 4.4 %collective-permute-start.18 = (f32[1,64,128]{1,0,2:T(1,128)S(1)}, f32[1,64,128]{1,0,2:T(1,128)S(1)}, u32[]{:S(2)}, u32[]{:S(2)}) collective-permute-start(f32[1,64,128]{1,0,2:T(1,128)S(1)} %get-tuple-element.27), channel_id=1, source_target_pairs={{32,0},{64,32},{96,64},{128,96},{160,128},{192,160},{224,192},{33,... | collective-permute-start | bytes 98312 | tf_op jit(solution)/shard_map/ppermute | solution.py:17
  140.6 7.7 %collective-permute-start.19 = (f32[1,64,128]{1,0,2:T(1,128)S(1)}, f32[1,64,128]{1,0,2:T(1,128)S(1)}, u32[]{:S(2)}, u32[]{:S(2)}) collective-permute-start(f32[1,64,128]{1,0,2:T(1,128)S(1)} %get-tuple-element.26), channel_id=1, source_target_pairs={{0,32},{32,64},{64,96},{96,128},{128,160},{160,192},{192,224},{1,3... | collective-permute-start | bytes 98312 | tf_op jit(solution)/shard_map/ppermute | solution.py:16
  152.7 7.8 %collective-permute-start.20 = (f32[18,1,128]{2,0,1:T(8,128)S(1)}, f32[18,1,128]{2,0,1:T(8,128)S(1)}, u32[]{:S(2)}, u32[]{:S(2)}) collective-permute-start(f32[18,1,128]{2,0,1:T(8,128)S(1)} %copy.160), channel_id=1, source_target_pairs={{8,0},{16,8},{24,16},{9,1},{17,9},{25,17},{10,2},{18,10},{26,18},{... | collective-permute-start | bytes 27656 | tf_op jit(solution)/shard_map/ppermute | solution.py:17
  156.5 5.6 %collective-permute-start.21 = (f32[18,1,128]{2,0,1:T(8,128)S(1)}, f32[18,1,128]{2,0,1:T(8,128)S(1)}, u32[]{:S(2)}, u32[]{:S(2)}) collective-permute-start(f32[18,1,128]{2,0,1:T(8,128)S(1)} %copy.162), channel_id=1, source_target_pairs={{0,8},{8,16},{16,24},{1,9},{9,17},{17,25},{2,10},{10,18},{18,26},{... | collective-permute-start | bytes 27656 | tf_op jit(solution)/shard_map/ppermute | solution.py:16
  164.7 6.7 %collective-permute-start.22 = (f32[18,66,1]{1,0,2:T(8,128)S(1)}, f32[18,66,1]{1,0,2:T(8,128)S(1)}, u32[]{:S(2)}, u32[]{:S(2)}) collective-permute-start(f32[18,66,1]{1,0,2:T(8,128)S(1)} %get-tuple-element.14), channel_id=1, source_target_pairs={{1,0},{2,1},{3,2},{4,3},{5,4},{6,5},{7,6},{9,8},{10,9},{11,10},{12... | collective-permute-start | bytes 14264 | tf_op jit(solution)/shard_map/ppermute | solution.py:17
  166.6 7.7 %collective-permute-start.23 = (f32[18,66,1]{1,0,2:T(8,128)S(1)}, f32[18,66,1]{1,0,2:T(8,128)S(1)}, u32[]{:S(2)}, u32[]{:S(2)}) collective-permute-start(f32[18,66,1]{1,0,2:T(8,128)S(1)} %get-tuple-element.15), channel_id=1, source_target_pairs={{0,1},{1,2},{2,3},{3,4},{4,5},{5,6},{6,7},{8,9},{9,10},{10,11},{11... | collective-permute-start | bytes 14264 | tf_op jit(solution)/shard_map/ppermute | solution.py:16
  (8 other events, 53.2 us)
where the time goes:
time: 224 us; the launch traced here: 222 us
  starting transfers between devices  73.3 us (33%)
  local copies, waits for them, and re-layouts  43.5 us (19%)
  other arithmetic  38.8 us (17%)
  blocking collectives  33.6 us (15%)
  waiting for transfers between devices  29.4 us (13%)
    ppermute x12, starting transfers between devices, padded_2(): after = lax.ppermute(leading, axis, down)  38.3 us
    ppermute x12, starting transfers between devices, padded_2(): before = lax.ppermute(last, axis, up)  35 us
    all_gather x1, blocking collectives, per_device(): gathered = lax.all_gather(coef, 'gz', axis=2, tiled=True)  33.6 us
    mul x4, other arithmetic, advance(): return (neighbours(padded) / 3.0 - previous) * (1.0 - 0.5 * weights)  31.7 us
    ppermute x12, waiting for transfers between devices, padded_2(): before = lax.ppermute(last, axis, up)  27.8 us
    slice x10, local copies, waits for them, and re-layouts, padded_2(): last = lax.slice_in_dim(shard, length - width, length, axis=dim)  12.3 us
    unnamed x26, local copies, waits for them, and re-layouts  10.5 us
    ppermute x4, local copies, waits for them, and re-layouts, padded_2(): before = lax.ppermute(last, axis, up)  6.71 us
  transfers between devices with their start and end apart: 24, of which 9 were waited for; matrix products, arithmetic and copies ran while one was open for 9% of the time, Pallas kernels for 0%

commit v1 on v0

v1 whole, which is shorter than its diff:
```python
import functools

import jax
import jax.numpy as jnp
import numpy as np
from jax import lax
from jax.experimental import pallas as pl
from jax.experimental.pallas import tpu as pltpu
from jax.sharding import PartitionSpec as P

ITERS = 4
X, Y, Z = 16, 64, 128
W = ITERS
N_FACE = W + 2 * (W - 1)
F32 = jnp.float32


def swap_a(n):
    return [(i, i ^ 1) for i in range(n)]


def swap_b(n):
    return [(i, (i + 1) % n if i % 2 else (i - 1) % n) for i in range(n)]


def dct_rows():
    k = np.arange(4)[:, None]
    i = np.arange(8)[None, :]
    scale = np.where(k == 0, np.sqrt(1.0 / 8.0), np.sqrt(2.0 / 8.0))
    return scale * np.cos(np.pi * (2 * i + 1) * k / 16.0)


def is_even(axis):
    return lax.rem(lax.axis_index(axis), 2) == 0


def b_is_inside(axis):
    index, count = lax.axis_index(axis), lax.axis_size(axis)
    return jnp.logical_and(index > 0, index < count - 1)


def iota(shape, dim):
    return lax.broadcasted_iota(jnp.int32, shape, dim)


def gain_of(mask):
    return 1.0 - 0.5 * mask.astype(F32)


def load(p, q, m, arr, x, rows=slice(None)):
    if arr == 0:
        return p[x, rows, :]
    if arr == 1:
        return q[x, rows, :]
    return gain_of(m[x, rows, :])


def y_pairs():
    return [((0, x), (1, x)) for x in range(X)] + [((2, 2 * i), (2, 2 * i + 1)) for i in range(X // 2)]


def face(p, q, m, right, store):
    p0 = jnp.where(right, X - W, 0)
    q0 = jnp.where(right, X - W + 1, 0)
    for k in range(W):
        store(k, 0, p0 + k)
    for k in range(W - 1):
        store(W + k, 1, q0 + k)
    for k in range(W - 1):
        store(2 * W - 1 + k, 2, q0 + k)


def pack_first(p, q, m, ya, yb, xb):
    even = is_even("gy")
    low = iota((8, Z), 0) < 4
    top, bottom = slice(Y - 8, Y), slice(0, 8)
    for t, (a, b) in enumerate(y_pairs()):
        up = jnp.where(low, pltpu.roll(load(p, q, m, *a, top), 4, 0), load(p, q, m, *b, top))
        down = jnp.where(low, load(p, q, m, *a, bottom), pltpu.roll(load(p, q, m, *b, bottom), 4, 0))
        ya[t] = jnp.where(even, up, down)
        yb[t] = jnp.where(even, down, up)

    def store(k, arr, x):
        xb[k] = load(p, q, m, arr, x)

    face(p, q, m, jnp.logical_not(is_even("gx")), store)


def pack_z(p, q, m, ra, rb, za, zb, yh):
    even = is_even("gy")
    low = iota((8, Z), 0) < 4
    keep_b = b_is_inside("gy")
    for t, (a, b) in enumerate(y_pairs()):
        va = ra[t]
        vb = jnp.where(keep_b, rb[t], 0.0)
        right, left = jnp.where(even, va, vb), jnp.where(even, vb, va)
        yh[a[0] * X + a[1]] = jnp.where(low, right, pltpu.roll(left, 4, 0))
        yh[b[0] * X + b[1]] = jnp.where(low, pltpu.roll(right, 4, 0), left)
    even_z = is_even("gz")
    for r in range(Y // 8 + 1):
        slot = iota((8, Z), 1) // 4
        for tile in range(2):
            up = jnp.zeros((8, Z), F32)
            down = jnp.zeros((8, Z), F32)
            for s in range(32):
                i = tile * 32 + s
                if i >= 3 * X:
                    break
                if r < Y // 8:
                    v = load(p, q, m, i // X, i % X, slice(8 * r, 8 * r + 8))
                else:
                    v = yh[i]
                v = pltpu.roll(v, 4 * s, 1) if s else v
                up = jnp.where(slot == (s + 31) % 32, v, up)
                down = jnp.where(slot == s, v, down)
            za[tile, 8 * r : 8 * r + 8, :] = jnp.where(even_z, up, down)
            zb[tile, 8 * r : 8 * r + 8, :] = jnp.where(even_z, down, up)


ROWS = Y + 8


def pack_x(p, q, m, yh, ra, rb, xa, xbc, zh):
    even = is_even("gz")
    keep_b = b_is_inside("gz")
    lane = iota((ROWS, Z), 1)
    for tile in range(2):
        va = ra[tile]
        vb = jnp.where(keep_b, rb[tile], 0.0)
        right, left = jnp.where(even, va, vb), jnp.where(even, vb, va)
        for s in range(32):
            i = tile * 32 + s
            if i >= 3 * X:
                break
            v = jnp.where(lane // 4 == s, right, left)
            zh[i] = pltpu.roll(v, (Z - 4 * s) % Z, 1) if s else v
    even_x = is_even("gx")
    slot = iota((ROWS, Z), 1) // 8
    main = N_FACE * Y

    def corners(right, out, base):
        acc = [jnp.zeros((ROWS, Z), F32)]

        def store(k, arr, x):
            out[base + 8 * k : base + 8 * k + 8, :] = yh[arr * X + x]
            acc[0] = jnp.where(slot == k, pltpu.roll(zh[arr * X + x], 8 * k + 4, 1), acc[0])

        face(p, q, m, right, store)
        out[base + 8 * N_FACE : base + 8 * N_FACE + ROWS, :] = acc[0]

    corners(jnp.logical_not(even_x), xbc, 0)

    def store(k, arr, x):
        xa[Y * k : Y * k + Y, :] = load(p, q, m, arr, x)

    face(p, q, m, even_x, store)
    corners(even_x, xa, main)


def advance(now, old, gain, put, lo, hi):
    n = X + 2 * W

    def body(j, carry):
        x = lax.rem(j + (lo + n), n)
        xm, xp = lax.rem(x + n - 1, n), lax.rem(x + 1, n)
        c = now[x]
        total = now[xm] + now[xp]
        total = total + pltpu.roll(c, 1, 0) + pltpu.roll(c, ROWS - 1, 0)
        total = total + pltpu.roll(c, 1, 1) + pltpu.roll(c, 2 * Z - 1, 1)
        put(x, (total * (1.0 / 3.0) - old[x]) * gain[x])
        return carry

    lax.fori_loop(0, hi - lo, body, 0)


def run_steps(p, q, m, yh, zh, xbm, xbc, xa, dz, dy, pressure, coef, cur, old, gain):
    ext = (cur, old, gain)
    for arr in range(3):
        for x in range(X):
            ext[arr][x, :Y, :Z] = load(p, q, m, arr, x)
            ext[arr][x, Y:, :Z] = yh[arr * X + x]
            ext[arr][x, :, Z:] = zh[arr * X + x]
    even = is_even("gx")
    keep_b = b_is_inside("gx")

    def unpack(right, main, corner, base, fix):
        z_tile = fix(corner[base + 8 * N_FACE : base + 8 * N_FACE + ROWS, :])
        p0 = jnp.where(right, X, X + W)
        q0 = jnp.where(right, X, X + W + 1)
        for k in range(N_FACE):
            arr = 0 if k < W else 1 if k < 2 * W - 1 else 2
            x = p0 + k if arr == 0 else q0 + (k - W if arr == 1 else k - 2 * W + 1)
            ext[arr][x, :Y, :Z] = fix(main(k))
            ext[arr][x, Y:, :Z] = fix(corner[base + 8 * k : base + 8 * k + 8, :])
            ext[arr][x, :, Z:] = pltpu.roll(z_tile, Z - 8 * k - 4, 1)

    unpack(even, lambda k: xa[Y * k : Y * k + Y, :], xa, N_FACE * Y, lambda v: v)
    unpack(jnp.logical_not(even), lambda k: xbm[k], xbc, 0, lambda v: jnp.where(keep_b, v, 0.0))

    for step in range(ITERS):
        now, before = (cur, old) if step % 2 == 0 else (old, cur)
        reach = ITERS - 1 - step

        def put(x, v, before=before):
            before[x] = v

        advance(now, before, gain, put, -reach, X + reach)
    final = cur if ITERS % 2 == 0 else old
    rows = dct_rows()
    parts = []
    for b in range(X // 8):
        f = [final[8 * b + i, :Y, :Z] for i in range(8)]
        for i in range(8):
            pressure[8 * b + i] = f[i]
        plus = [f[i] + f[7 - i] for i in range(4)]
        minus = [f[i] - f[7 - i] for i in range(4)]
        for k in range(4):
            terms = plus if k % 2 == 0 else minus
            parts.append(sum(float(rows[k, i]) * terms[i] for i in range(4)))
    half = X // 4
    left = jnp.concatenate(parts[:half], axis=0)
    right = jnp.concatenate(parts[half:], axis=0)
    both = jnp.concatenate([left, right], axis=1)
    along_z = jnp.dot(both, dz[...], precision=lax.Precision.HIGHEST, preferred_element_type=F32)
    result = jnp.dot(dy[...], along_z, precision=lax.Precision.HIGHEST, preferred_element_type=F32)
    for d in range(coef.shape[0]):
        coef[d] = result


def place(writer, got, out):
    mine = writer[0, 0] == lax.axis_index("gz")
    low = iota((Y // 2, Z), 1) < Z // 2

    @pl.when(mine)
    def _():
        for t in range(got.shape[0] // 2):
            for h in range(X // 4):
                a = got[2 * t, h * (Y // 2) : (h + 1) * (Y // 2), :]
                b = got[2 * t + 1, h * (Y // 2) : (h + 1) * (Y // 2), :]
                out[0, h, :, t * Z : (t + 1) * Z] = jnp.where(low, a, pltpu.roll(b, Z // 2, 1))
                out[0, h + X // 4, :, t * Z : (t + 1) * Z] = jnp.where(low, pltpu.roll(a, Z // 2, 1), b)

    @pl.when(jnp.logical_not(mine))
    def _():
        out[...] = jnp.zeros_like(out)


def call(kernel, outs, *args, smem=0, scratch=(), limit=40 << 20):
    vm = pl.BlockSpec(memory_space=pltpu.VMEM)
    sm = pl.BlockSpec(memory_space=pltpu.SMEM)
    return pl.pallas_call(
        kernel,
        out_shape=[jax.ShapeDtypeStruct(s, F32) for s in outs],
        in_specs=[sm] * smem + [vm] * (len(args) - smem),
        out_specs=[vm] * len(outs),
        scratch_shapes=list(scratch),
        compiler_params=pltpu.CompilerParams(vmem_limit_bytes=limit),
    )(*args)


def matrices():
    rows = dct_rows()
    z = np.kron(np.eye(Z // 8), rows.T)
    dz = np.kron(np.eye(2), z)
    y = np.kron(np.eye(Y // 8), rows)
    dy = np.kron(np.eye(X // 4), y)
    return dz.astype(np.float32), dy.astype(np.float32)


def per_device(p, q, m, writer):
    sizes = {a: lax.axis_size(a) for a in ("gx", "gy", "gz")}

    def swap(v, axis, kind):
        return lax.ppermute(v, axis, kind(sizes[axis]))

    n_y = X + X // 2
    ya, yb, xb = call(pack_first, [(n_y, 8, Z), (n_y, 8, Z), (N_FACE, Y, Z)], p, q, m)
    ya, yb = swap(ya, "gy", swap_a), swap(yb, "gy", swap_b)
    xb = swap(xb, "gx", swap_b)
    za, zb, yh = call(pack_z, [(2, ROWS, Z), (2, ROWS, Z), (3 * X, 8, Z)], p, q, m, ya, yb)
    za, zb = swap(za, "gz", swap_a), swap(zb, "gz", swap_b)
    n_corner = 8 * N_FACE + ROWS
    xa, xbc, zh = call(
        pack_x, [(N_FACE * Y + n_corner, Z), (n_corner, Z), (3 * X, ROWS, Z)], p, q, m, yh, za, zb
    )
    xa, xbc = swap(xa, "gx", swap_a), swap(xbc, "gx", swap_b)
    dz, dy = matrices()
    ext = pltpu.VMEM((X + 2 * W, ROWS, 2 * Z), F32)
    n = sizes["gz"]
    pressure, coef = call(
        run_steps, [(X, Y, Z), (n, 2 * Y, Z)], p, q, m, yh, zh, xb, xbc, xa, dz, dy, scratch=[ext, ext, ext]
    )
    got = lax.all_to_all(coef, "gz", 0, 0, tiled=True)
    (out,) = call(place, [(1, X // 2, Y // 2, n * Z // 2)], writer, got, smem=1)
    return pressure, out


def solution(mesh):
    return jax.shard_map(
        per_device,
        mesh=mesh,
        in_specs=(P("gx", "gy", "gz"), P("gx", "gy", "gz"), P("gx", "gy", "gz"), P("gx", "gy")),
        out_specs=(P("gx", "gy", "gz"), P("gz", "gx", "gy", None)),
        check_vma=False,
    )
```

time: 224 us -> 60.6 us (0.27)
  the two profiles are of different devices: /device:TPU:176 before, /device:TPU:24 now
where the time goes in v1:
time: 60.6 us; the launch traced here: 60.4 us
  waiting for transfers between devices  24.9 us (41%)
  starting transfers between devices  17.7 us (29%)
  Pallas kernels  13.3 us (22%)
  local copies, waits for them, and re-layouts  3.12 us (5%)
  between operations  1.33 us (2%)
    ppermute x7, waiting for transfers between devices, swap(): return lax.ppermute(v, axis, kind(sizes[axis]))  17.3 us
    ppermute x7, starting transfers between devices, swap(): return lax.ppermute(v, axis, kind(sizes[axis]))  13.7 us
    pallas_call x5, Pallas kernels, call(): pl.pallas_call(kernel, out_shape=[jax.ShapeDtypeStruct(s, F32) for s in o...  13.3 us
    all_to_all x1, waiting for transfers between devices, per_device(): got = lax.all_to_all(coef, 'gz', 0, 0, tiled=True)  7.63 us
    all_to_all x1, starting transfers between devices, per_device(): got = lax.all_to_all(coef, 'gz', 0, 0, tiled=True)  3.96 us
    unnamed x10, local copies, waits for them, and re-layouts  3.12 us
  transfers between devices with their start and end apart: 8, of which 5 were waited for; matrix products, arithmetic and copies ran while one was open for 0% of the time, Pallas kernels for 0%

profile of v1, /device:TPU:24, one launch (start us, length us, event | category | flops | bytes accessed | tf_op | source)
XLA Modules:
  0.0 60.4 jit_solution(12604391401158925335)
XLA Ops:
  0.6 1.0 %copy-done = f32[16,64,128]{2,1,0:T(8,128)S(1)} copy-done((f32[16,64,128]{2,1,0:T(8,128)S(1)}, f32[16,64,128]{2,1,0:T(8,128)}, u32[]{:S(2)}) %copy-start) | copy-done | bytes 524312
  1.7 1.0 %copy-done.1 = f32[16,64,128]{2,1,0:T(8,128)S(1)} copy-done((f32[16,64,128]{2,1,0:T(8,128)S(1)}, f32[16,64,128]{2,1,0:T(8,128)}, u32[]{:S(2)}) %copy-start.1) | copy-done | bytes 524312
  2.7 1.0 %copy-done.2 = s32[16,64,128]{2,1,0:T(8,128)S(1)} copy-done((s32[16,64,128]{2,1,0:T(8,128)S(1)}, s32[16,64,128]{2,1,0:T(8,128)}, u32[]{:S(2)}) %copy-start.2) | copy-done | bytes 524312
  3.8 0.1 shard_map.77
  3.8 0.8 %collective-permute-start = (f32[24,8,128]{2,1,0:T(8,128)S(1)}, f32[24,8,128]{2,1,0:T(8,128)S(1)}, u32[]{:S(2)}, u32[]{:S(2)}) collective-permute-start(f32[24,8,128]{2,1,0:T(8,128)S(1)} %get-tuple-element.13), channel_id=1, source_target_pairs={{0,8},{8,0},{16,24},{24,16},{1,9},{9,1},{17,25},{25,17},{2,10},{10... | collective-permute-start | bytes 294920 | tf_op jit(solution)/shard_map/ppermute | solution.py:274
  4.7 1.3 %collective-permute-start.1 = (f32[24,8,128]{2,1,0:T(8,128)S(1)}, f32[24,8,128]{2,1,0:T(8,128)S(1)}, u32[]{:S(2)}, u32[]{:S(2)}) collective-permute-start(f32[24,8,128]{2,1,0:T(8,128)S(1)} %get-tuple-element.14), channel_id=1, source_target_pairs={{0,24},{8,16},{16,8},{24,0},{1,25},{9,17},{17,9},{25,1},{2,26},{10... | collective-permute-start | bytes 294920 | tf_op jit(solution)/shard_map/ppermute | solution.py:274
  6.0 2.5 %collective-permute-done.ra = f32[24,8,128]{2,1,0:T(8,128)S(1)} collective-permute-done((f32[24,8,128]{2,1,0:T(8,128)S(1)}, f32[24,8,128]{2,1,0:T(8,128)S(1)}, u32[]{:S(2)}, u32[]{:S(2)}) %collective-permute-start) | collective-permute-done | bytes 98336 | tf_op jit(solution)/shard_map/ppermute | solution.py:274
  8.5 2.0 %collective-permute-done.1.rb = f32[24,8,128]{2,1,0:T(8,128)S(1)} collective-permute-done((f32[24,8,128]{2,1,0:T(8,128)S(1)}, f32[24,8,128]{2,1,0:T(8,128)S(1)}, u32[]{:S(2)}, u32[]{:S(2)}) %collective-permute-start.1) | collective-permute-done | bytes 98336 | tf_op jit(solution)/shard_map/ppermute | solution.py:274
  10.5 0.5 shard_map.78
  11.0 1.6 %collective-permute-start.2 = (f32[2,72,128]{2,1,0:T(8,128)S(1)}, f32[2,72,128]{2,1,0:T(8,128)S(1)}, u32[]{:S(2)}, u32[]{:S(2)}) collective-permute-start(f32[2,72,128]{2,1,0:T(8,128)S(1)} %get-tuple-element.16), channel_id=1, source_target_pairs={{0,1},{1,0},{2,3},{3,2},{4,5},{5,4},{6,7},{7,6},{8,9},{9,8},{10,11... | collective-permute-start | bytes 221192 | tf_op jit(solution)/shard_map/ppermute | solution.py:274
  12.6 3.4 %collective-permute-start.3 = (f32[2,72,128]{2,1,0:T(8,128)S(1)}, f32[2,72,128]{2,1,0:T(8,128)S(1)}, u32[]{:S(2)}, u32[]{:S(2)}) collective-permute-start(f32[2,72,128]{2,1,0:T(8,128)S(1)} %get-tuple-element.17), channel_id=1, source_target_pairs={{0,7},{1,2},{2,1},{3,4},{4,3},{5,6},{6,5},{7,0},{8,15},{9,10},{10,... | collective-permute-start | bytes 221192 | tf_op jit(solution)/shard_map/ppermute | solution.py:274
  16.0 0.0 collective-permute-done.2.ra
  16.0 3.0 %collective-permute-done.3.rb = f32[2,72,128]{2,1,0:T(8,128)S(1)} collective-permute-done((f32[2,72,128]{2,1,0:T(8,128)S(1)}, f32[2,72,128]{2,1,0:T(8,128)S(1)}, u32[]{:S(2)}, u32[]{:S(2)}) %collective-permute-start.3) | collective-permute-done | bytes 73760 | tf_op jit(solution)/shard_map/ppermute | solution.py:274
  19.0 0.8 %shard_map.79 = (f32[792,128]{1,0:T(8,128)S(1)}, f32[152,128]{1,0:T(8,128)S(1)}, f32[48,72,128]{2,1,0:T(8,128)S(1)}) custom-call(f32[16,64,128]{2,1,0:T(8,128)S(1)} %copy-done, f32[16,64,128]{2,1,0:T(8,128)S(1)} %copy-done.1, s32[16,64,128]{2,1,0:T(8,128)S(1)} %copy-done.2, f32[48,8,128]{2,1,0:T(8,128)S(1)} %get-tuple-element.15.yh, ...), custom_call_target="tpu_custom_call" | custom-call | tf_op jit(solution)/shard_map/pallas_call | solution.py:251
  19.8 0.1 collective-permute-start.6
  19.9 6.4 %collective-permute-start.4 = (f32[10,64,128]{2,1,0:T(8,128)S(1)}, f32[10,64,128]{2,1,0:T(8,128)S(1)}, u32[]{:S(2)}, u32[]{:S(2)}) collective-permute-start(f32[10,64,128]{2,1,0:T(8,128)S(1)} %get-tuple-element.19), channel_id=1, source_target_pairs={{0,224},{32,64},{64,32},{96,128},{128,96},{160,192},{192,160},{224... | collective-permute-start | bytes 983048 | tf_op jit(solution)/shard_map/ppermute | solution.py:274
  26.3 0.0 collective-permute-start.5
  26.3 9.8 %collective-permute-done.5.xbc = f32[152,128]{1,0:T(8,128)S(1)} collective-permute-done((f32[152,128]{1,0:T(8,128)S(1)}, f32[152,128]{1,0:T(8,128)S(1)}, u32[]{:S(2)}, u32[]{:S(2)}) %collective-permute-start.5) | collective-permute-done | bytes 77856 | tf_op jit(solution)/shard_map/ppermute | solution.py:274
  36.1 0.0 collective-permute-done.4.xbm
  36.1 0.0 collective-permute-done.6.xa
  36.1 11.0 %shard_map.80 = (f32[16,64,128]{2,1,0:T(8,128)}, f32[8,128,128]{2,1,0:T(8,128)}) custom-call(f32[16,64,128]{2,1,0:T(8,128)S(1)} %copy-done, f32[16,64,128]{2,1,0:T(8,128)S(1)} %copy-done.1, s32[16,64,128]{2,1,0:T(8,128)S(1)} %copy-done.2, f32[48,8,128]{2,1,0:T(8,128)S(1)} %get-tuple-element.15.yh, f32[48,72,128]{2,1,0:T(8,128)S(1)} %get-tuple-element.18.zh, ...), custom_call_target="tpu_custom_call" | custom-call | tf_op jit(solution)/shard_map/pallas_call | solution.py:251
  47.1 4.0 %all-to-all-start = ((f32[8,128,128]{2,1,0:T(8,128)}), f32[8,128,128]{2,1,0:T(8,128)S(1)}, u32[]{:S(2)}, u32[]{:S(2)}) async-start(f32[8,128,128]{2,1,0:T(8,128)} %get-tuple-element.23), calls=%async_computation | async-start | bytes 1048576 | tf_op jit(solution)/shard_map/all_to_all | solution.py:293
  51.8 7.6 %all-to-all-done.got = f32[8,128,128]{2,1,0:T(8,128)S(1)} async-done(((f32[8,128,128]{2,1,0:T(8,128)}), f32[8,128,128]{2,1,0:T(8,128)S(1)}, u32[]{:S(2)}, u32[]{:S(2)}) %all-to-all-start) | async-done | bytes 524320 | tf_op jit(solution)/shard_map/all_to_all | solution.py:293
  59.4 1.0 %shard_map.81 = f32[1,8,32,512]{3,2,1,0:T(8,128)} custom-call(s32[1,1]{1,0:T(1,128)S(6)} %copy.8.writer, f32[8,128,128]{2,1,0:T(8,128)S(1)} %all-to-all-done.got), custom_call_target="tpu_custom_call" | custom-call | tf_op jit(solution)/shard_map/pallas_call | solution.py:251
  (7 shorter events, 0.0 us)
Async XLA Ops:
  0.6 1.0 %copy-start = (f32[16,64,128]{2,1,0:T(8,128)S(1)}, f32[16,64,128]{2,1,0:T(8,128)}, u32[]{:S(2)}) copy-start(f32[16,64,128]{2,1,0:T(8,128)} %p.7) | copy-start | bytes 1572868
  1.7 1.0 %copy-start.1 = (f32[16,64,128]{2,1,0:T(8,128)S(1)}, f32[16,64,128]{2,1,0:T(8,128)}, u32[]{:S(2)}) copy-start(f32[16,64,128]{2,1,0:T(8,128)} %q.7) | copy-start | bytes 1572868
  2.7 1.0 %copy-start.2 = (s32[16,64,128]{2,1,0:T(8,128)S(1)}, s32[16,64,128]{2,1,0:T(8,128)}, u32[]{:S(2)}) copy-start(s32[16,64,128]{2,1,0:T(8,128)} %m.7) | copy-start | bytes 1572868
  3.8 4.7 %collective-permute-start = (f32[24,8,128]{2,1,0:T(8,128)S(1)}, f32[24,8,128]{2,1,0:T(8,128)S(1)}, u32[]{:S(2)}, u32[]{:S(2)}) collective-permute-start(f32[24,8,128]{2,1,0:T(8,128)S(1)} %get-tuple-element.13), channel_id=1, source_target_pairs={{0,8},{8,0},{16,24},{24,16},{1,9},{9,1},{17,25},{25,17},{2,10},{10... | collective-permute-start | bytes 294920 | tf_op jit(solution)/shard_map/ppermute | solution.py:274
  4.6 31.5 %copy-start.3 = (f32[256,128]{1,0:T(8,128)S(1)}, f32[256,128]{1,0:T(8,128)}, u32[]{:S(2)}) copy-start(f32[256,128]{1,0:T(8,128)} %constant.4.clone.dz) | copy-start | bytes 393220
  4.7 31.5 %copy-start.4 = (f32[128,256]{1,0:T(8,128)S(1)}, f32[128,256]{1,0:T(8,128)}, u32[]{:S(2)}) copy-start(f32[128,256]{1,0:T(8,128)} %constant.5.clone.dy) | copy-start | bytes 393220
  4.7 5.8 %collective-permute-start.1 = (f32[24,8,128]{2,1,0:T(8,128)S(1)}, f32[24,8,128]{2,1,0:T(8,128)S(1)}, u32[]{:S(2)}, u32[]{:S(2)}) collective-permute-start(f32[24,8,128]{2,1,0:T(8,128)S(1)} %get-tuple-element.14), channel_id=1, source_target_pairs={{0,24},{8,16},{16,8},{24,0},{1,25},{9,17},{17,9},{25,1},{2,26},{10... | collective-permute-start | bytes 294920 | tf_op jit(solution)/shard_map/ppermute | solution.py:274
  11.0 5.0 %collective-permute-start.2 = (f32[2,72,128]{2,1,0:T(8,128)S(1)}, f32[2,72,128]{2,1,0:T(8,128)S(1)}, u32[]{:S(2)}, u32[]{:S(2)}) collective-permute-start(f32[2,72,128]{2,1,0:T(8,128)S(1)} %get-tuple-element.16), channel_id=1, source_target_pairs={{0,1},{1,0},{2,3},{3,2},{4,5},{5,4},{6,7},{7,6},{8,9},{9,8},{10,11... | collective-permute-start | bytes 221192 | tf_op jit(solution)/shard_map/ppermute | solution.py:274
  12.6 6.5 %collective-permute-start.3 = (f32[2,72,128]{2,1,0:T(8,128)S(1)}, f32[2,72,128]{2,1,0:T(8,128)S(1)}, u32[]{:S(2)}, u32[]{:S(2)}) collective-permute-start(f32[2,72,128]{2,1,0:T(8,128)S(1)} %get-tuple-element.17), channel_id=1, source_target_pairs={{0,7},{1,2},{2,1},{3,4},{4,3},{5,6},{6,5},{7,0},{8,15},{9,10},{10,... | collective-permute-start | bytes 221192 | tf_op jit(solution)/shard_map/ppermute | solution.py:274
  19.8 16.3 %collective-permute-start.6 = (f32[792,128]{1,0:T(8,128)S(1)}, f32[792,128]{1,0:T(8,128)S(1)}, u32[]{:S(2)}, u32[]{:S(2)}) collective-permute-start(f32[792,128]{1,0:T(8,128)S(1)} %get-tuple-element.21), channel_id=1, source_target_pairs={{0,32},{32,0},{64,96},{96,64},{128,160},{160,128},{192,224},{224,1... | collective-permute-start | bytes 1216520 | tf_op jit(solution)/shard_map/ppermute | solution.py:274
  19.9 16.2 %collective-permute-start.4 = (f32[10,64,128]{2,1,0:T(8,128)S(1)}, f32[10,64,128]{2,1,0:T(8,128)S(1)}, u32[]{:S(2)}, u32[]{:S(2)}) collective-permute-start(f32[10,64,128]{2,1,0:T(8,128)S(1)} %get-tuple-element.19), channel_id=1, source_target_pairs={{0,224},{32,64},{64,32},{96,128},{128,96},{160,192},{192,160},{224... | collective-permute-start | bytes 983048 | tf_op jit(solution)/shard_map/ppermute | solution.py:274
  26.3 9.8 %collective-permute-start.5 = (f32[152,128]{1,0:T(8,128)S(1)}, f32[152,128]{1,0:T(8,128)S(1)}, u32[]{:S(2)}, u32[]{:S(2)}) collective-permute-start(f32[152,128]{1,0:T(8,128)S(1)} %get-tuple-element.20), channel_id=1, source_target_pairs={{0,224},{32,64},{64,32},{96,128},{128,96},{160,192},{192,160},{224... | collective-permute-start | bytes 233480 | tf_op jit(solution)/shard_map/ppermute | solution.py:274
  47.1 12.2 %all-to-all-start = ((f32[8,128,128]{2,1,0:T(8,128)}), f32[8,128,128]{2,1,0:T(8,128)S(1)}, u32[]{:S(2)}, u32[]{:S(2)}) async-start(f32[8,128,128]{2,1,0:T(8,128)} %get-tuple-element.23), calls=%async_computation | async-start | bytes 1048576 | tf_op jit(solution)/shard_map/all_to_all | solution.py:293

commit v2 on v1

v2 whole, which is shorter than its diff:
```python
import functools

import jax
import jax.numpy as jnp
import numpy as np
from jax import lax
from jax.experimental import pallas as pl
from jax.experimental.pallas import tpu as pltpu
from jax.sharding import PartitionSpec as P

ITERS = 4
X, Y, Z = 16, 64, 128
W = ITERS
N_FACE = W + 2 * (W - 1)
F32 = jnp.float32


def swap_a(v, axis):
    return lax.ppermute(v, axis, [(i, i ^ 1) for i in range(lax.axis_size(axis))])


def swap_b(v, axis):
    other = "gy" if axis == "gx" else "gx"
    names = ("gx", "gy") if axis == "gx" else ("gx", axis)
    n, m = lax.axis_size(axis), lax.axis_size(other)

    def flat(i, o):
        return i * m + o if axis == "gx" else o * n + i

    pairs = []
    for o in range(m):
        for i in range(n):
            j = i + 1 if i % 2 else i - 1
            pairs.append((flat(i, o), flat(j, o) if 0 <= j < n else flat(i, o ^ 1)))
    return lax.ppermute(v, names, pairs)


def dct_rows():
    k = np.arange(4)[:, None]
    i = np.arange(8)[None, :]
    scale = np.where(k == 0, np.sqrt(1.0 / 8.0), np.sqrt(2.0 / 8.0))
    return scale * np.cos(np.pi * (2 * i + 1) * k / 16.0)


def is_even(axis):
    return lax.rem(lax.axis_index(axis), 2) == 0


def b_is_inside(axis):
    index, count = lax.axis_index(axis), lax.axis_size(axis)
    return jnp.logical_and(index > 0, index < count - 1)


def iota(shape, dim):
    return lax.broadcasted_iota(jnp.int32, shape, dim)


def gain_of(mask):
    return 1.0 - 0.5 * mask.astype(F32)


def load(p, q, m, arr, x, rows=slice(None)):
    if arr == 0:
        return p[x, rows, :]
    if arr == 1:
        return q[x, rows, :]
    return gain_of(m[x, rows, :])


def y_pairs():
    return [((0, x), (1, x)) for x in range(X)] + [((2, 2 * i), (2, 2 * i + 1)) for i in range(X // 2)]


def face_items(right):
    p0 = jnp.where(right, X - W, 0)
    q0 = jnp.where(right, X - W + 1, 0)
    return [(0, p0 + k) for k in range(W)] + [(a, q0 + k) for a in (1, 2) for k in range(W - 1)]


def halo_slots(right):
    p0 = jnp.where(right, X + W, 0)
    q0 = jnp.where(right, X + W, 1)
    return [(0, p0 + k) for k in range(W)] + [(a, q0 + k) for a in (1, 2) for k in range(W - 1)]


def pack_y(p, q, m, ya, yb, ep, eq, em, sems):
    copies = []
    for src, dst in ((p, ep), (q, eq), (m, em)):
        for side, at in enumerate((0, Y - 8)):
            copies.append(pltpu.make_async_copy(src.at[:, at : at + 8, :], dst.at[side], sems.at[len(copies)]))
    for c in copies:
        c.start()
    for c in copies:
        c.wait()
    even = is_even("gy")
    low = iota((8, Z), 0) < 4

    def edge(arr, x, side):
        v = (ep, eq, em)[arr][side, x]
        return gain_of(v) if arr == 2 else v

    for t, (a, b) in enumerate(y_pairs()):
        up = jnp.where(low, pltpu.roll(edge(*a, 1), 4, 0), edge(*b, 1))
        down = jnp.where(low, edge(*a, 0), pltpu.roll(edge(*b, 0), 4, 0))
        ya[t] = jnp.where(even, up, down)
        yb[t] = jnp.where(even, down, up)


def pack_faces(p, q, m, _, xa, xb):
    even = is_even("gx")
    for out, right in ((xa, even), (xb, jnp.logical_not(even))):
        for k, (arr, x) in enumerate(face_items(right)):
            out[k] = load(p, q, m, arr, x)


def pack_z(p, q, m, ra, rb, za, zb, yh):
    even = is_even("gy")
    low = iota((8, Z), 0) < 4
    keep_b = b_is_inside("gy")
    for t, (a, b) in enumerate(y_pairs()):
        va = ra[t]
        vb = jnp.where(keep_b, rb[t], 0.0)
        right, left = jnp.where(even, va, vb), jnp.where(even, vb, va)
        yh[a[0] * X + a[1]] = jnp.where(low, right, pltpu.roll(left, 4, 0))
        yh[b[0] * X + b[1]] = jnp.where(low, pltpu.roll(right, 4, 0), left)
    even_z = is_even("gz")
    for r in range(Y // 8 + 1):
        slot = iota((8, Z), 1) // 4
        for tile in range(2):
            up = jnp.zeros((8, Z), F32)
            down = jnp.zeros((8, Z), F32)
            for s in range(32):
                i = tile * 32 + s
                if i >= 3 * X:
                    break
                if r < Y // 8:
                    v = load(p, q, m, i // X, i % X, slice(8 * r, 8 * r + 8))
                else:
                    v = yh[i]
                v = pltpu.roll(v, 4 * s, 1) if s else v
                up = jnp.where(slot == (s + 31) % 32, v, up)
                down = jnp.where(slot == s, v, down)
            za[tile, 8 * r : 8 * r + 8, :] = jnp.where(even_z, up, down)
            zb[tile, 8 * r : 8 * r + 8, :] = jnp.where(even_z, down, up)


ROWS = Y + 2 * W
SLOTS = X + 2 * W
TOP = 8
TALL = TOP + ROWS + 8
CORNER = 8 * N_FACE + ROWS


def z_sides(ra, rb, tile):
    even = is_even("gz")
    va = ra[tile]
    vb = jnp.where(b_is_inside("gz"), rb[tile], 0.0)
    return jnp.where(even, va, vb), jnp.where(even, vb, va)


def z_item(right, left, lane, s):
    v = jnp.where(lane // 4 == s, right, left)
    return pltpu.roll(v, (Z - 4 * s) % Z, 1) if s else v


def pack_x(yh, ra, rb, xac, xbc, zh):
    lane = iota((ROWS, Z), 1)
    edge = set(range(W)) | set(range(X - W, X))
    for tile in range(2):
        right, left = z_sides(ra, rb, tile)
        for s in range(32):
            i = tile * 32 + s
            if i < 3 * X and i % X in edge:
                zh[i] = z_item(right, left, lane, s)
    even_x = is_even("gx")
    slot = lane // 8

    def corners(right, out):
        acc = jnp.zeros((ROWS, Z), F32)
        for k, (arr, x) in enumerate(face_items(right)):
            out[8 * k : 8 * k + 8, :] = yh[arr * X + x]
            acc = jnp.where(slot == k, pltpu.roll(zh[arr * X + x], 8 * k + 4, 1), acc)
        out[8 * N_FACE : CORNER, :] = acc

    corners(jnp.logical_not(even_x), xbc)
    corners(even_x, xac)


def put_rows(ref, s, v):
    ref[s, TOP + W : TOP + W + Y, :] = v[:Y]
    put_edges(ref, s, v[Y:])


def put_edges(ref, s, v):
    ref[s, TOP + W + Y : TOP + ROWS, :] = v[:W]
    ref[s, TOP : TOP + W, :] = v[W:]


def update(out, now, old, gain, s, halo):
    size = 24
    first = iota((size, Z), 1) == 0
    last = iota((size, Z), 1) == Z - 1
    for r in range(TOP, TOP + ROWS, size):
        here, above, below = slice(r, r + size), slice(r - 1, r + size - 1), slice(r + 1, r + size + 1)
        c, h = now[0][s, here, :], now[1][s, here, :]
        cr, hr = pltpu.roll(c, 1, 1), pltpu.roll(h, 1, 1)
        cl, hl = pltpu.roll(c, Z - 1, 1), pltpu.roll(h, Z - 1, 1)
        along_z = (
            jnp.where(first, hr, cr) + jnp.where(last, hl, cl),
            jnp.where(first, cr, hr) + jnp.where(last, cl, hl),
        )
        for i in range(2 if halo else 1):
            total = now[i][s - 1, here, :] + now[i][s + 1, here, :]
            total = total + now[i][s, above, :] + now[i][s, below, :] + along_z[i]
            out[i][s, here, :] = (total * (1.0 / 3.0) - old[i][s, here, :]) * gain[i][s, here, :]


def unflatten(refs):
    pairs = [(refs[2 * i], refs[2 * i + 1]) for i in range(2 + ITERS)] + [(refs[2 * (2 + ITERS)],)]
    return pairs[0], pairs[1], pairs[2:]


N_EXT = 2 * (2 + ITERS) + 1


def run_inside(p, q, m, yh, ra, rb, *refs):
    old, gain, level = unflatten(refs)
    ext = (level[0], old, gain)
    lane = iota((ROWS, Z), 1)
    for tile in range(2):
        right, left = z_sides(ra, rb, tile)
        for s in range(32):
            i = tile * 32 + s
            if i < 3 * X:
                put_rows(ext[i // X][1], W + i % X, z_item(right, left, lane, s))
    for arr in range(3):
        for x in range(X):
            ext[arr][0][W + x, TOP + W : TOP + W + Y, :] = load(p, q, m, arr, x)
            put_edges(ext[arr][0], W + x, yh[arr * X + x])
    for t in range(1, ITERS + 1):
        before = level[t - 2] if t >= 2 else old

        def body(j, carry, t=t, before=before):
            update(level[t], level[t - 1], before, gain, W + t + j, t < ITERS)
            return carry

        lax.fori_loop(0, X - 2 * t, body, 0)


def run_rest(*args):
    xam, xbm, xac, xbc, dz, dy = args[N_EXT : N_EXT + 6]
    refs = args[N_EXT + 6 : 2 * N_EXT + 6]
    pressure, coef = args[2 * N_EXT + 6 :]
    old, gain, level = unflatten(refs)
    ext = (level[0], old, gain)
    even = is_even("gx")
    keep_b = b_is_inside("gx")

    def unpack(right, main, corner, fix):
        z_tile = fix(corner[8 * N_FACE : CORNER, :])
        for k, (arr, s) in enumerate(halo_slots(right)):
            ext[arr][0][s, TOP + W : TOP + W + Y, :] = fix(main[k])
            put_edges(ext[arr][0], s, fix(corner[8 * k : 8 * k + 8, :]))
            put_rows(ext[arr][1], s, pltpu.roll(z_tile, Z - 8 * k - 4, 1))

    unpack(even, xam, xac, lambda v: v)
    unpack(jnp.logical_not(even), xbm, xbc, lambda v: jnp.where(keep_b, v, 0.0))
    for t in range(1, ITERS + 1):
        before = level[t - 2] if t >= 2 else old

        def body(j, carry, t=t, before=before):
            s = jnp.where(j < W, t + j, X + W - t + j - W)
            update(level[t], level[t - 1], before, gain, s, t < ITERS)
            return carry

        lax.fori_loop(0, 2 * W, body, 0)
    rows = dct_rows()
    parts = []
    for b in range(X // 8):
        f = [level[ITERS][0][W + 8 * b + i, TOP + W : TOP + W + Y, :] for i in range(8)]
        for i in range(8):
            pressure[8 * b + i] = f[i]
        plus = [f[i] + f[7 - i] for i in range(4)]
        minus = [f[i] - f[7 - i] for i in range(4)]
        for k in range(4):
            terms = plus if k % 2 == 0 else minus
            parts.append(sum(float(rows[k, i]) * terms[i] for i in range(4)))
    half = X // 4
    left = jnp.concatenate(parts[:half], axis=0)
    right = jnp.concatenate(parts[half:], axis=0)
    both = jnp.concatenate([left, right], axis=1)
    along_z = jnp.dot(both, dz[...], precision=lax.Precision.HIGHEST, preferred_element_type=F32)
    result = jnp.dot(dy[...], along_z, precision=lax.Precision.HIGHEST, preferred_element_type=F32)
    for d in range(coef.shape[0]):
        coef[d] = result


def place(writer, got, out):
    mine = writer[0, 0] == lax.axis_index("gz")
    low = iota((Y // 2, Z), 1) < Z // 2

    @pl.when(mine)
    def _():
        for t in range(got.shape[0] // 2):
            for h in range(X // 4):
                a = got[2 * t, h * (Y // 2) : (h + 1) * (Y // 2), :]
                b = got[2 * t + 1, h * (Y // 2) : (h + 1) * (Y // 2), :]
                out[0, h, :, t * Z : (t + 1) * Z] = jnp.where(low, a, pltpu.roll(b, Z // 2, 1))
                out[0, h + X // 4, :, t * Z : (t + 1) * Z] = jnp.where(low, pltpu.roll(a, Z // 2, 1), b)

    @pl.when(jnp.logical_not(mine))
    def _():
        out[...] = jnp.zeros_like(out)


def call(kernel, outs, *args, first=pltpu.VMEM, n_first=0, scratch=(), aliases=None, cost=1 << 18, flops=0):
    vm = pl.BlockSpec(memory_space=pltpu.VMEM)
    other = pl.BlockSpec(memory_space=first)
    return pl.pallas_call(
        kernel,
        out_shape=[jax.ShapeDtypeStruct(s, F32) for s in outs],
        in_specs=[other] * n_first + [vm] * (len(args) - n_first),
        out_specs=[vm] * len(outs),
        scratch_shapes=list(scratch),
        input_output_aliases=aliases or {},
        cost_estimate=pl.CostEstimate(flops=flops, transcendentals=0, bytes_accessed=cost),
        compiler_params=pltpu.CompilerParams(vmem_limit_bytes=8 << 20),
    )(*args)


def matrices():
    rows = dct_rows()
    z = np.kron(np.eye(Z // 8), rows.T)
    dz = np.kron(np.eye(2), z)
    y = np.kron(np.eye(Y // 8), rows)
    dy = np.kron(np.eye(X // 4), y)
    return dz.astype(np.float32), dy.astype(np.float32)


def per_device(p, q, m, writer):
    n_y = X + X // 2
    edges = [pltpu.VMEM((2, X, 8, Z), d) for d in (F32, F32, jnp.int32)]
    far = [pltpu.with_memory_space_constraint(v, pltpu.HBM) for v in (p, q, m)]
    ya, yb = call(
        pack_y, [(n_y, 8, Z), (n_y, 8, Z)], *far, first=pltpu.HBM, n_first=3,
        scratch=[*edges, pltpu.SemaphoreType.DMA((6,))],
    )
    ya0 = ya
    ya, yb = swap_a(ya, "gy"), swap_b(yb, "gy")
    xa, xb = call(pack_faces, [(N_FACE, Y, Z)] * 2, p, q, m, ya0)
    xa, xb = swap_a(xa, "gx"), swap_b(xb, "gx")
    za, zb, yh = call(pack_z, [(2, ROWS, Z), (2, ROWS, Z), (3 * X, 8, Z)], p, q, m, ya, yb, flops=10000000000)
    za, zb = swap_a(za, "gz"), swap_b(zb, "gz")
    xac, xbc = call(
        pack_x, [(CORNER, Z), (CORNER, Z)], yh, za, zb, scratch=[pltpu.VMEM((3 * X, ROWS, Z), F32)], flops=10000000000
    )
    xac, xbc = swap_a(xac, "gx"), swap_b(xbc, "gx")
    ext = call(run_inside, [(SLOTS, TALL, Z)] * N_EXT, p, q, m, yh, za, zb, flops=10000000000)
    dz, dy = matrices()
    n = lax.axis_size("gz")
    *_, pressure, coef = call(
        run_rest, [(SLOTS, TALL, Z)] * N_EXT + [(X, Y, Z), (n, 2 * Y, Z)], *ext, xa, xb, xac, xbc, dz, dy,
        aliases={i: i for i in range(N_EXT)}, cost=8 << 20,
    )
    got = lax.all_to_all(coef, "gz", 0, 0, tiled=True)
    (out,) = call(place, [(1, X // 2, Y // 2, n * Z // 2)], writer, got, first=pltpu.SMEM, n_first=1)
    return pressure, out


def solution(mesh):
    return jax.shard_map(
        per_device,
        mesh=mesh,
        in_specs=(P("gx", "gy", "gz"), P("gx", "gy", "gz"), P("gx", "gy", "gz"), P("gx", "gy")),
        out_specs=(P("gx", "gy", "gz"), P("gz", "gx", "gy", None)),
        check_vma=False,
    )
```

time: 60.6 us -> 47 us (0.78)
  the two profiles are of different devices: /device:TPU:24 before, /device:TPU:81 now
where the time goes in v2:
time: 47 us; the launch traced here: 46.8 us
  starting transfers between devices  20.2 us (43%)
  Pallas kernels  14.2 us (30%)
  waiting for transfers between devices  11 us (23%)
  between operations  1.39 us (3%)
    pallas_call x7, Pallas kernels, call(): pl.pallas_call(kernel, out_shape=[jax.ShapeDtypeStruct(s, F32) for s in o...  14.2 us
    ppermute x4, starting transfers between devices, swap_b(): return lax.ppermute(v, names, pairs)  8.98 us
    all_to_all x1, starting transfers between devices, per_device(): got = lax.all_to_all(coef, 'gz', 0, 0, tiled=True)  8.69 us
    all_to_all x1, waiting for transfers between devices, per_device(): got = lax.all_to_all(coef, 'gz', 0, 0, tiled=True)  6.48 us
    ppermute x4, starting transfers between devices, swap_a(): lax.ppermute(v, axis, [(i, i ^ 1) for i in range(lax.axis_size(axis))])  2.57 us
    ppermute x4, waiting for transfers between devices, swap_a(): lax.ppermute(v, axis, [(i, i ^ 1) for i in range(lax.axis_size(axis))])  2.47 us
    ppermute x4, waiting for transfers between devices, swap_b(): return lax.ppermute(v, names, pairs)  2.01 us
  transfers between devices with their start and end apart: 9, of which 4 were waited for; matrix products, arithmetic and copies ran while one was open for 0% of the time, Pallas kernels for 13%

profile of v2, /device:TPU:81, one launch (start us, length us, event | category | flops | bytes accessed | tf_op | source)
XLA Modules:
  0.0 46.8 jit_solution(16777248166897846606)
XLA Ops:
  0.7 1.2 %shard_map.77 = (f32[24,8,128]{2,1,0:T(8,128)S(1)}, f32[24,8,128]{2,1,0:T(8,128)S(1)}) custom-call(f32[16,64,128]{2,1,0:T(8,128)} %p.7, f32[16,64,128]{2,1,0:T(8,128)} %q.7, s32[16,64,128]{2,1,0:T(8,128)} %m.7), custom_call_target="tpu_custom_call" | custom-call | bytes 262144 | tf_op jit(solution)/shard_map/pallas_call | solution.py:319
  1.9 1.1 %collective-permute-start = (f32[24,8,128]{2,1,0:T(8,128)S(1)}, f32[24,8,128]{2,1,0:T(8,128)S(1)}, u32[]{:S(2)}, u32[]{:S(2)}) collective-permute-start(f32[24,8,128]{2,1,0:T(8,128)S(1)} %get-tuple-element.26._), channel_id=1, source_target_pairs={{0,8},{8,0},{16,24},{24,16},{1,9},{9,1},{17,25},{25,17},{2,10},{10... | collective-permute-start | bytes 294920 | tf_op jit(solution)/shard_map/ppermute | solution.py:19
  3.0 0.0 collective-permute-start.1
  3.0 2.5 %collective-permute-done.ra = f32[24,8,128]{2,1,0:T(8,128)S(1)} collective-permute-done((f32[24,8,128]{2,1,0:T(8,128)S(1)}, f32[24,8,128]{2,1,0:T(8,128)S(1)}, u32[]{:S(2)}, u32[]{:S(2)}) %collective-permute-start) | collective-permute-done | bytes 98336 | tf_op jit(solution)/shard_map/ppermute | solution.py:19
  5.4 1.3 %collective-permute-done.1.rb = f32[24,8,128]{2,1,0:T(8,128)S(1)} collective-permute-done((f32[24,8,128]{2,1,0:T(8,128)S(1)}, f32[24,8,128]{2,1,0:T(8,128)S(1)}, u32[]{:S(2)}, u32[]{:S(2)}) %collective-permute-start.1) | collective-permute-done | bytes 98336 | tf_op jit(solution)/shard_map/ppermute | solution.py:35
  6.7 0.5 %shard_map.78 = (f32[2,72,128]{2,1,0:T(8,128)S(1)}, f32[2,72,128]{2,1,0:T(8,128)S(1)}, f32[48,8,128]{2,1,0:T(8,128)S(1)}) custom-call(f32[16,64,128]{2,1,0:T(8,128)S(1)} %copy-done, f32[16,64,128]{2,1,0:T(8,128)S(1)} %copy-done.1, s32[16,64,128]{2,1,0:T(8,128)S(1)} %copy-done.2, f32[24,8,128]{2,1,0:T(8,128)S(1)} %collective-permute-done.ra, ...), custom_call_target="tpu_custom_call" | custom-call | flops 10000000000 | bytes 262144 | tf_op jit(solution)/shard_map/pallas_call | solution.py:319
  7.2 1.3 %collective-permute-start.2 = (f32[2,72,128]{2,1,0:T(8,128)S(1)}, f32[2,72,128]{2,1,0:T(8,128)S(1)}, u32[]{:S(2)}, u32[]{:S(2)}) collective-permute-start(f32[2,72,128]{2,1,0:T(8,128)S(1)} %get-tuple-element.29), channel_id=1, source_target_pairs={{0,1},{1,0},{2,3},{3,2},{4,5},{5,4},{6,7},{7,6},{8,9},{9,8},{10,11... | collective-permute-start | bytes 221192 | tf_op jit(solution)/shard_map/ppermute | solution.py:19
  8.5 2.1 %collective-permute-start.3 = (f32[2,72,128]{2,1,0:T(8,128)S(1)}, f32[2,72,128]{2,1,0:T(8,128)S(1)}, u32[]{:S(2)}, u32[]{:S(2)}) collective-permute-start(f32[2,72,128]{2,1,0:T(8,128)S(1)} %get-tuple-element.30), channel_id=1, source_target_pairs={{0,32},{1,2},{2,1},{3,4},{4,3},{5,6},{6,5},{7,39},{32,0},{33,34},{... | collective-permute-start | bytes 221192 | tf_op jit(solution)/shard_map/ppermute | solution.py:35
  10.7 0.1 collective-permute-start.4
  10.8 4.6 %collective-permute-start.5 = (f32[10,64,128]{2,1,0:T(8,128)S(1)}, f32[10,64,128]{2,1,0:T(8,128)S(1)}, u32[]{:S(2)}, u32[]{:S(2)}) collective-permute-start(f32[10,64,128]{2,1,0:T(8,128)S(1)} %get-tuple-element.45), channel_id=1, source_target_pairs={{0,8},{32,64},{64,32},{96,128},{128,96},{160,192},{192,160},{224,2... | collective-permute-start | bytes 983048 | tf_op jit(solution)/shard_map/ppermute | solution.py:35
  15.4 0.0 collective-permute-done.2.ra
  15.4 0.0 collective-permute-done.3.rb
  15.4 0.6 %shard_map.81 = (f32[152,128]{1,0:T(8,128)S(1)}, f32[152,128]{1,0:T(8,128)S(1)}) custom-call(f32[48,8,128]{2,1,0:T(8,128)S(1)} %get-tuple-element.28.yh, f32[2,72,128]{2,1,0:T(8,128)S(1)} %collective-permute-done.2.ra, f32[2,72,128]{2,1,0:T(8,128)S(1)} %collective-permute-done.3.rb), custom_call_target="tpu_custom_call" | custom-call | flops 10000000000 | bytes 262144 | tf_op jit(solution)/shard_map/pallas_call | solution.py:319
  15.9 0.1 collective-permute-start.6
  16.0 0.0 copy-start.3
  16.1 0.0 copy-start.4
  16.1 2.3 %collective-permute-start.7 = (f32[152,128]{1,0:T(8,128)S(1)}, f32[152,128]{1,0:T(8,128)S(1)}, u32[]{:S(2)}, u32[]{:S(2)}) collective-permute-start(f32[152,128]{1,0:T(8,128)S(1)} %get-tuple-element.47), channel_id=1, source_target_pairs={{0,8},{32,64},{64,32},{96,128},{128,96},{160,192},{192,160},{224,2... | collective-permute-start | bytes 233480 | tf_op jit(solution)/shard_map/ppermute | solution.py:35
  18.4 5.4 %shard_map.79 = (f32[24,88,128]{2,1,0:T(8,128)S(1)}, f32[24,88,128]{2,1,0:T(8,128)S(1)}, f32[24,88,128]{2,1,0:T(8,128)S(1)}, f32[24,88,128]{2,1,0:T(8,128)S(1)},...) custom-call(f32[16,64,128]{2,1,0:T(8,128)S(1)} %copy-done, ...), custom_call_target="tpu_custom_call" | custom-call | flops 10000000000 | bytes 262144 | tf_op jit(solution)/shard_map/pallas_call | solution.py:319
  23.8 0.0 collective-permute-done.6.args_15_
  23.8 0.7 %collective-permute-done.7.args_16_ = f32[152,128]{1,0:T(8,128)S(1)} collective-permute-done((f32[152,128]{1,0:T(8,128)S(1)}, f32[152,128]{1,0:T(8,128)S(1)}, u32[]{:S(2)}, u32[]{:S(2)}) %collective-permute-start.7) | collective-permute-done | bytes 77856 | tf_op jit(solution)/shard_map/ppermute | solution.py:35
  24.6 5.6 %shard_map.82 = (f32[24,88,128]{2,1,0:T(8,128)S(1)}, f32[24,88,128]{2,1,0:T(8,128)S(1)}, f32[24,88,128]{2,1,0:T(8,128)S(1)}, f32[24,88,128]{2,1,0:T(8,128)S(1)},...) custom-call(f32[24,88,128]{2,1,0:T(8,128)S(1)} %get-tuple-element.31, ...), custom_call_target="tpu_custom_call", output_to_operand_aliasing={{0}: (0, {}), {1}: (1, {}), {2}: (2, {}), {3}: (3, {}), {4}... | custom-call | bytes 8388608 | tf_op jit(solution)/shard_map/pallas_call | solution.py:319
  30.2 8.7 %all-to-all-start = ((f32[8,128,128]{2,1,0:T(8,128)}), f32[8,128,128]{2,1,0:T(8,128)S(1)}, u32[]{:S(2)}, u32[]{:S(2)}) async-start(f32[8,128,128]{2,1,0:T(8,128)} %get-tuple-element.49), calls=%async_computation | async-start | bytes 1048576 | tf_op jit(solution)/shard_map/all_to_all | solution.py:365
  39.5 6.5 %all-to-all-done.got = f32[8,128,128]{2,1,0:T(8,128)S(1)} async-done(((f32[8,128,128]{2,1,0:T(8,128)}), f32[8,128,128]{2,1,0:T(8,128)S(1)}, u32[]{:S(2)}, u32[]{:S(2)}) %all-to-all-start) | async-done | bytes 524320 | tf_op jit(solution)/shard_map/all_to_all | solution.py:365
  46.0 0.8 %shard_map.83 = f32[1,8,32,512]{3,2,1,0:T(8,128)} custom-call(s32[1,1]{1,0:T(1,128)S(6)} %copy.34.writer, f32[8,128,128]{2,1,0:T(8,128)S(1)} %all-to-all-done.got), custom_call_target="tpu_custom_call" | custom-call | bytes 262144 | tf_op jit(solution)/shard_map/pallas_call | solution.py:319
  (11 shorter events, 0.1 us)
Async XLA Ops:
  0.6 6.1 %copy-start = (f32[16,64,128]{2,1,0:T(8,128)S(1)}, f32[16,64,128]{2,1,0:T(8,128)}, u32[]{:S(2)}) copy-start(f32[16,64,128]{2,1,0:T(8,128)} %p.7) | copy-start | bytes 1572868
  0.6 6.1 %copy-start.1 = (f32[16,64,128]{2,1,0:T(8,128)S(1)}, f32[16,64,128]{2,1,0:T(8,128)}, u32[]{:S(2)}) copy-start(f32[16,64,128]{2,1,0:T(8,128)} %q.7) | copy-start | bytes 1572868
  0.6 6.1 %copy-start.2 = (s32[16,64,128]{2,1,0:T(8,128)S(1)}, s32[16,64,128]{2,1,0:T(8,128)}, u32[]{:S(2)}) copy-start(s32[16,64,128]{2,1,0:T(8,128)} %m.7) | copy-start | bytes 1572868
  1.9 3.6 %collective-permute-start = (f32[24,8,128]{2,1,0:T(8,128)S(1)}, f32[24,8,128]{2,1,0:T(8,128)S(1)}, u32[]{:S(2)}, u32[]{:S(2)}) collective-permute-start(f32[24,8,128]{2,1,0:T(8,128)S(1)} %get-tuple-element.26._), channel_id=1, source_target_pairs={{0,8},{8,0},{16,24},{24,16},{1,9},{9,1},{17,25},{25,17},{2,10},{10... | collective-permute-start | bytes 294920 | tf_op jit(solution)/shard_map/ppermute | solution.py:19
  3.0 3.8 %collective-permute-start.1 = (f32[24,8,128]{2,1,0:T(8,128)S(1)}, f32[24,8,128]{2,1,0:T(8,128)S(1)}, u32[]{:S(2)}, u32[]{:S(2)}) collective-permute-start(f32[24,8,128]{2,1,0:T(8,128)S(1)} %get-tuple-element.27), channel_id=1, source_target_pairs={{0,32},{8,16},{16,8},{24,56},{32,0},{40,48},{48,40},{56,24},{64,96... | collective-permute-start | bytes 294920 | tf_op jit(solution)/shard_map/ppermute | solution.py:35
  7.2 8.1 %collective-permute-start.2 = (f32[2,72,128]{2,1,0:T(8,128)S(1)}, f32[2,72,128]{2,1,0:T(8,128)S(1)}, u32[]{:S(2)}, u32[]{:S(2)}) collective-permute-start(f32[2,72,128]{2,1,0:T(8,128)S(1)} %get-tuple-element.29), channel_id=1, source_target_pairs={{0,1},{1,0},{2,3},{3,2},{4,5},{5,4},{6,7},{7,6},{8,9},{9,8},{10,11... | collective-permute-start | bytes 221192 | tf_op jit(solution)/shard_map/ppermute | solution.py:19
  8.5 6.8 %collective-permute-start.3 = (f32[2,72,128]{2,1,0:T(8,128)S(1)}, f32[2,72,128]{2,1,0:T(8,128)S(1)}, u32[]{:S(2)}, u32[]{:S(2)}) collective-permute-start(f32[2,72,128]{2,1,0:T(8,128)S(1)} %get-tuple-element.30), channel_id=1, source_target_pairs={{0,32},{1,2},{2,1},{3,4},{4,3},{5,6},{6,5},{7,39},{32,0},{33,34},{... | collective-permute-start | bytes 221192 | tf_op jit(solution)/shard_map/ppermute | solution.py:35
  10.7 13.8 %collective-permute-start.4 = (f32[10,64,128]{2,1,0:T(8,128)S(1)}, f32[10,64,128]{2,1,0:T(8,128)S(1)}, u32[]{:S(2)}, u32[]{:S(2)}) collective-permute-start(f32[10,64,128]{2,1,0:T(8,128)S(1)} %get-tuple-element.44), channel_id=1, source_target_pairs={{0,32},{32,0},{64,96},{96,64},{128,160},{160,128},{192,224},{224,1... | collective-permute-start | bytes 983048 | tf_op jit(solution)/shard_map/ppermute | solution.py:19
  10.8 13.8 %collective-permute-start.5 = (f32[10,64,128]{2,1,0:T(8,128)S(1)}, f32[10,64,128]{2,1,0:T(8,128)S(1)}, u32[]{:S(2)}, u32[]{:S(2)}) collective-permute-start(f32[10,64,128]{2,1,0:T(8,128)S(1)} %get-tuple-element.45), channel_id=1, source_target_pairs={{0,8},{32,64},{64,32},{96,128},{128,96},{160,192},{192,160},{224,2... | collective-permute-start | bytes 983048 | tf_op jit(solution)/shard_map/ppermute | solution.py:35
  15.9 7.9 %collective-permute-start.6 = (f32[152,128]{1,0:T(8,128)S(1)}, f32[152,128]{1,0:T(8,128)S(1)}, u32[]{:S(2)}, u32[]{:S(2)}) collective-permute-start(f32[152,128]{1,0:T(8,128)S(1)} %get-tuple-element.46), channel_id=1, source_target_pairs={{0,32},{32,0},{64,96},{96,64},{128,160},{160,128},{192,224},{224,1... | collective-permute-start | bytes 233480 | tf_op jit(solution)/shard_map/ppermute | solution.py:19
  16.0 8.5 %copy-start.3 = (f32[256,128]{1,0:T(8,128)S(1)}, f32[256,128]{1,0:T(8,128)}, u32[]{:S(2)}) copy-start(f32[256,128]{1,0:T(8,128)} %constant.4.clone.args_17_) | copy-start | bytes 393220
  16.1 8.5 %copy-start.4 = (f32[128,256]{1,0:T(8,128)S(1)}, f32[128,256]{1,0:T(8,128)}, u32[]{:S(2)}) copy-start(f32[128,256]{1,0:T(8,128)} %constant.5.clone.args_18_) | copy-start | bytes 393220
  16.1 8.5 %collective-permute-start.7 = (f32[152,128]{1,0:T(8,128)S(1)}, f32[152,128]{1,0:T(8,128)S(1)}, u32[]{:S(2)}, u32[]{:S(2)}) collective-permute-start(f32[152,128]{1,0:T(8,128)S(1)} %get-tuple-element.47), channel_id=1, source_target_pairs={{0,8},{32,64},{64,32},{96,128},{128,96},{160,192},{192,160},{224,2... | collective-permute-start | bytes 233480 | tf_op jit(solution)/shard_map/ppermute | solution.py:35
  30.2 15.8 %all-to-all-start = ((f32[8,128,128]{2,1,0:T(8,128)}), f32[8,128,128]{2,1,0:T(8,128)S(1)}, u32[]{:S(2)}, u32[]{:S(2)}) async-start(f32[8,128,128]{2,1,0:T(8,128)} %get-tuple-element.49), calls=%async_computation | async-start | bytes 1048576 | tf_op jit(solution)/shard_map/all_to_all | solution.py:365

commit v3 on v2

--- a/solution.py
+++ b/solution.py
@@ -33,6 +33,9 @@
             j = i + 1 if i % 2 else i - 1
             pairs.append((flat(i, o), flat(j, o) if 0 <= j < n else flat(i, o ^ 1)))
     return lax.ppermute(v, names, pairs)
+
+
+FLOPS_Z, FLOPS_X, FLOPS_IN = 10**9, 10**9, 10**10
 
 
 def dct_rows():
@@ -106,11 +109,14 @@
         yb[t] = jnp.where(even, down, up)
 
 
-def pack_faces(p, q, m, _, xa, xb):
-    even = is_even("gx")
-    for out, right in ((xa, even), (xb, jnp.logical_not(even))):
-        for k, (arr, x) in enumerate(face_items(right)):
-            out[k] = load(p, q, m, arr, x)
+def pack_face(lo, hi, p, q, m, _, xb):
+    for k, (arr, x) in enumerate(face_items(jnp.logical_not(is_even("gx")))[lo:hi]):
+        xb[k] = load(p, q, m, arr, x)
+
+
+def pack_face_last(writer, p, q, m, _, xb, mine):
+    pack_face(CUT, N_FACE, p, q, m, _, xb)
+    mine[...] = jnp.full(mine.shape, (writer[0, 0] == lax.axis_index("gz")).astype(F32))
 
 
 def pack_z(p, q, m, ra, rb, za, zb, yh):
@@ -149,6 +155,8 @@
 TOP = 8
 TALL = TOP + ROWS + 8
 CORNER = 8 * N_FACE + ROWS
+MAIN = N_FACE * Y
+CUT = N_FACE // 2
 
 
 def z_sides(ra, rb, tile):
@@ -163,7 +171,7 @@
     return pltpu.roll(v, (Z - 4 * s) % Z, 1) if s else v
 
 
-def pack_x(yh, ra, rb, xac, xbc, zh):
+def pack_x(p, q, m, yh, ra, rb, _, xa, xbc, zh):
     lane = iota((ROWS, Z), 1)
     edge = set(range(W)) | set(range(X - W, X))
     for tile in range(2):
@@ -175,15 +183,17 @@
     even_x = is_even("gx")
     slot = lane // 8
 
-    def corners(right, out):
+    def corners(right, out, base):
         acc = jnp.zeros((ROWS, Z), F32)
         for k, (arr, x) in enumerate(face_items(right)):
-            out[8 * k : 8 * k + 8, :] = yh[arr * X + x]
+            out[base + 8 * k : base + 8 * k + 8, :] = yh[arr * X + x]
             acc = jnp.where(slot == k, pltpu.roll(zh[arr * X + x], 8 * k + 4, 1), acc)
-        out[8 * N_FACE : CORNER, :] = acc
-
-    corners(jnp.logical_not(even_x), xbc)
-    corners(even_x, xac)
+        out[base + 8 * N_FACE : base + CORNER, :] = acc
+
+    corners(jnp.logical_not(even_x), xbc, 0)
+    corners(even_x, xa, MAIN)
+    for k, (arr, x) in enumerate(face_items(even_x)):
+        xa[Y * k : Y * k + Y, :] = load(p, q, m, arr, x)
 
 
 def put_rows(ref, s, v):
@@ -196,11 +206,12 @@
     ref[s, TOP : TOP + W, :] = v[W:]
 
 
-def update(out, now, old, gain, s, halo):
-    size = 24
+def update(out, now, old, gain, s, last_step):
+    size = 32 if last_step else 24
     first = iota((size, Z), 1) == 0
     last = iota((size, Z), 1) == Z - 1
-    for r in range(TOP, TOP + ROWS, size):
+    start, count = (TOP + W, Y) if last_step else (TOP, ROWS)
+    for r in range(start, start + count, size):
         here, above, below = slice(r, r + size), slice(r - 1, r + size - 1), slice(r + 1, r + size + 1)
         c, h = now[0][s, here, :], now[1][s, here, :]
         cr, hr = pltpu.roll(c, 1, 1), pltpu.roll(h, 1, 1)
@@ -209,10 +220,14 @@
             jnp.where(first, hr, cr) + jnp.where(last, hl, cl),
             jnp.where(first, cr, hr) + jnp.where(last, cl, hl),
         )
-        for i in range(2 if halo else 1):
+        for i in range(1 if last_step else 2):
             total = now[i][s - 1, here, :] + now[i][s + 1, here, :]
             total = total + now[i][s, above, :] + now[i][s, below, :] + along_z[i]
-            out[i][s, here, :] = (total * (1.0 / 3.0) - old[i][s, here, :]) * gain[i][s, here, :]
+            v = (total * (1.0 / 3.0) - old[i][s, here, :]) * gain[i][s, here, :]
+            if last_step:
+                out[0][s - W, r - start : r - start + size, :] = v
+            else:
+                out[i][s, here, :] = v
 
 
 def unflatten(refs):
@@ -221,9 +236,16 @@
 
 
 N_EXT = 2 * (2 + ITERS) + 1
-
-
-def run_inside(p, q, m, yh, ra, rb, *refs):
+EXT = [(SLOTS, TALL, Z)] * (N_EXT - 1) + [(X, Y, Z)]
+
+
+def unpack_face(ext, lo, hi, xb):
+    keep_b = b_is_inside("gx")
+    for k, (arr, s) in enumerate(halo_slots(jnp.logical_not(is_even("gx")))[lo:hi]):
+        ext[arr][0][s, TOP + W : TOP + W + Y, :] = jnp.where(keep_b, xb[k], 0.0)
+
+
+def run_inside(p, q, m, yh, ra, rb, xb1, *refs):
     old, gain, level = unflatten(refs)
     ext = (level[0], old, gain)
     lane = iota((ROWS, Z), 1)
@@ -237,49 +259,48 @@
         for x in range(X):
             ext[arr][0][W + x, TOP + W : TOP + W + Y, :] = load(p, q, m, arr, x)
             put_edges(ext[arr][0], W + x, yh[arr * X + x])
+    unpack_face(ext, 0, CUT, xb1)
     for t in range(1, ITERS + 1):
         before = level[t - 2] if t >= 2 else old
 
         def body(j, carry, t=t, before=before):
-            update(level[t], level[t - 1], before, gain, W + t + j, t < ITERS)
+            update(level[t], level[t - 1], before, gain, W + t + j, t == ITERS)
             return carry
 
-        lax.fori_loop(0, X - 2 * t, body, 0)
+        lax.fori_loop(0, X - 2 * t, body, 0, unroll=True)
 
 
 def run_rest(*args):
-    xam, xbm, xac, xbc, dz, dy = args[N_EXT : N_EXT + 6]
-    refs = args[N_EXT + 6 : 2 * N_EXT + 6]
-    pressure, coef = args[2 * N_EXT + 6 :]
+    xb2, xa, xbc, dz, dy = args[N_EXT : N_EXT + 5]
+    refs = args[N_EXT + 5 : 2 * N_EXT + 5]
+    coef, pressure, sem = args[2 * N_EXT + 5 :]
     old, gain, level = unflatten(refs)
     ext = (level[0], old, gain)
     even = is_even("gx")
     keep_b = b_is_inside("gx")
 
-    def unpack(right, main, corner, fix):
-        z_tile = fix(corner[8 * N_FACE : CORNER, :])
+    def unpack(right, corner, base, fix):
+        z_tile = fix(corner[base + 8 * N_FACE : base + CORNER, :])
         for k, (arr, s) in enumerate(halo_slots(right)):
-            ext[arr][0][s, TOP + W : TOP + W + Y, :] = fix(main[k])
-            put_edges(ext[arr][0], s, fix(corner[8 * k : 8 * k + 8, :]))
+            put_edges(ext[arr][0], s, fix(corner[base + 8 * k : base + 8 * k + 8, :]))
             put_rows(ext[arr][1], s, pltpu.roll(z_tile, Z - 8 * k - 4, 1))
 
-    unpack(even, xam, xac, lambda v: v)
-    unpack(jnp.logical_not(even), xbm, xbc, lambda v: jnp.where(keep_b, v, 0.0))
+    for k, (arr, s) in enumerate(halo_slots(even)):
+        ext[arr][0][s, TOP + W : TOP + W + Y, :] = xa[Y * k : Y * k + Y, :]
+    unpack(even, xa, MAIN, lambda v: v)
+    unpack_face(ext, CUT, N_FACE, xb2)
+    unpack(jnp.logical_not(even), xbc, 0, lambda v: jnp.where(keep_b, v, 0.0))
     for t in range(1, ITERS + 1):
         before = level[t - 2] if t >= 2 else old
-
-        def body(j, carry, t=t, before=before):
-            s = jnp.where(j < W, t + j, X + W - t + j - W)
-            update(level[t], level[t - 1], before, gain, s, t < ITERS)
-            return carry
-
-        lax.fori_loop(0, 2 * W, body, 0)
+        for s in [*range(t, t + W), *range(X + W - t, X + 2 * W - t)]:
+            update(level[t], level[t - 1], before, gain, s, t == ITERS)
+    final = level[ITERS][0]
+    copy = pltpu.make_async_copy(final, pressure, sem)
+    copy.start()
     rows = dct_rows()
     parts = []
     for b in range(X // 8):
-        f = [level[ITERS][0][W + 8 * b + i, TOP + W : TOP + W + Y, :] for i in range(8)]
-        for i in range(8):
-            pressure[8 * b + i] = f[i]
+        f = [final[8 * b + i] for i in range(8)]
         plus = [f[i] + f[7 - i] for i in range(4)]
         minus = [f[i] - f[7 - i] for i in range(4)]
         for k in range(4):
@@ -290,37 +311,32 @@
     right = jnp.concatenate(parts[half:], axis=0)
     both = jnp.concatenate([left, right], axis=1)
     along_z = jnp.dot(both, dz[...], precision=lax.Precision.HIGHEST, preferred_element_type=F32)
-    result = jnp.dot(dy[...], along_z, precision=lax.Precision.HIGHEST, preferred_element_type=F32)
-    for d in range(coef.shape[0]):
-        coef[d] = result
-
-
-def place(writer, got, out):
-    mine = writer[0, 0] == lax.axis_index("gz")
-    low = iota((Y // 2, Z), 1) < Z // 2
-
-    @pl.when(mine)
-    def _():
-        for t in range(got.shape[0] // 2):
-            for h in range(X // 4):
-                a = got[2 * t, h * (Y // 2) : (h + 1) * (Y // 2), :]
-                b = got[2 * t + 1, h * (Y // 2) : (h + 1) * (Y // 2), :]
-                out[0, h, :, t * Z : (t + 1) * Z] = jnp.where(low, a, pltpu.roll(b, Z // 2, 1))
-                out[0, h + X // 4, :, t * Z : (t + 1) * Z] = jnp.where(low, pltpu.roll(a, Z // 2, 1), b)
-
-    @pl.when(jnp.logical_not(mine))
-    def _():
-        out[...] = jnp.zeros_like(out)
-
-
-def call(kernel, outs, *args, first=pltpu.VMEM, n_first=0, scratch=(), aliases=None, cost=1 << 18, flops=0):
+    coef[...] = jnp.dot(dy[...], along_z, precision=lax.Precision.HIGHEST, preferred_element_type=F32)
+    copy.wait()
+
+
+def place(mine, got, out):
+    half, rows = X // 4, Y // 2
+    low = iota((rows, Z), 1) < Z // 2
+    keep = jnp.concatenate([mine[...]] * (rows // 8), axis=0) > 0.5
+    for t in range(got.shape[0] // 2):
+        for h in range(half):
+            a = got[2 * t, h * rows : (h + 1) * rows, :]
+            b = got[2 * t + 1, h * rows : (h + 1) * rows, :]
+            at = slice(t * Z, (t + 1) * Z)
+            out[0, h, :, at] = jnp.where(keep, jnp.where(low, a, pltpu.roll(b, Z // 2, 1)), 0.0)
+            out[0, h + half, :, at] = jnp.where(keep, jnp.where(low, pltpu.roll(a, Z // 2, 1), b), 0.0)
+
+
+def call(kernel, outs, *args, first=pltpu.VMEM, n_first=0, n_far=0, scratch=(), aliases=None, cost=1 << 18, flops=0):
     vm = pl.BlockSpec(memory_space=pltpu.VMEM)
+    far = pl.BlockSpec(memory_space=pltpu.HBM)
     other = pl.BlockSpec(memory_space=first)
     return pl.pallas_call(
         kernel,
         out_shape=[jax.ShapeDtypeStruct(s, F32) for s in outs],
         in_specs=[other] * n_first + [vm] * (len(args) - n_first),
-        out_specs=[vm] * len(outs),
+        out_specs=[vm] * (len(outs) - n_far) + [far] * n_far,
         scratch_shapes=list(scratch),
         input_output_aliases=aliases or {},
         cost_estimate=pl.CostEstimate(flops=flops, transcendentals=0, bytes_accessed=cost),
@@ -345,25 +361,31 @@
         pack_y, [(n_y, 8, Z), (n_y, 8, Z)], *far, first=pltpu.HBM, n_first=3,
         scratch=[*edges, pltpu.SemaphoreType.DMA((6,))],
     )
-    ya0 = ya
+    (xb1,) = call(functools.partial(pack_face, 0, CUT), [(CUT, Y, Z)], p, q, m, ya)
     ya, yb = swap_a(ya, "gy"), swap_b(yb, "gy")
-    xa, xb = call(pack_faces, [(N_FACE, Y, Z)] * 2, p, q, m, ya0)
-    xa, xb = swap_a(xa, "gx"), swap_b(xb, "gx")
-    za, zb, yh = call(pack_z, [(2, ROWS, Z), (2, ROWS, Z), (3 * X, 8, Z)], p, q, m, ya, yb, flops=10000000000)
+    xb1 = swap_b(xb1, "gx")
+    za, zb, yh = call(
+        pack_z, [(2, ROWS, Z), (2, ROWS, Z), (3 * X, 8, Z)], p, q, m, ya, yb, flops=FLOPS_Z
+    )
+    xb2, mine = call(
+        pack_face_last, [(N_FACE - CUT, Y, Z), (8, Z)], writer, p, q, m, yh, first=pltpu.SMEM, n_first=1
+    )
     za, zb = swap_a(za, "gz"), swap_b(zb, "gz")
-    xac, xbc = call(
-        pack_x, [(CORNER, Z), (CORNER, Z)], yh, za, zb, scratch=[pltpu.VMEM((3 * X, ROWS, Z), F32)], flops=10000000000
-    )
-    xac, xbc = swap_a(xac, "gx"), swap_b(xbc, "gx")
-    ext = call(run_inside, [(SLOTS, TALL, Z)] * N_EXT, p, q, m, yh, za, zb, flops=10000000000)
+    xb2 = swap_b(xb2, "gx")
+    xa, xbc = call(
+        pack_x, [(MAIN + CORNER, Z), (CORNER, Z)], p, q, m, yh, za, zb, xb1, flops=FLOPS_X,
+        scratch=[pltpu.VMEM((3 * X, ROWS, Z), F32)],
+    )
+    xa, xbc = swap_a(xa, "gx"), swap_b(xbc, "gx")
+    ext = call(run_inside, EXT, p, q, m, yh, za, zb, xb1, flops=FLOPS_IN)
     dz, dy = matrices()
     n = lax.axis_size("gz")
-    *_, pressure, coef = call(
-        run_rest, [(SLOTS, TALL, Z)] * N_EXT + [(X, Y, Z), (n, 2 * Y, Z)], *ext, xa, xb, xac, xbc, dz, dy,
-        aliases={i: i for i in range(N_EXT)}, cost=8 << 20,
-    )
-    got = lax.all_to_all(coef, "gz", 0, 0, tiled=True)
-    (out,) = call(place, [(1, X // 2, Y // 2, n * Z // 2)], writer, got, first=pltpu.SMEM, n_first=1)
+    *_, coef, pressure = call(
+        run_rest, [*EXT, (2 * Y, Z), (X, Y, Z)], *ext, xb2, xa, xbc, dz, dy,
+        aliases={i: i for i in range(N_EXT)}, cost=8 << 20, n_far=1, scratch=[pltpu.SemaphoreType.DMA],
+    )
+    got = lax.all_to_all(jnp.broadcast_to(coef, (n, 2 * Y, Z)), "gz", 0, 0, tiled=True)
+    (out,) = call(place, [(1, X // 2, Y // 2, n * Z // 2)], mine, got)
     return pressure, out
 
 

time: 47 us -> 42.8 us (0.911)
  the two profiles are of different devices: /device:TPU:81 before, /device:TPU:72 now
where the time goes in v3:
time: 42.8 us; the launch traced here: 42.7 us
  blocking collectives  18.8 us (44%)
  starting transfers between devices  8.21 us (19%)
  Pallas kernels  7.79 us (18%)
  waiting for transfers between devices  6.44 us (15%)
  between operations  1.44 us (3%)
    all_to_all x1, blocking collectives, per_device(): lax.all_to_all(jnp.broadcast_to(coef, (n, 2 * Y, Z)), 'gz', 0, 0, tiled=T...  18.8 us
    pallas_call x8, Pallas kernels, call(): pl.pallas_call(kernel, out_shape=[jax.ShapeDtypeStruct(s, F32) for s in o...  7.79 us
    ppermute x3, starting transfers between devices, swap_a(): lax.ppermute(v, axis, [(i, i ^ 1) for i in range(lax.axis_size(axis))])  5.6 us
    ppermute x3, waiting for transfers between devices, swap_a(): lax.ppermute(v, axis, [(i, i ^ 1) for i in range(lax.axis_size(axis))])  3.63 us
    ppermute x5, waiting for transfers between devices, swap_b(): return lax.ppermute(v, names, pairs)  2.81 us
    ppermute x5, starting transfers between devices, swap_b(): return lax.ppermute(v, names, pairs)  2.61 us
  transfers between devices with their start and end apart: 8, of which 3 were waited for; matrix products, arithmetic and copies ran while one was open for 0% of the time, Pallas kernels for 8%

profile of v3, /device:TPU:72, one launch (start us, length us, event | category | flops | bytes accessed | tf_op | source)
XLA Modules:
  0.0 42.7 jit_solution(4206104950852084476)
XLA Ops:
  0.7 1.2 %shard_map.77 = (f32[24,8,128]{2,1,0:T(8,128)S(1)}, f32[24,8,128]{2,1,0:T(8,128)S(1)}) custom-call(f32[16,64,128]{2,1,0:T(8,128)} %p.11, f32[16,64,128]{2,1,0:T(8,128)} %q.11, s32[16,64,128]{2,1,0:T(8,128)} %m.11), custom_call_target="tpu_custom_call" | custom-call | bytes 262144 | tf_op jit(solution)/shard_map/pallas_call | solution.py:335
  1.9 1.7 %collective-permute-start.1 = (f32[24,8,128]{2,1,0:T(8,128)S(1)}, f32[24,8,128]{2,1,0:T(8,128)S(1)}, u32[]{:S(2)}, u32[]{:S(2)}) collective-permute-start(f32[24,8,128]{2,1,0:T(8,128)S(1)} %get-tuple-element.27), channel_id=1, source_target_pairs={{0,32},{8,16},{16,8},{24,56},{32,0},{40,48},{48,40},{56,24},{64,96... | collective-permute-start | bytes 294920 | tf_op jit(solution)/shard_map/ppermute | solution.py:35
  3.5 0.0 collective-permute-start
  3.6 0.2 collective-permute-start.4
  3.8 2.8 %collective-permute-done.1.rb = f32[24,8,128]{2,1,0:T(8,128)S(1)} collective-permute-done((f32[24,8,128]{2,1,0:T(8,128)S(1)}, f32[24,8,128]{2,1,0:T(8,128)S(1)}, u32[]{:S(2)}, u32[]{:S(2)}) %collective-permute-start.1) | collective-permute-done | bytes 98336 | tf_op jit(solution)/shard_map/ppermute | solution.py:35
  6.6 1.6 %collective-permute-done.ra = f32[24,8,128]{2,1,0:T(8,128)S(1)} collective-permute-done((f32[24,8,128]{2,1,0:T(8,128)S(1)}, f32[24,8,128]{2,1,0:T(8,128)S(1)}, u32[]{:S(2)}, u32[]{:S(2)}) %collective-permute-start) | collective-permute-done | bytes 98336 | tf_op jit(solution)/shard_map/ppermute | solution.py:19
  8.2 0.5 %shard_map.78 = (f32[2,72,128]{2,1,0:T(8,128)S(1)}, f32[2,72,128]{2,1,0:T(8,128)S(1)}, f32[48,8,128]{2,1,0:T(8,128)S(1)}) custom-call(f32[16,64,128]{2,1,0:T(8,128)S(1)} %copy-done, f32[16,64,128]{2,1,0:T(8,128)S(1)} %copy-done.1, s32[16,64,128]{2,1,0:T(8,128)S(1)} %copy-done.2, f32[24,8,128]{2,1,0:T(8,128)S(1)} %collective-permute-done.ra, ...), custom_call_target="tpu_custom_call" | custom-call | flops 1000000000 | bytes 262144 | tf_op jit(solution)/shard_map/pallas_call | solution.py:335
  8.7 1.6 %collective-permute-start.2 = (f32[2,72,128]{2,1,0:T(8,128)S(1)}, f32[2,72,128]{2,1,0:T(8,128)S(1)}, u32[]{:S(2)}, u32[]{:S(2)}) collective-permute-start(f32[2,72,128]{2,1,0:T(8,128)S(1)} %get-tuple-element.29), channel_id=1, source_target_pairs={{0,1},{1,0},{2,3},{3,2},{4,5},{5,4},{6,7},{7,6},{8,9},{9,8},{10,11... | collective-permute-start | bytes 221192 | tf_op jit(solution)/shard_map/ppermute | solution.py:19
  10.2 0.0 collective-permute-start.3
  10.9 0.1 collective-permute-start.5
  11.0 0.0 collective-permute-done.4.xb1._
  11.0 2.1 %collective-permute-done.2.ra = f32[2,72,128]{2,1,0:T(8,128)S(1)} collective-permute-done((f32[2,72,128]{2,1,0:T(8,128)S(1)}, f32[2,72,128]{2,1,0:T(8,128)S(1)}, u32[]{:S(2)}, u32[]{:S(2)}) %collective-permute-start.2) | collective-permute-done | bytes 73760 | tf_op jit(solution)/shard_map/ppermute | solution.py:19
  13.1 0.0 collective-permute-done.3.rb
  13.1 0.6 %shard_map.82 = (f32[792,128]{1,0:T(8,128)S(1)}, f32[152,128]{1,0:T(8,128)S(1)}) custom-call(f32[16,64,128]{2,1,0:T(8,128)S(1)} %copy-done, f32[16,64,128]{2,1,0:T(8,128)S(1)} %copy-done.1, s32[16,64,128]{2,1,0:T(8,128)S(1)} %copy-done.2, f32[48,8,128]{2,1,0:T(8,128)S(1)} %get-tuple-element.28.yh._, f32[2,72,128]{2,1,0:T(8,128)S(1)} %collective-permute-done.2.ra, ...), custom_call_target="tpu_custom_call" | custom-call | flops 1000000000 | bytes 262144 | tf_op jit(solution)/shard_map/pallas_call | solution.py:335
  13.7 0.7 %collective-permute-start.7 = (f32[152,128]{1,0:T(8,128)S(1)}, f32[152,128]{1,0:T(8,128)S(1)}, u32[]{:S(2)}, u32[]{:S(2)}) collective-permute-start(f32[152,128]{1,0:T(8,128)S(1)} %get-tuple-element.46), channel_id=1, source_target_pairs={{0,8},{32,64},{64,32},{96,128},{128,96},{160,192},{192,160},{224,2... | collective-permute-start | bytes 233480 | tf_op jit(solution)/shard_map/ppermute | solution.py:35
  14.3 4.0 %collective-permute-start.6 = (f32[792,128]{1,0:T(8,128)S(1)}, f32[792,128]{1,0:T(8,128)S(1)}, u32[]{:S(2)}, u32[]{:S(2)}) collective-permute-start(f32[792,128]{1,0:T(8,128)S(1)} %get-tuple-element.45), channel_id=1, source_target_pairs={{0,32},{32,0},{64,96},{96,64},{128,160},{160,128},{192,224},{224,1... | collective-permute-start | bytes 1216520 | tf_op jit(solution)/shard_map/ppermute | solution.py:19
  18.4 2.2 %shard_map.80 = (f32[24,88,128]{2,1,0:T(8,128)S(1)}, f32[24,88,128]{2,1,0:T(8,128)S(1)}, f32[24,88,128]{2,1,0:T(8,128)S(1)}, f32[24,88,128]{2,1,0:T(8,128)S(1)},...) custom-call(f32[16,64,128]{2,1,0:T(8,128)S(1)} %copy-done, ...), custom_call_target="tpu_custom_call" | custom-call | flops 10000000000 | bytes 262144 | tf_op jit(solution)/shard_map/pallas_call | solution.py:335
  20.5 0.0 collective-permute-done.7.args_15_
  20.6 0.0 collective-permute-done.5.args_13_
  20.6 0.0 collective-permute-done.6.args_14_
  20.6 0.0 copy-done.3
  20.6 2.3 %shard_map.83 = (f32[24,88,128]{2,1,0:T(8,128)S(1)}, f32[24,88,128]{2,1,0:T(8,128)S(1)}, f32[24,88,128]{2,1,0:T(8,128)S(1)}, f32[24,88,128]{2,1,0:T(8,128)S(1)},...) custom-call(f32[24,88,128]{2,1,0:T(8,128)S(1)} %get-tuple-element.31, ...), custom_call_target="tpu_custom_call", output_to_operand_aliasing={{0}: (0, {}), {1}: (1, {}), {2}: (2, {}), {3}: (3, {}), {4}... | custom-call | bytes 8388608 | tf_op jit(solution)/shard_map/pallas_call | solution.py:335
  22.9 18.8 %all_to_all.5.got = f32[8,128,128]{2,1,0:T(8,128)S(1)} all-to-all(f32[8,128,128]{2,1,0:T(8,128)S(1)} %broadcast_in_dim.3), channel_id=1, replica_groups=mesh['gx'=8,'gy'=4,'gz'=8] {'gz'}, dimensions={0} | all-to-all | bytes 1048576 | tf_op jit(solution)/shard_map/all_to_all | solution.py:387
  41.7 1.0 %shard_map.84 = f32[1,8,32,512]{3,2,1,0:T(8,128)} custom-call(f32[8,128]{1,0:T(8,128)S(1)} %get-tuple-element.48.mine, f32[8,128,128]{2,1,0:T(8,128)S(1)} %all_to_all.5.got), custom_call_target="tpu_custom_call" | custom-call | bytes 262144 | tf_op jit(solution)/shard_map/pallas_call | solution.py:335
  (12 shorter events, 0.1 us)
Async XLA Ops:
  0.6 2.9 %copy-start.2 = (s32[16,64,128]{2,1,0:T(8,128)S(1)}, s32[16,64,128]{2,1,0:T(8,128)}, u32[]{:S(2)}) copy-start(s32[16,64,128]{2,1,0:T(8,128)} %m.11) | copy-start | bytes 1572868
  0.6 2.9 %copy-start.1 = (f32[16,64,128]{2,1,0:T(8,128)S(1)}, f32[16,64,128]{2,1,0:T(8,128)}, u32[]{:S(2)}) copy-start(f32[16,64,128]{2,1,0:T(8,128)} %q.11) | copy-start | bytes 1572868
  0.6 2.9 %copy-start = (f32[16,64,128]{2,1,0:T(8,128)S(1)}, f32[16,64,128]{2,1,0:T(8,128)}, u32[]{:S(2)}) copy-start(f32[16,64,128]{2,1,0:T(8,128)} %p.11) | copy-start | bytes 1572868
  1.9 4.7 %collective-permute-start.1 = (f32[24,8,128]{2,1,0:T(8,128)S(1)}, f32[24,8,128]{2,1,0:T(8,128)S(1)}, u32[]{:S(2)}, u32[]{:S(2)}) collective-permute-start(f32[24,8,128]{2,1,0:T(8,128)S(1)} %get-tuple-element.27), channel_id=1, source_target_pairs={{0,32},{8,16},{16,8},{24,56},{32,0},{40,48},{48,40},{56,24},{64,96... | collective-permute-start | bytes 294920 | tf_op jit(solution)/shard_map/ppermute | solution.py:35
  3.5 4.6 %collective-permute-start = (f32[24,8,128]{2,1,0:T(8,128)S(1)}, f32[24,8,128]{2,1,0:T(8,128)S(1)}, u32[]{:S(2)}, u32[]{:S(2)}) collective-permute-start(f32[24,8,128]{2,1,0:T(8,128)S(1)} %get-tuple-element.26._), channel_id=1, source_target_pairs={{0,8},{8,0},{16,24},{24,16},{1,9},{9,1},{17,25},{25,17},{2,10},{10... | collective-permute-start | bytes 294920 | tf_op jit(solution)/shard_map/ppermute | solution.py:19
  3.6 7.4 %collective-permute-start.4 = (f32[5,64,128]{2,1,0:T(8,128)S(1)}, f32[5,64,128]{2,1,0:T(8,128)S(1)}, u32[]{:S(2)}, u32[]{:S(2)}) collective-permute-start(f32[5,64,128]{2,1,0:T(8,128)S(1)} %shard_map.79), channel_id=1, source_target_pairs={{0,8},{32,64},{64,32},{96,128},{128,96},{160,192},{192,160},{224,2... | collective-permute-start | bytes 491528 | tf_op jit(solution)/shard_map/ppermute | solution.py:35
  8.7 4.4 %collective-permute-start.2 = (f32[2,72,128]{2,1,0:T(8,128)S(1)}, f32[2,72,128]{2,1,0:T(8,128)S(1)}, u32[]{:S(2)}, u32[]{:S(2)}) collective-permute-start(f32[2,72,128]{2,1,0:T(8,128)S(1)} %get-tuple-element.29), channel_id=1, source_target_pairs={{0,1},{1,0},{2,3},{3,2},{4,5},{5,4},{6,7},{7,6},{8,9},{9,8},{10,11... | collective-permute-start | bytes 221192 | tf_op jit(solution)/shard_map/ppermute | solution.py:19
  10.2 2.9 %collective-permute-start.3 = (f32[2,72,128]{2,1,0:T(8,128)S(1)}, f32[2,72,128]{2,1,0:T(8,128)S(1)}, u32[]{:S(2)}, u32[]{:S(2)}) collective-permute-start(f32[2,72,128]{2,1,0:T(8,128)S(1)} %get-tuple-element.30), channel_id=1, source_target_pairs={{0,32},{1,2},{2,1},{3,4},{4,3},{5,6},{6,5},{7,39},{32,0},{33,34},{... | collective-permute-start | bytes 221192 | tf_op jit(solution)/shard_map/ppermute | solution.py:35
  10.9 9.6 %collective-permute-start.5 = (f32[5,64,128]{2,1,0:T(8,128)S(1)}, f32[5,64,128]{2,1,0:T(8,128)S(1)}, u32[]{:S(2)}, u32[]{:S(2)}) collective-permute-start(f32[5,64,128]{2,1,0:T(8,128)S(1)} %get-tuple-element.44), channel_id=1, source_target_pairs={{0,8},{32,64},{64,32},{96,128},{128,96},{160,192},{192,160},{224,2... | collective-permute-start | bytes 491528 | tf_op jit(solution)/shard_map/ppermute | solution.py:35
  13.7 6.9 %collective-permute-start.7 = (f32[152,128]{1,0:T(8,128)S(1)}, f32[152,128]{1,0:T(8,128)S(1)}, u32[]{:S(2)}, u32[]{:S(2)}) collective-permute-start(f32[152,128]{1,0:T(8,128)S(1)} %get-tuple-element.46), channel_id=1, source_target_pairs={{0,8},{32,64},{64,32},{96,128},{128,96},{160,192},{192,160},{224,2... | collective-permute-start | bytes 233480 | tf_op jit(solution)/shard_map/ppermute | solution.py:35
  14.3 6.2 %copy-start.3 = (f32[128,256]{1,0:T(8,128)S(1)}, f32[128,256]{1,0:T(8,128)}, u32[]{:S(2)}) copy-start(f32[128,256]{1,0:T(8,128)} %constant.5.clone.args_17_) | copy-start | bytes 393220
  14.3 6.2 %copy-start.4 = (f32[256,128]{1,0:T(8,128)S(1)}, f32[256,128]{1,0:T(8,128)}, u32[]{:S(2)}) copy-start(f32[256,128]{1,0:T(8,128)} %constant.4.clone.args_16_) | copy-start | bytes 393220
  14.3 6.2 %collective-permute-start.6 = (f32[792,128]{1,0:T(8,128)S(1)}, f32[792,128]{1,0:T(8,128)S(1)}, u32[]{:S(2)}, u32[]{:S(2)}) collective-permute-start(f32[792,128]{1,0:T(8,128)S(1)} %get-tuple-element.45), channel_id=1, source_target_pairs={{0,32},{32,0},{64,96},{96,64},{128,160},{160,128},{192,224},{224,1... | collective-permute-start | bytes 1216520 | tf_op jit(solution)/shard_map/ppermute | solution.py:19

commit v4 on v3

--- a/solution.py
+++ b/solution.py
@@ -78,6 +78,18 @@
     p0 = jnp.where(right, X - W, 0)
     q0 = jnp.where(right, X - W + 1, 0)
     return [(0, p0 + k) for k in range(W)] + [(a, q0 + k) for a in (1, 2) for k in range(W - 1)]
+
+
+def far_items(right):
+    p0 = jnp.where(right, X - W + 1, 0)
+    q0 = jnp.where(right, X - W + 2, 0)
+    return [(0, p0 + k) for k in range(W - 1)] + [(a, q0 + k) for a in (1, 2) for k in range(W - 2)]
+
+
+def far_slots(right):
+    p0 = jnp.where(right, X + W, 1)
+    q0 = jnp.where(right, X + W, 2)
+    return [(0, p0 + k) for k in range(W - 1)] + [(a, q0 + k) for a in (1, 2) for k in range(W - 2)]
 
 
 def halo_slots(right):
@@ -109,13 +121,12 @@
         yb[t] = jnp.where(even, down, up)
 
 
-def pack_face(lo, hi, p, q, m, _, xb):
-    for k, (arr, x) in enumerate(face_items(jnp.logical_not(is_even("gx")))[lo:hi]):
+def pack_far(p, q, m, _, xb):
+    for k, (arr, x) in enumerate(far_items(jnp.logical_not(is_even("gx")))):
         xb[k] = load(p, q, m, arr, x)
 
 
-def pack_face_last(writer, p, q, m, _, xb, mine):
-    pack_face(CUT, N_FACE, p, q, m, _, xb)
+def read_writer(writer, _, mine):
     mine[...] = jnp.full(mine.shape, (writer[0, 0] == lax.axis_index("gz")).astype(F32))
 
 
@@ -154,9 +165,10 @@
 SLOTS = X + 2 * W
 TOP = 8
 TALL = TOP + ROWS + 8
-CORNER = 8 * N_FACE + ROWS
 MAIN = N_FACE * Y
-CUT = N_FACE // 2
+NEAR_ALL = MAIN + 8 * N_FACE + ROWS
+N_FAR = 3 * W - 5
+FAR_LATE = Y + 8 * N_FAR + ROWS
 
 
 def z_sides(ra, rb, tile):
@@ -171,7 +183,17 @@
     return pltpu.roll(v, (Z - 4 * s) % Z, 1) if s else v
 
 
-def pack_x(p, q, m, yh, ra, rb, _, xa, xbc, zh):
+def next_layer(p, q, m, yh, zh, x):
+    c, t, h = p[x], yh[x], zh[x][:Y]
+    row, lane = iota((Y, Z), 0), iota((Y, Z), 1)
+    total = p[x - 1] + p[x + 1]
+    total = total + jnp.where(row == 0, t[7:8], pltpu.roll(c, 1, 0)) + jnp.where(row == Y - 1, t[0:1], pltpu.roll(c, Y - 1, 0))
+    total = total + jnp.where(lane == 0, pltpu.roll(h, 1, 1), pltpu.roll(c, 1, 1))
+    total = total + jnp.where(lane == Z - 1, pltpu.roll(h, Z - 1, 1), pltpu.roll(c, Z - 1, 1))
+    return (total * (1.0 / 3.0) - q[x]) * gain_of(m[x])
+
+
+def pack_x(p, q, m, yh, ra, rb, _, __, xa, xb, zh):
     lane = iota((ROWS, Z), 1)
     edge = set(range(W)) | set(range(X - W, X))
     for tile in range(2):
@@ -183,15 +205,17 @@
     even_x = is_even("gx")
     slot = lane // 8
 
-    def corners(right, out, base):
+    def corners(items, out, base):
         acc = jnp.zeros((ROWS, Z), F32)
-        for k, (arr, x) in enumerate(face_items(right)):
+        for k, (arr, x) in enumerate(items):
             out[base + 8 * k : base + 8 * k + 8, :] = yh[arr * X + x]
             acc = jnp.where(slot == k, pltpu.roll(zh[arr * X + x], 8 * k + 4, 1), acc)
-        out[base + 8 * N_FACE : base + CORNER, :] = acc
-
-    corners(jnp.logical_not(even_x), xbc, 0)
-    corners(even_x, xa, MAIN)
+        end = base + 8 * len(items)
+        out[end : end + ROWS, :] = acc
+
+    xb[:Y, :] = next_layer(p, q, m, yh, zh, jnp.where(even_x, W - 2, X - W + 1))
+    corners(far_items(jnp.logical_not(even_x)), xb, Y)
+    corners(face_items(even_x), xa, MAIN)
     for k, (arr, x) in enumerate(face_items(even_x)):
         xa[Y * k : Y * k + Y, :] = load(p, q, m, arr, x)
 
@@ -239,13 +263,7 @@
 EXT = [(SLOTS, TALL, Z)] * (N_EXT - 1) + [(X, Y, Z)]
 
 
-def unpack_face(ext, lo, hi, xb):
-    keep_b = b_is_inside("gx")
-    for k, (arr, s) in enumerate(halo_slots(jnp.logical_not(is_even("gx")))[lo:hi]):
-        ext[arr][0][s, TOP + W : TOP + W + Y, :] = jnp.where(keep_b, xb[k], 0.0)
-
-
-def run_inside(p, q, m, yh, ra, rb, xb1, *refs):
+def run_inside(p, q, m, yh, ra, rb, xf, *refs):
     old, gain, level = unflatten(refs)
     ext = (level[0], old, gain)
     lane = iota((ROWS, Z), 1)
@@ -259,7 +277,9 @@
         for x in range(X):
             ext[arr][0][W + x, TOP + W : TOP + W + Y, :] = load(p, q, m, arr, x)
             put_edges(ext[arr][0], W + x, yh[arr * X + x])
-    unpack_face(ext, 0, CUT, xb1)
+    keep_b = b_is_inside("gx")
+    for k, (arr, s) in enumerate(far_slots(jnp.logical_not(is_even("gx")))):
+        ext[arr][0][s, TOP + W : TOP + W + Y, :] = jnp.where(keep_b, xf[k], 0.0)
     for t in range(1, ITERS + 1):
         before = level[t - 2] if t >= 2 else old
 
@@ -270,30 +290,49 @@
         lax.fori_loop(0, X - 2 * t, body, 0, unroll=True)
 
 
-def run_rest(*args):
-    xb2, xa, xbc, dz, dy = args[N_EXT : N_EXT + 5]
-    refs = args[N_EXT + 5 : 2 * N_EXT + 5]
-    coef, pressure, sem = args[2 * N_EXT + 5 :]
+def unpack_corners(ext, slots, corner, base, fix):
+    end = base + 8 * len(slots)
+    z_tile = fix(corner[end : end + ROWS, :])
+    for k, (arr, s) in enumerate(slots):
+        put_edges(ext[arr][0], s, fix(corner[base + 8 * k : base + 8 * k + 8, :]))
+        put_rows(ext[arr][1], s, pltpu.roll(z_tile, Z - 8 * k - 4, 1))
+
+
+def run_side(right, old, gain, level, first_count):
+    for t in range(1, ITERS + 1):
+        before = level[t - 2] if t >= 2 else old
+        for j in range(first_count if t == 1 else W):
+            s = jnp.where(right, X + W - t + j, W + t - 1 - j)
+            update(level[t], level[t - 1], before, gain, s, t == ITERS)
+
+
+def run_near(*args):
+    xa = args[N_EXT]
+    old, gain, level = unflatten(args[N_EXT + 1 :])
+    ext = (level[0], old, gain)
+    even = is_even("gx")
+    slots = halo_slots(even)
+    for k, (arr, s) in enumerate(slots):
+        ext[arr][0][s, TOP + W : TOP + W + Y, :] = xa[Y * k : Y * k + Y, :]
+    unpack_corners(ext, slots, xa, MAIN, lambda v: v)
+    run_side(even, old, gain, level, W)
+
+
+def run_far(*args):
+    xb, dz, dy = args[N_EXT : N_EXT + 3]
+    refs = args[N_EXT + 3 : 2 * N_EXT + 3]
+    coef, pressure, sem = args[2 * N_EXT + 3 :]
     old, gain, level = unflatten(refs)
     ext = (level[0], old, gain)
-    even = is_even("gx")
+    right = jnp.logical_not(is_even("gx"))
     keep_b = b_is_inside("gx")
 
-    def unpack(right, corner, base, fix):
-        z_tile = fix(corner[base + 8 * N_FACE : base + CORNER, :])
-        for k, (arr, s) in enumerate(halo_slots(right)):
-            put_edges(ext[arr][0], s, fix(corner[base + 8 * k : base + 8 * k + 8, :]))
-            put_rows(ext[arr][1], s, pltpu.roll(z_tile, Z - 8 * k - 4, 1))
-
-    for k, (arr, s) in enumerate(halo_slots(even)):
-        ext[arr][0][s, TOP + W : TOP + W + Y, :] = xa[Y * k : Y * k + Y, :]
-    unpack(even, xa, MAIN, lambda v: v)
-    unpack_face(ext, CUT, N_FACE, xb2)
-    unpack(jnp.logical_not(even), xbc, 0, lambda v: jnp.where(keep_b, v, 0.0))
-    for t in range(1, ITERS + 1):
-        before = level[t - 2] if t >= 2 else old
-        for s in [*range(t, t + W), *range(X + W - t, X + 2 * W - t)]:
-            update(level[t], level[t - 1], before, gain, s, t == ITERS)
+    def fix(v):
+        return jnp.where(keep_b, v, 0.0)
+
+    unpack_corners(ext, far_slots(right), xb, Y, fix)
+    level[1][0][jnp.where(right, X + 2 * W - 2, 1), TOP + W : TOP + W + Y, :] = fix(xb[:Y, :])
+    run_side(right, old, gain, level, W - 1)
     final = level[ITERS][0]
     copy = pltpu.make_async_copy(final, pressure, sem)
     copy.start()
@@ -315,17 +354,23 @@
     copy.wait()
 
 
-def place(mine, got, out):
+def place(mine, got, out, buf, sems):
     half, rows = X // 4, Y // 2
     low = iota((rows, Z), 1) < Z // 2
     keep = jnp.concatenate([mine[...]] * (rows // 8), axis=0) > 0.5
-    for t in range(got.shape[0] // 2):
-        for h in range(half):
+    copies = []
+    for h in range(half):
+        for t in range(got.shape[0] // 2):
             a = got[2 * t, h * rows : (h + 1) * rows, :]
             b = got[2 * t + 1, h * rows : (h + 1) * rows, :]
             at = slice(t * Z, (t + 1) * Z)
-            out[0, h, :, at] = jnp.where(keep, jnp.where(low, a, pltpu.roll(b, Z // 2, 1)), 0.0)
-            out[0, h + half, :, at] = jnp.where(keep, jnp.where(low, pltpu.roll(a, Z // 2, 1), b), 0.0)
+            buf[h, :, at] = jnp.where(keep, jnp.where(low, a, pltpu.roll(b, Z // 2, 1)), 0.0)
+            buf[h + half, :, at] = jnp.where(keep, jnp.where(low, pltpu.roll(a, Z // 2, 1), b), 0.0)
+        for i in (h, h + half):
+            copies.append(pltpu.make_async_copy(buf.at[i], out.at[0, i], sems.at[i]))
+            copies[-1].start()
+    for c in copies:
+        c.wait()
 
 
 def call(kernel, outs, *args, first=pltpu.VMEM, n_first=0, n_far=0, scratch=(), aliases=None, cost=1 << 18, flops=0):
@@ -361,31 +406,33 @@
         pack_y, [(n_y, 8, Z), (n_y, 8, Z)], *far, first=pltpu.HBM, n_first=3,
         scratch=[*edges, pltpu.SemaphoreType.DMA((6,))],
     )
-    (xb1,) = call(functools.partial(pack_face, 0, CUT), [(CUT, Y, Z)], p, q, m, ya)
+    (xf,) = call(pack_far, [(N_FAR, Y, Z)], p, q, m, ya)
     ya, yb = swap_a(ya, "gy"), swap_b(yb, "gy")
-    xb1 = swap_b(xb1, "gx")
+    xf = swap_b(xf, "gx")
     za, zb, yh = call(
         pack_z, [(2, ROWS, Z), (2, ROWS, Z), (3 * X, 8, Z)], p, q, m, ya, yb, flops=FLOPS_Z
     )
-    xb2, mine = call(
-        pack_face_last, [(N_FACE - CUT, Y, Z), (8, Z)], writer, p, q, m, yh, first=pltpu.SMEM, n_first=1
-    )
     za, zb = swap_a(za, "gz"), swap_b(zb, "gz")
-    xb2 = swap_b(xb2, "gx")
-    xa, xbc = call(
-        pack_x, [(MAIN + CORNER, Z), (CORNER, Z)], p, q, m, yh, za, zb, xb1, flops=FLOPS_X,
+    (mine,) = call(read_writer, [(8, Z)], writer, yh, first=pltpu.SMEM, n_first=1)
+    xa, xb = call(
+        pack_x, [(NEAR_ALL, Z), (FAR_LATE, Z)], p, q, m, yh, za, zb, xf, mine, flops=FLOPS_X,
         scratch=[pltpu.VMEM((3 * X, ROWS, Z), F32)],
     )
-    xa, xbc = swap_a(xa, "gx"), swap_b(xbc, "gx")
-    ext = call(run_inside, EXT, p, q, m, yh, za, zb, xb1, flops=FLOPS_IN)
+    xa, xb = swap_a(xa, "gx"), swap_b(xb, "gx")
+    same = {i: i for i in range(N_EXT)}
+    ext = call(run_inside, EXT, p, q, m, yh, za, zb, xf, flops=FLOPS_IN)
+    ext = call(run_near, EXT, *ext, xa, aliases=same, flops=FLOPS_IN)
     dz, dy = matrices()
     n = lax.axis_size("gz")
     *_, coef, pressure = call(
-        run_rest, [*EXT, (2 * Y, Z), (X, Y, Z)], *ext, xb2, xa, xbc, dz, dy,
-        aliases={i: i for i in range(N_EXT)}, cost=8 << 20, n_far=1, scratch=[pltpu.SemaphoreType.DMA],
+        run_far, [*EXT, (2 * Y, Z), (X, Y, Z)], *ext, xb, dz, dy,
+        aliases=same, n_far=1, scratch=[pltpu.SemaphoreType.DMA],
     )
     got = lax.all_to_all(jnp.broadcast_to(coef, (n, 2 * Y, Z)), "gz", 0, 0, tiled=True)
-    (out,) = call(place, [(1, X // 2, Y // 2, n * Z // 2)], mine, got)
+    size = (X // 2, Y // 2, n * Z // 2)
+    (out,) = call(
+        place, [(1, *size)], mine, got, n_far=1, scratch=[pltpu.VMEM(size, F32), pltpu.SemaphoreType.DMA((X // 2,))]
+    )
     return pressure, out
 
 

time: 42.8 us -> 41.9 us (0.979); the launches traced: 42.7 us -> 41.3 us
  blocking collectives: 18.8 us -> 16.5 us
    all_to_all x1, blocking collectives: 18.8 us -> 16.5 us  [per_device(): lax.all_to_all(jnp.broadcast_to(coef, (n, 2 * Y, Z)), 'gz', 0, 0, tiled=T...]
    ppermute x3, starting transfers between devices: 5.6 us -> 6.66 us  [swap_a(): lax.ppermute(v, axis, [(i, i ^ 1) for i in range(lax.axis_size(axis))])]
    ppermute x5 -> x4, starting transfers between devices: 2.61 us -> 1.94 us  [swap_b(): return lax.ppermute(v, names, pairs)]
    pallas_call x8 -> x9, Pallas kernels: 7.79 us -> 8.1 us  [call(): pl.pallas_call(kernel, out_shape=[jax.ShapeDtypeStruct(s, F32) for s in o...]
    ppermute x5 -> x4, waiting for transfers between devices: 2.81 us -> 2.8 us  [swap_b(): return lax.ppermute(v, names, pairs)]
  transfers between devices with their start and end apart: 8 -> 7, of which waited for: 3 -> 3; matrix products, arithmetic and copies ran while one was open for 0% -> 0% of each run, Pallas kernels for 8% -> 9%
where the time goes in v4:
time: 41.9 us; the launch traced here: 41.3 us
  blocking collectives  16.5 us (39%)
  starting transfers between devices  8.61 us (21%)
  Pallas kernels  8.1 us (19%)
  waiting for transfers between devices  6.56 us (16%)
  between operations  1.43 us (3%)
    all_to_all x1, blocking collectives, per_device(): lax.all_to_all(jnp.broadcast_to(coef, (n, 2 * Y, Z)), 'gz', 0, 0, tiled=T...  16.5 us
    pallas_call x9, Pallas kernels, call(): pl.pallas_call(kernel, out_shape=[jax.ShapeDtypeStruct(s, F32) for s in o...  8.1 us
    ppermute x3, starting transfers between devices, swap_a(): lax.ppermute(v, axis, [(i, i ^ 1) for i in range(lax.axis_size(axis))])  6.66 us
    ppermute x3, waiting for transfers between devices, swap_a(): lax.ppermute(v, axis, [(i, i ^ 1) for i in range(lax.axis_size(axis))])  3.77 us
    ppermute x4, waiting for transfers between devices, swap_b(): return lax.ppermute(v, names, pairs)  2.8 us
    ppermute x4, starting transfers between devices, swap_b(): return lax.ppermute(v, names, pairs)  1.94 us
  transfers between devices with their start and end apart: 7, of which 3 were waited for; matrix products, arithmetic and copies ran while one was open for 0% of the time, Pallas kernels for 9%

profile of v4, /device:TPU:72, one launch (start us, length us, event | category | flops | bytes accessed | tf_op | source)
XLA Modules:
  0.0 41.3 jit_solution(15666348257260410431)
XLA Ops:
  0.7 1.2 %shard_map.77 = (f32[24,8,128]{2,1,0:T(8,128)S(1)}, f32[24,8,128]{2,1,0:T(8,128)S(1)}) custom-call(f32[16,64,128]{2,1,0:T(8,128)} %p.9, f32[16,64,128]{2,1,0:T(8,128)} %q.9, s32[16,64,128]{2,1,0:T(8,128)} %m.9), custom_call_target="tpu_custom_call" | custom-call | bytes 262144 | tf_op jit(solution)/shard_map/pallas_call | solution.py:380
  1.9 1.7 %collective-permute-start.1 = (f32[24,8,128]{2,1,0:T(8,128)S(1)}, f32[24,8,128]{2,1,0:T(8,128)S(1)}, u32[]{:S(2)}, u32[]{:S(2)}) collective-permute-start(f32[24,8,128]{2,1,0:T(8,128)S(1)} %get-tuple-element.38), channel_id=1, source_target_pairs={{0,32},{8,16},{16,8},{24,56},{32,0},{40,48},{48,40},{56,24},{64,96... | collective-permute-start | bytes 294920 | tf_op jit(solution)/shard_map/ppermute | solution.py:35
  3.6 0.2 collective-permute-start.4
  3.8 2.8 %collective-permute-done.1.rb = f32[24,8,128]{2,1,0:T(8,128)S(1)} collective-permute-done((f32[24,8,128]{2,1,0:T(8,128)S(1)}, f32[24,8,128]{2,1,0:T(8,128)S(1)}, u32[]{:S(2)}, u32[]{:S(2)}) %collective-permute-start.1) | collective-permute-done | bytes 98336 | tf_op jit(solution)/shard_map/ppermute | solution.py:35
  6.6 1.6 %collective-permute-done.ra = f32[24,8,128]{2,1,0:T(8,128)S(1)} collective-permute-done((f32[24,8,128]{2,1,0:T(8,128)S(1)}, f32[24,8,128]{2,1,0:T(8,128)S(1)}, u32[]{:S(2)}, u32[]{:S(2)}) %collective-permute-start) | collective-permute-done | bytes 98336 | tf_op jit(solution)/shard_map/ppermute | solution.py:19
  8.2 0.5 %shard_map.78 = (f32[2,72,128]{2,1,0:T(8,128)S(1)}, f32[2,72,128]{2,1,0:T(8,128)S(1)}, f32[48,8,128]{2,1,0:T(8,128)S(1)}) custom-call(f32[16,64,128]{2,1,0:T(8,128)S(1)} %copy-done, f32[16,64,128]{2,1,0:T(8,128)S(1)} %copy-done.1, s32[16,64,128]{2,1,0:T(8,128)S(1)} %copy-done.2, f32[24,8,128]{2,1,0:T(8,128)S(1)} %collective-permute-done.ra, ...), custom_call_target="tpu_custom_call" | custom-call | flops 1000000000 | bytes 262144 | tf_op jit(solution)/shard_map/pallas_call | solution.py:380
  8.7 1.6 %collective-permute-start.2 = (f32[2,72,128]{2,1,0:T(8,128)S(1)}, f32[2,72,128]{2,1,0:T(8,128)S(1)}, u32[]{:S(2)}, u32[]{:S(2)}) collective-permute-start(f32[2,72,128]{2,1,0:T(8,128)S(1)} %get-tuple-element.40), channel_id=1, source_target_pairs={{0,1},{1,0},{2,3},{3,2},{4,5},{5,4},{6,7},{7,6},{8,9},{9,8},{10,11... | collective-permute-start | bytes 221192 | tf_op jit(solution)/shard_map/ppermute | solution.py:19
  10.2 0.0 collective-permute-start.3
  10.9 2.2 %collective-permute-done.2.ra = f32[2,72,128]{2,1,0:T(8,128)S(1)} collective-permute-done((f32[2,72,128]{2,1,0:T(8,128)S(1)}, f32[2,72,128]{2,1,0:T(8,128)S(1)}, u32[]{:S(2)}, u32[]{:S(2)}) %collective-permute-start.2) | collective-permute-done | bytes 73760 | tf_op jit(solution)/shard_map/ppermute | solution.py:19
  13.1 0.0 collective-permute-done.3.rb
  13.1 0.0 collective-permute-done.4.xf._
  13.1 0.5 %shard_map.82 = (f32[792,128]{1,0:T(8,128)S(1)}, f32[192,128]{1,0:T(8,128)S(1)}) custom-call(f32[16,64,128]{2,1,0:T(8,128)S(1)} %copy-done, f32[16,64,128]{2,1,0:T(8,128)S(1)} %copy-done.1, s32[16,64,128]{2,1,0:T(8,128)S(1)} %copy-done.2, f32[48,8,128]{2,1,0:T(8,128)S(1)} %get-tuple-element.39.yh._, f32[2,72,128]{2,1,0:T(8,128)S(1)} %collective-permute-done.2.ra, ...), custom_call_target="tpu_custom_call" | custom-call | flops 1000000000 | bytes 262144 | tf_op jit(solution)/shard_map/pallas_call | solution.py:380
  13.6 0.1 collective-permute-start.6
  13.7 5.1 %collective-permute-start.5 = (f32[792,128]{1,0:T(8,128)S(1)}, f32[792,128]{1,0:T(8,128)S(1)}, u32[]{:S(2)}, u32[]{:S(2)}) collective-permute-start(f32[792,128]{1,0:T(8,128)S(1)} %get-tuple-element.55), channel_id=1, source_target_pairs={{0,32},{32,0},{64,96},{96,64},{128,160},{160,128},{192,224},{224,1... | collective-permute-start | bytes 1216520 | tf_op jit(solution)/shard_map/ppermute | solution.py:19
  18.8 2.2 %shard_map.80 = (f32[24,88,128]{2,1,0:T(8,128)S(1)}, f32[24,88,128]{2,1,0:T(8,128)S(1)}, f32[24,88,128]{2,1,0:T(8,128)S(1)}, f32[24,88,128]{2,1,0:T(8,128)S(1)},...) custom-call(f32[16,64,128]{2,1,0:T(8,128)S(1)} %copy-done, ...), custom_call_target="tpu_custom_call" | custom-call | flops 10000000000 | bytes 262144 | tf_op jit(solution)/shard_map/pallas_call | solution.py:380
  21.0 0.0 collective-permute-done.5.args_13_
  21.0 0.0 copy-start.3
  21.0 0.0 copy-start.4
  21.0 0.9 %shard_map.83 = (f32[24,88,128]{2,1,0:T(8,128)S(1)}, f32[24,88,128]{2,1,0:T(8,128)S(1)}, f32[24,88,128]{2,1,0:T(8,128)S(1)}, f32[24,88,128]{2,1,0:T(8,128)S(1)},...) custom-call(f32[24,88,128]{2,1,0:T(8,128)S(1)} %get-tuple-element.42, ...), custom_call_target="tpu_custom_call", output_to_operand_aliasing={{0}: (0, {}), {1}: (1, {}), {2}: (2, {}), {3}: (3, {}), {4}... | custom-call | flops 10000000000 | bytes 262144 | tf_op jit(solution)/shard_map/pallas_call | solution.py:380
  21.9 0.0 collective-permute-done.6.args_13_
  21.9 0.0 copy-done.4
  22.0 1.8 %shard_map.84 = (f32[24,88,128]{2,1,0:T(8,128)S(1)}, f32[24,88,128]{2,1,0:T(8,128)S(1)}, f32[24,88,128]{2,1,0:T(8,128)S(1)}, f32[24,88,128]{2,1,0:T(8,128)S(1)},...) custom-call(f32[24,88,128]{2,1,0:T(8,128)S(1)} %get-tuple-element.56, ...), custom_call_target="tpu_custom_call", output_to_operand_aliasing={{0}: (0, {}), {1}: (1, {}), {2}: (2, {}), {3}: (3, {}), {4}... | custom-call | bytes 262144 | tf_op jit(solution)/shard_map/pallas_call | solution.py:380
  23.9 16.5 %all_to_all.5.got = f32[8,128,128]{2,1,0:T(8,128)S(1)} all-to-all(f32[8,128,128]{2,1,0:T(8,128)S(1)} %broadcast_in_dim.3), channel_id=1, replica_groups=mesh['gx'=8,'gy'=4,'gz'=8] {'gz'}, dimensions={0} | all-to-all | bytes 1048576 | tf_op jit(solution)/shard_map/all_to_all | solution.py:431
  40.4 0.9 %shard_map.85 = f32[1,8,32,512]{3,2,1,0:T(8,128)} custom-call(f32[8,128]{1,0:T(8,128)S(1)} %shard_map.81.__.mine, f32[8,128,128]{2,1,0:T(8,128)S(1)} %all_to_all.5.got), custom_call_target="tpu_custom_call" | custom-call | bytes 262144 | tf_op jit(solution)/shard_map/pallas_call | solution.py:380
  (11 shorter events, 0.1 us)
Async XLA Ops:
  0.6 2.9 %copy-start.2 = (s32[16,64,128]{2,1,0:T(8,128)S(1)}, s32[16,64,128]{2,1,0:T(8,128)}, u32[]{:S(2)}) copy-start(s32[16,64,128]{2,1,0:T(8,128)} %m.9) | copy-start | bytes 1572868
  0.6 2.9 %copy-start.1 = (f32[16,64,128]{2,1,0:T(8,128)S(1)}, f32[16,64,128]{2,1,0:T(8,128)}, u32[]{:S(2)}) copy-start(f32[16,64,128]{2,1,0:T(8,128)} %q.9) | copy-start | bytes 1572868
  0.6 2.9 %copy-start = (f32[16,64,128]{2,1,0:T(8,128)S(1)}, f32[16,64,128]{2,1,0:T(8,128)}, u32[]{:S(2)}) copy-start(f32[16,64,128]{2,1,0:T(8,128)} %p.9) | copy-start | bytes 1572868
  1.9 4.7 %collective-permute-start.1 = (f32[24,8,128]{2,1,0:T(8,128)S(1)}, f32[24,8,128]{2,1,0:T(8,128)S(1)}, u32[]{:S(2)}, u32[]{:S(2)}) collective-permute-start(f32[24,8,128]{2,1,0:T(8,128)S(1)} %get-tuple-element.38), channel_id=1, source_target_pairs={{0,32},{8,16},{16,8},{24,56},{32,0},{40,48},{48,40},{56,24},{64,96... | collective-permute-start | bytes 294920 | tf_op jit(solution)/shard_map/ppermute | solution.py:35
  3.5 4.6 %collective-permute-start = (f32[24,8,128]{2,1,0:T(8,128)S(1)}, f32[24,8,128]{2,1,0:T(8,128)S(1)}, u32[]{:S(2)}, u32[]{:S(2)}) collective-permute-start(f32[24,8,128]{2,1,0:T(8,128)S(1)} %get-tuple-element.37._), channel_id=1, source_target_pairs={{0,8},{8,0},{16,24},{24,16},{1,9},{9,1},{17,25},{25,17},{2,10},{10... | collective-permute-start | bytes 294920 | tf_op jit(solution)/shard_map/ppermute | solution.py:19
  3.6 9.5 %collective-permute-start.4 = (f32[7,64,128]{2,1,0:T(8,128)S(1)}, f32[7,64,128]{2,1,0:T(8,128)S(1)}, u32[]{:S(2)}, u32[]{:S(2)}) collective-permute-start(f32[7,64,128]{2,1,0:T(8,128)S(1)} %shard_map.79), channel_id=1, source_target_pairs={{0,8},{32,64},{64,32},{96,128},{128,96},{160,192},{192,160},{224,2... | collective-permute-start | bytes 688136 | tf_op jit(solution)/shard_map/ppermute | solution.py:35
  8.7 4.4 %collective-permute-start.2 = (f32[2,72,128]{2,1,0:T(8,128)S(1)}, f32[2,72,128]{2,1,0:T(8,128)S(1)}, u32[]{:S(2)}, u32[]{:S(2)}) collective-permute-start(f32[2,72,128]{2,1,0:T(8,128)S(1)} %get-tuple-element.40), channel_id=1, source_target_pairs={{0,1},{1,0},{2,3},{3,2},{4,5},{5,4},{6,7},{7,6},{8,9},{9,8},{10,11... | collective-permute-start | bytes 221192 | tf_op jit(solution)/shard_map/ppermute | solution.py:19
  10.2 2.9 %collective-permute-start.3 = (f32[2,72,128]{2,1,0:T(8,128)S(1)}, f32[2,72,128]{2,1,0:T(8,128)S(1)}, u32[]{:S(2)}, u32[]{:S(2)}) collective-permute-start(f32[2,72,128]{2,1,0:T(8,128)S(1)} %get-tuple-element.41), channel_id=1, source_target_pairs={{0,32},{1,2},{2,1},{3,4},{4,3},{5,6},{6,5},{7,39},{32,0},{33,34},{... | collective-permute-start | bytes 221192 | tf_op jit(solution)/shard_map/ppermute | solution.py:35
  13.6 8.3 %collective-permute-start.6 = (f32[192,128]{1,0:T(8,128)S(1)}, f32[192,128]{1,0:T(8,128)S(1)}, u32[]{:S(2)}, u32[]{:S(2)}) collective-permute-start(f32[192,128]{1,0:T(8,128)S(1)} %get-tuple-element.69), channel_id=1, source_target_pairs={{0,8},{32,64},{64,32},{96,128},{128,96},{160,192},{192,160},{224,2... | collective-permute-start | bytes 294920 | tf_op jit(solution)/shard_map/ppermute | solution.py:35
  13.7 7.3 %collective-permute-start.5 = (f32[792,128]{1,0:T(8,128)S(1)}, f32[792,128]{1,0:T(8,128)S(1)}, u32[]{:S(2)}, u32[]{:S(2)}) collective-permute-start(f32[792,128]{1,0:T(8,128)S(1)} %get-tuple-element.55), channel_id=1, source_target_pairs={{0,32},{32,0},{64,96},{96,64},{128,160},{160,128},{192,224},{224,1... | collective-permute-start | bytes 1216520 | tf_op jit(solution)/shard_map/ppermute | solution.py:19
  21.0 0.9 %copy-start.3 = (f32[128,256]{1,0:T(8,128)S(1)}, f32[128,256]{1,0:T(8,128)}, u32[]{:S(2)}) copy-start(f32[128,256]{1,0:T(8,128)} %constant.5.clone.args_15_) | copy-start | bytes 393220
  21.0 1.0 %copy-start.4 = (f32[256,128]{1,0:T(8,128)S(1)}, f32[256,128]{1,0:T(8,128)}, u32[]{:S(2)}) copy-start(f32[256,128]{1,0:T(8,128)} %constant.4.clone.args_14_) | copy-start | bytes 393220

commit v5 on v4

--- a/solution.py
+++ b/solution.py
@@ -86,16 +86,11 @@
     return [(0, p0 + k) for k in range(W - 1)] + [(a, q0 + k) for a in (1, 2) for k in range(W - 2)]
 
 
-def far_slots(right):
-    p0 = jnp.where(right, X + W, 1)
-    q0 = jnp.where(right, X + W, 2)
-    return [(0, p0 + k) for k in range(W - 1)] + [(a, q0 + k) for a in (1, 2) for k in range(W - 2)]
-
-
-def halo_slots(right):
-    p0 = jnp.where(right, X + W, 0)
-    q0 = jnp.where(right, X + W, 1)
-    return [(0, p0 + k) for k in range(W)] + [(a, q0 + k) for a in (1, 2) for k in range(W - 1)]
+def halo_items(right, width):
+    def at(k, n):
+        return jnp.where(right, k, n - 1 - k)
+
+    return [(0, at(k, width)) for k in range(width)] + [(a, at(k, width - 1)) for a in (1, 2) for k in range(width - 1)]
 
 
 def pack_y(p, q, m, ya, yb, ep, eq, em, sems):
@@ -162,7 +157,6 @@
 
 
 ROWS = Y + 2 * W
-SLOTS = X + 2 * W
 TOP = 8
 TALL = TOP + ROWS + 8
 MAIN = N_FACE * Y
@@ -193,7 +187,7 @@
     return (total * (1.0 / 3.0) - q[x]) * gain_of(m[x])
 
 
-def pack_x(p, q, m, yh, ra, rb, _, __, xa, xb, zh):
+def pack_x(p, q, m, yh, rb, ra, _, xa, xb, zh):
     lane = iota((ROWS, Z), 1)
     edge = set(range(W)) | set(range(X - W, X))
     for tile in range(2):
@@ -230,41 +224,44 @@
     ref[s, TOP : TOP + W, :] = v[W:]
 
 
-def update(out, now, old, gain, s, last_step):
+def views(pair, i):
+    return tuple(ref.at[i] for ref in pair)
+
+
+def update(out, centre, one_side, other_side, old, gain):
+    last_step = len(out) == 1
     size = 32 if last_step else 24
     first = iota((size, Z), 1) == 0
     last = iota((size, Z), 1) == Z - 1
     start, count = (TOP + W, Y) if last_step else (TOP, ROWS)
     for r in range(start, start + count, size):
         here, above, below = slice(r, r + size), slice(r - 1, r + size - 1), slice(r + 1, r + size + 1)
-        c, h = now[0][s, here, :], now[1][s, here, :]
+        c, h = centre[0][here, :], centre[1][here, :]
         cr, hr = pltpu.roll(c, 1, 1), pltpu.roll(h, 1, 1)
         cl, hl = pltpu.roll(c, Z - 1, 1), pltpu.roll(h, Z - 1, 1)
         along_z = (
             jnp.where(first, hr, cr) + jnp.where(last, hl, cl),
             jnp.where(first, cr, hr) + jnp.where(last, cl, hl),
         )
-        for i in range(1 if last_step else 2):
-            total = now[i][s - 1, here, :] + now[i][s + 1, here, :]
-            total = total + now[i][s, above, :] + now[i][s, below, :] + along_z[i]
-            v = (total * (1.0 / 3.0) - old[i][s, here, :]) * gain[i][s, here, :]
+        for i in range(len(out)):
+            total = one_side[i][here, :] + other_side[i][here, :]
+            total = total + centre[i][above, :] + centre[i][below, :] + along_z[i]
+            v = (total * (1.0 / 3.0) - old[i][here, :]) * gain[i][here, :]
             if last_step:
-                out[0][s - W, r - start : r - start + size, :] = v
+                out[i][r - start : r - start + size, :] = v
             else:
-                out[i][s, here, :] = v
-
-
-def unflatten(refs):
-    pairs = [(refs[2 * i], refs[2 * i + 1]) for i in range(2 + ITERS)] + [(refs[2 * (2 + ITERS)],)]
-    return pairs[0], pairs[1], pairs[2:]
-
-
-N_EXT = 2 * (2 + ITERS) + 1
-EXT = [(SLOTS, TALL, Z)] * (N_EXT - 1) + [(X, Y, Z)]
-
-
-def run_inside(p, q, m, yh, ra, rb, xf, *refs):
-    old, gain, level = unflatten(refs)
+                out[i][here, :] = v
+
+
+def pairs(refs):
+    return [tuple(refs[i : i + 2]) for i in range(0, len(refs), 2)]
+
+
+N_EXT = 2 * (2 + ITERS)
+
+
+def run_inside(p, q, m, yh, rb, ra, *refs):
+    (old, gain, *level), inner = pairs(refs[:N_EXT]), refs[N_EXT]
     ext = (level[0], old, gain)
     lane = iota((ROWS, Z), 1)
     for tile in range(2):
@@ -272,74 +269,91 @@
         for s in range(32):
             i = tile * 32 + s
             if i < 3 * X:
-                put_rows(ext[i // X][1], W + i % X, z_item(right, left, lane, s))
+                put_rows(ext[i // X][1], i % X, z_item(right, left, lane, s))
     for arr in range(3):
         for x in range(X):
-            ext[arr][0][W + x, TOP + W : TOP + W + Y, :] = load(p, q, m, arr, x)
-            put_edges(ext[arr][0], W + x, yh[arr * X + x])
-    keep_b = b_is_inside("gx")
-    for k, (arr, s) in enumerate(far_slots(jnp.logical_not(is_even("gx")))):
-        ext[arr][0][s, TOP + W : TOP + W + Y, :] = jnp.where(keep_b, xf[k], 0.0)
+            ext[arr][0][x, TOP + W : TOP + W + Y, :] = load(p, q, m, arr, x)
+            put_edges(ext[arr][0], x, yh[arr * X + x])
     for t in range(1, ITERS + 1):
         before = level[t - 2] if t >= 2 else old
-
-        def body(j, carry, t=t, before=before):
-            update(level[t], level[t - 1], before, gain, W + t + j, t == ITERS)
-            return carry
-
-        lax.fori_loop(0, X - 2 * t, body, 0, unroll=True)
-
-
-def unpack_corners(ext, slots, corner, base, fix):
-    end = base + 8 * len(slots)
+        for x in range(t, X - t):
+            out = (inner.at[x - W],) if t == ITERS else views(level[t], x)
+            now = [views(level[t - 1], x + d) for d in (0, -1, 1)]
+            update(out, *now, views(before, x), views(gain, x))
+
+
+def halo_scratch(width):
+    sizes = [width, width - 1, width - 1] + [W] * (ITERS - 1)
+    return [pltpu.VMEM((n, TALL, Z), F32) for n in sizes for _ in range(2)]
+
+
+N_HALO = 2 * (2 + ITERS)
+
+
+def unpack_corners(halo, items, corner, base, fix):
+    end = base + 8 * len(items)
     z_tile = fix(corner[end : end + ROWS, :])
-    for k, (arr, s) in enumerate(slots):
-        put_edges(ext[arr][0], s, fix(corner[base + 8 * k : base + 8 * k + 8, :]))
-        put_rows(ext[arr][1], s, pltpu.roll(z_tile, Z - 8 * k - 4, 1))
-
-
-def run_side(right, old, gain, level, first_count):
+    for k, (arr, i) in enumerate(items):
+        put_edges(halo[arr][0], i, fix(corner[base + 8 * k : base + 8 * k + 8, :]))
+        put_rows(halo[arr][1], i, pltpu.roll(z_tile, Z - 8 * k - 4, 1))
+
+
+def run_side(right, known, halo, final, given):
+    old, gain, *level = known
+    beyond, strip = halo[:3], halo[2:]
+
+    def own(e):
+        return jnp.where(right, X - 1 + e, -e)
+
+    def either(arr, inside, e):
+        return views(beyond[arr], e - 1) if e >= 1 else views(inside, own(e))
+
+    def at(t, e):
+        if t == 0:
+            return either(0, level[0], e)
+        return views(strip[t], e + t - 1) if e > -t else views(level[t], own(e))
+
     for t in range(1, ITERS + 1):
-        before = level[t - 2] if t >= 2 else old
-        for j in range(first_count if t == 1 else W):
-            s = jnp.where(right, X + W - t + j, W + t - 1 - j)
-            update(level[t], level[t - 1], before, gain, s, t == ITERS)
+        for e in range(1 - t, W + 1 - t - (given if t == 1 else 0)):
+            out = (final.at[jnp.where(right, W - 1 + e, -e)],) if t == ITERS else views(strip[t], e + t - 1)
+            before = at(t - 2, e) if t >= 2 else either(1, old, e)
+            update(out, at(t - 1, e), at(t - 1, e - 1), at(t - 1, e + 1), before, either(2, gain, e))
 
 
 def run_near(*args):
-    xa = args[N_EXT]
-    old, gain, level = unflatten(args[N_EXT + 1 :])
-    ext = (level[0], old, gain)
+    known, xa, final, halo = pairs(args[:N_EXT]), args[N_EXT], args[N_EXT + 1], pairs(args[N_EXT + 2 :])
     even = is_even("gx")
-    slots = halo_slots(even)
-    for k, (arr, s) in enumerate(slots):
-        ext[arr][0][s, TOP + W : TOP + W + Y, :] = xa[Y * k : Y * k + Y, :]
-    unpack_corners(ext, slots, xa, MAIN, lambda v: v)
-    run_side(even, old, gain, level, W)
+    items = halo_items(even, W)
+    for k, (arr, i) in enumerate(items):
+        halo[arr][0][i, TOP + W : TOP + W + Y, :] = xa[Y * k : Y * k + Y, :]
+    unpack_corners(halo, items, xa, MAIN, lambda v: v)
+    run_side(even, known, halo, final, 0)
 
 
 def run_far(*args):
-    xb, dz, dy = args[N_EXT : N_EXT + 3]
-    refs = args[N_EXT + 3 : 2 * N_EXT + 3]
-    coef, pressure, sem = args[2 * N_EXT + 3 :]
-    old, gain, level = unflatten(refs)
-    ext = (level[0], old, gain)
-    right = jnp.logical_not(is_even("gx"))
+    known, rest = pairs(args[:N_EXT]), args[N_EXT:]
+    inner, near, xf, xb, dz, dy, coef, far = rest[:8]
+    halo = pairs(rest[8:])
+    even = is_even("gx")
+    right = jnp.logical_not(even)
     keep_b = b_is_inside("gx")
 
     def fix(v):
         return jnp.where(keep_b, v, 0.0)
 
-    unpack_corners(ext, far_slots(right), xb, Y, fix)
-    level[1][0][jnp.where(right, X + 2 * W - 2, 1), TOP + W : TOP + W + Y, :] = fix(xb[:Y, :])
-    run_side(right, old, gain, level, W - 1)
-    final = level[ITERS][0]
-    copy = pltpu.make_async_copy(final, pressure, sem)
-    copy.start()
+    items = halo_items(right, W - 1)
+    for k, (arr, i) in enumerate(items):
+        halo[arr][0][i, TOP + W : TOP + W + Y, :] = fix(xf[k])
+    unpack_corners(halo, items, xb, Y, fix)
+    halo[3][0][W - 1, TOP + W : TOP + W + Y, :] = fix(xb[:Y, :])
+    run_side(right, known, halo, far, 1)
+    low = [jnp.where(even, far[i], near[i]) for i in range(W)]
+    high = [jnp.where(even, near[i], far[i]) for i in range(W)]
+    layers = [*low, *(inner[i] for i in range(X - 2 * W)), *high]
     rows = dct_rows()
     parts = []
     for b in range(X // 8):
-        f = [final[8 * b + i] for i in range(8)]
+        f = layers[8 * b : 8 * b + 8]
         plus = [f[i] + f[7 - i] for i in range(4)]
         minus = [f[i] - f[7 - i] for i in range(4)]
         for k in range(4):
@@ -351,14 +365,21 @@
     both = jnp.concatenate([left, right], axis=1)
     along_z = jnp.dot(both, dz[...], precision=lax.Precision.HIGHEST, preferred_element_type=F32)
     coef[...] = jnp.dot(dy[...], along_z, precision=lax.Precision.HIGHEST, preferred_element_type=F32)
-    copy.wait()
-
-
-def place(mine, got, out, buf, sems):
+
+
+def place(mine, got, inner, near, far, out, pressure, buf, sems):
+    even = is_even("gx")
+    near_at, far_at = jnp.where(even, X - W, 0), jnp.where(even, 0, X - W)
+    copies = [
+        pltpu.make_async_copy(inner, pressure.at[pl.ds(W, X - 2 * W)], sems.at[X // 2]),
+        pltpu.make_async_copy(near, pressure.at[pl.ds(near_at, W)], sems.at[X // 2 + 1]),
+        pltpu.make_async_copy(far, pressure.at[pl.ds(far_at, W)], sems.at[X // 2 + 2]),
+    ]
+    for c in copies:
+        c.start()
     half, rows = X // 4, Y // 2
     low = iota((rows, Z), 1) < Z // 2
     keep = jnp.concatenate([mine[...]] * (rows // 8), axis=0) > 0.5
-    copies = []
     for h in range(half):
         for t in range(got.shape[0] // 2):
             a = got[2 * t, h * rows : (h + 1) * rows, :]
@@ -373,7 +394,7 @@
         c.wait()
 
 
-def call(kernel, outs, *args, first=pltpu.VMEM, n_first=0, n_far=0, scratch=(), aliases=None, cost=1 << 18, flops=0):
+def call(kernel, outs, *args, first=pltpu.VMEM, n_first=0, n_far=0, scratch=(), flops=0):
     vm = pl.BlockSpec(memory_space=pltpu.VMEM)
     far = pl.BlockSpec(memory_space=pltpu.HBM)
     other = pl.BlockSpec(memory_space=first)
@@ -383,8 +404,7 @@
         in_specs=[other] * n_first + [vm] * (len(args) - n_first),
         out_specs=[vm] * (len(outs) - n_far) + [far] * n_far,
         scratch_shapes=list(scratch),
-        input_output_aliases=aliases or {},
-        cost_estimate=pl.CostEstimate(flops=flops, transcendentals=0, bytes_accessed=cost),
+        cost_estimate=pl.CostEstimate(flops=flops, transcendentals=0, bytes_accessed=1 << 18),
         compiler_params=pltpu.CompilerParams(vmem_limit_bytes=8 << 20),
     )(*args)
 
@@ -406,32 +426,33 @@
         pack_y, [(n_y, 8, Z), (n_y, 8, Z)], *far, first=pltpu.HBM, n_first=3,
         scratch=[*edges, pltpu.SemaphoreType.DMA((6,))],
     )
-    (xf,) = call(pack_far, [(N_FAR, Y, Z)], p, q, m, ya)
     ya, yb = swap_a(ya, "gy"), swap_b(yb, "gy")
-    xf = swap_b(xf, "gx")
     za, zb, yh = call(
         pack_z, [(2, ROWS, Z), (2, ROWS, Z), (3 * X, 8, Z)], p, q, m, ya, yb, flops=FLOPS_Z
     )
     za, zb = swap_a(za, "gz"), swap_b(zb, "gz")
+    (xf,) = call(pack_far, [(N_FAR, Y, Z)], p, q, m, yh)
+    xf = swap_b(xf, "gx")
     (mine,) = call(read_writer, [(8, Z)], writer, yh, first=pltpu.SMEM, n_first=1)
     xa, xb = call(
-        pack_x, [(NEAR_ALL, Z), (FAR_LATE, Z)], p, q, m, yh, za, zb, xf, mine, flops=FLOPS_X,
+        pack_x, [(NEAR_ALL, Z), (FAR_LATE, Z)], p, q, m, yh, zb, za, mine, flops=FLOPS_X,
         scratch=[pltpu.VMEM((3 * X, ROWS, Z), F32)],
     )
     xa, xb = swap_a(xa, "gx"), swap_b(xb, "gx")
-    same = {i: i for i in range(N_EXT)}
-    ext = call(run_inside, EXT, p, q, m, yh, za, zb, xf, flops=FLOPS_IN)
-    ext = call(run_near, EXT, *ext, xa, aliases=same, flops=FLOPS_IN)
+    *ext, inner = call(
+        run_inside, [(X, TALL, Z)] * N_EXT + [(X - 2 * W, Y, Z)], p, q, m, yh, zb, za, flops=FLOPS_IN
+    )
+    (near,) = call(run_near, [(W, Y, Z)], *ext, xa, scratch=halo_scratch(W))
     dz, dy = matrices()
     n = lax.axis_size("gz")
-    *_, coef, pressure = call(
-        run_far, [*EXT, (2 * Y, Z), (X, Y, Z)], *ext, xb, dz, dy,
-        aliases=same, n_far=1, scratch=[pltpu.SemaphoreType.DMA],
+    coef, far = call(
+        run_far, [(2 * Y, Z), (W, Y, Z)], *ext, inner, near, xf, xb, dz, dy, scratch=halo_scratch(W - 1)
     )
     got = lax.all_to_all(jnp.broadcast_to(coef, (n, 2 * Y, Z)), "gz", 0, 0, tiled=True)
     size = (X // 2, Y // 2, n * Z // 2)
-    (out,) = call(
-        place, [(1, *size)], mine, got, n_far=1, scratch=[pltpu.VMEM(size, F32), pltpu.SemaphoreType.DMA((X // 2,))]
+    out, pressure = call(
+        place, [(1, *size), (X, Y, Z)], mine, got, inner, near, far, n_far=2,
+        scratch=[pltpu.VMEM(size, F32), pltpu.SemaphoreType.DMA((X // 2 + 3,))],
     )
     return pressure, out
 

time: 41.9 us -> 41 us (0.979)
  waiting for transfers between devices: 6.56 us -> 4.11 us
  starting transfers between devices: 8.61 us -> 10.8 us
    ppermute x4, waiting for transfers between devices: 2.8 us -> 0.84 us  [swap_b(): return lax.ppermute(v, names, pairs)]
    ppermute x4, starting transfers between devices: 1.94 us -> 3.81 us  [swap_b(): return lax.ppermute(v, names, pairs)]
    ppermute x3, waiting for transfers between devices: 3.77 us -> 3.26 us  [swap_a(): lax.ppermute(v, axis, [(i, i ^ 1) for i in range(lax.axis_size(axis))])]
    all_to_all x1, blocking collectives: 16.5 us -> 16.1 us  [per_device(): lax.all_to_all(jnp.broadcast_to(coef, (n, 2 * Y, Z)), 'gz', 0, 0, tiled=T...]
where the time goes in v5:
time: 41 us; the launch traced here: 40.4 us
  blocking collectives  16.1 us (39%)
  starting transfers between devices  10.8 us (26%)
  Pallas kernels  7.87 us (19%)
  waiting for transfers between devices  4.11 us (10%)
  between operations  1.43 us (3%)
    all_to_all x1, blocking collectives, per_device(): lax.all_to_all(jnp.broadcast_to(coef, (n, 2 * Y, Z)), 'gz', 0, 0, tiled=T...  16.1 us
    pallas_call x9, Pallas kernels, call(): pl.pallas_call(kernel, out_shape=[jax.ShapeDtypeStruct(s, F32) for s in o...  7.87 us
    ppermute x3, starting transfers between devices, swap_a(): lax.ppermute(v, axis, [(i, i ^ 1) for i in range(lax.axis_size(axis))])  6.98 us
    ppermute x4, starting transfers between devices, swap_b(): return lax.ppermute(v, names, pairs)  3.81 us
    ppermute x3, waiting for transfers between devices, swap_a(): lax.ppermute(v, axis, [(i, i ^ 1) for i in range(lax.axis_size(axis))])  3.26 us
    ppermute x4, waiting for transfers between devices, swap_b(): return lax.ppermute(v, names, pairs)  0.84 us
  transfers between devices with their start and end apart: 7, of which 3 were waited for; matrix products, arithmetic and copies ran while one was open for 0% of the time, Pallas kernels for 9%

profile of v5, /device:TPU:72, one launch (start us, length us, event | category | flops | bytes accessed | tf_op | source)
XLA Modules:
  0.0 40.4 jit_solution(16301506356441589341)
XLA Ops:
  0.7 1.2 %shard_map.77 = (f32[24,8,128]{2,1,0:T(8,128)S(1)}, f32[24,8,128]{2,1,0:T(8,128)S(1)}) custom-call(f32[16,64,128]{2,1,0:T(8,128)} %p.9, f32[16,64,128]{2,1,0:T(8,128)} %q.9, s32[16,64,128]{2,1,0:T(8,128)} %m.9), custom_call_target="tpu_custom_call" | custom-call | bytes 262144 | tf_op jit(solution)/shard_map/pallas_call | solution.py:401
  1.9 0.5 %collective-permute-start = (f32[24,8,128]{2,1,0:T(8,128)S(1)}, f32[24,8,128]{2,1,0:T(8,128)S(1)}, u32[]{:S(2)}, u32[]{:S(2)}) collective-permute-start(f32[24,8,128]{2,1,0:T(8,128)S(1)} %get-tuple-element.26), channel_id=1, source_target_pairs={{0,8},{8,0},{16,24},{24,16},{1,9},{9,1},{17,25},{25,17},{2,10},{10... | collective-permute-start | bytes 294920 | tf_op jit(solution)/shard_map/ppermute | solution.py:19
  2.4 2.4 %collective-permute-start.1 = (f32[24,8,128]{2,1,0:T(8,128)S(1)}, f32[24,8,128]{2,1,0:T(8,128)S(1)}, u32[]{:S(2)}, u32[]{:S(2)}) collective-permute-start(f32[24,8,128]{2,1,0:T(8,128)S(1)} %get-tuple-element.27), channel_id=1, source_target_pairs={{0,32},{8,16},{16,8},{24,56},{32,0},{40,48},{48,40},{56,24},{64,96... | collective-permute-start | bytes 294920 | tf_op jit(solution)/shard_map/ppermute | solution.py:35
  4.8 1.8 %collective-permute-done.ra = f32[24,8,128]{2,1,0:T(8,128)S(1)} collective-permute-done((f32[24,8,128]{2,1,0:T(8,128)S(1)}, f32[24,8,128]{2,1,0:T(8,128)S(1)}, u32[]{:S(2)}, u32[]{:S(2)}) %collective-permute-start) | collective-permute-done | bytes 98336 | tf_op jit(solution)/shard_map/ppermute | solution.py:19
  6.6 0.8 %collective-permute-done.1.rb = f32[24,8,128]{2,1,0:T(8,128)S(1)} collective-permute-done((f32[24,8,128]{2,1,0:T(8,128)S(1)}, f32[24,8,128]{2,1,0:T(8,128)S(1)}, u32[]{:S(2)}, u32[]{:S(2)}) %collective-permute-start.1) | collective-permute-done | bytes 98336 | tf_op jit(solution)/shard_map/ppermute | solution.py:35
  7.4 0.5 %shard_map.78 = (f32[2,72,128]{2,1,0:T(8,128)S(1)}, f32[2,72,128]{2,1,0:T(8,128)S(1)}, f32[48,8,128]{2,1,0:T(8,128)S(1)}) custom-call(f32[16,64,128]{2,1,0:T(8,128)S(1)} %copy-done, f32[16,64,128]{2,1,0:T(8,128)S(1)} %copy-done.1, s32[16,64,128]{2,1,0:T(8,128)S(1)} %copy-done.2, f32[24,8,128]{2,1,0:T(8,128)S(1)} %collective-permute-done.ra, ...), custom_call_target="tpu_custom_call" | custom-call | flops 1000000000 | bytes 262144 | tf_op jit(solution)/shard_map/pallas_call | solution.py:401
  7.9 0.1 collective-permute-start.2
  8.0 3.0 %collective-permute-start.3 = (f32[2,72,128]{2,1,0:T(8,128)S(1)}, f32[2,72,128]{2,1,0:T(8,128)S(1)}, u32[]{:S(2)}, u32[]{:S(2)}) collective-permute-start(f32[2,72,128]{2,1,0:T(8,128)S(1)} %get-tuple-element.30), channel_id=1, source_target_pairs={{0,1},{1,0},{2,3},{3,2},{4,5},{5,4},{6,7},{7,6},{8,9},{9,8},{10,11... | collective-permute-start | bytes 221192 | tf_op jit(solution)/shard_map/ppermute | solution.py:19
  11.7 0.1 collective-permute-start.5
  11.8 0.0 collective-permute-done.2.rb
  11.8 1.5 %collective-permute-done.3.ra = f32[2,72,128]{2,1,0:T(8,128)S(1)} collective-permute-done((f32[2,72,128]{2,1,0:T(8,128)S(1)}, f32[2,72,128]{2,1,0:T(8,128)S(1)}, u32[]{:S(2)}, u32[]{:S(2)}) %collective-permute-start.3) | collective-permute-done | bytes 73760 | tf_op jit(solution)/shard_map/ppermute | solution.py:19
  13.3 0.5 %shard_map.81 = (f32[792,128]{1,0:T(8,128)S(1)}, f32[192,128]{1,0:T(8,128)S(1)}) custom-call(f32[16,64,128]{2,1,0:T(8,128)S(1)} %copy-done, f32[16,64,128]{2,1,0:T(8,128)S(1)} %copy-done.1, s32[16,64,128]{2,1,0:T(8,128)S(1)} %copy-done.2, f32[48,8,128]{2,1,0:T(8,128)S(1)} %get-tuple-element.28._.yh, f32[2,72,128]{2,1,0:T(8,128)S(1)} %collective-permute-done.2.rb, ...), custom_call_target="tpu_custom_call" | custom-call | flops 1000000000 | bytes 262144 | tf_op jit(solution)/shard_map/pallas_call | solution.py:401
  13.9 1.2 %collective-permute-start.6 = (f32[192,128]{1,0:T(8,128)S(1)}, f32[192,128]{1,0:T(8,128)S(1)}, u32[]{:S(2)}, u32[]{:S(2)}) collective-permute-start(f32[192,128]{1,0:T(8,128)S(1)} %get-tuple-element.45), channel_id=1, source_target_pairs={{0,8},{32,64},{64,32},{96,128},{128,96},{160,192},{192,160},{224,2... | collective-permute-start | bytes 294920 | tf_op jit(solution)/shard_map/ppermute | solution.py:35
  15.1 3.5 %collective-permute-start.4 = (f32[792,128]{1,0:T(8,128)S(1)}, f32[792,128]{1,0:T(8,128)S(1)}, u32[]{:S(2)}, u32[]{:S(2)}) collective-permute-start(f32[792,128]{1,0:T(8,128)S(1)} %get-tuple-element.44), channel_id=1, source_target_pairs={{0,32},{32,0},{64,96},{96,64},{128,160},{160,128},{192,224},{224,1... | collective-permute-start | bytes 1216520 | tf_op jit(solution)/shard_map/ppermute | solution.py:19
  18.6 2.1 %shard_map.80 = (f32[16,88,128]{2,1,0:T(8,128)S(1)}, f32[16,88,128]{2,1,0:T(8,128)S(1)}, f32[16,88,128]{2,1,0:T(8,128)S(1)}, f32[16,88,128]{2,1,0:T(8,128)S(1)},...) custom-call(f32[16,64,128]{2,1,0:T(8,128)S(1)} %copy-done, ...), custom_call_target="tpu_custom_call" | custom-call | flops 10000000000 | bytes 262144 | tf_op jit(solution)/shard_map/pallas_call | solution.py:401
  20.7 0.0 collective-permute-done.4.args_12_
  20.7 0.0 copy-start.3
  20.7 0.0 copy-start.4
  20.7 0.8 %shard_map.82.args_13_.near = f32[4,64,128]{2,1,0:T(8,128)S(1)} custom-call(f32[16,88,128]{2,1,0:T(8,128)S(1)} %get-tuple-element.31.args_0_, f32[16,88,128]{2,1,0:T(8,128)S(1)} %get-tuple-element.32.args_1_, f32[16,88,128]{2,1,0:T(8,128)S(1)} %get-tuple-element.33.args_2_, f32[16,88,128]{2,1,0:T(8,128)S(1)} %get-tuple-element.34.args_3_, ...), custom_call_target="tpu_custom_call" | custom-call | bytes 262144 | tf_op jit(solution)/shard_map/pallas_call | solution.py:401
  21.6 0.0 copy-done.3
  21.6 0.1 copy-done.4
  21.7 1.6 %shard_map.84 = (f32[128,128]{1,0:T(8,128)S(1)}, f32[4,64,128]{2,1,0:T(8,128)S(1)}) custom-call(f32[16,88,128]{2,1,0:T(8,128)S(1)} %get-tuple-element.31.args_0_, f32[16,88,128]{2,1,0:T(8,128)S(1)} %get-tuple-element.32.args_1_, f32[16,88,128]{2,1,0:T(8,128)S(1)} %get-tuple-element.33.args_2_, f32[16,88,128]{2,1,0:T(8,128)S(1)} %get-tuple-element.34.args_3_, ...), custom_call_target="tpu_custom_call" | custom-call | bytes 262144 | tf_op jit(solution)/shard_map/pallas_call | solution.py:401
  23.3 16.1 %all_to_all.5.got = f32[8,128,128]{2,1,0:T(8,128)S(1)} all-to-all(f32[8,128,128]{2,1,0:T(8,128)S(1)} %broadcast_in_dim.3), channel_id=1, replica_groups=mesh['gx'=8,'gy'=4,'gz'=8] {'gz'}, dimensions={0} | all-to-all | bytes 1048576 | tf_op jit(solution)/shard_map/all_to_all | solution.py:451
  39.4 1.1 %shard_map.85 = (f32[1,8,32,512]{3,2,1,0:T(8,128)}, f32[16,64,128]{2,1,0:T(8,128)}) custom-call(f32[8,128]{1,0:T(8,128)S(1)} %shard_map.79._.mine, f32[8,128,128]{2,1,0:T(8,128)S(1)} %all_to_all.5.got, f32[8,64,128]{2,1,0:T(8,128)S(1)} %get-tuple-element.43.args_12_.inner, f32[4,64,128]{2,1,0:T(8,128)S(1)} %shard_map.82.args_13_.near, ...), custom_call_target="tpu_custom_call" | custom-call | bytes 262144 | tf_op jit(solution)/shard_map/pallas_call | solution.py:401
  (11 shorter events, 0.1 us)
Async XLA Ops:
  0.6 6.8 %copy-start.2 = (s32[16,64,128]{2,1,0:T(8,128)S(1)}, s32[16,64,128]{2,1,0:T(8,128)}, u32[]{:S(2)}) copy-start(s32[16,64,128]{2,1,0:T(8,128)} %m.9) | copy-start | bytes 1572868
  0.6 6.8 %copy-start.1 = (f32[16,64,128]{2,1,0:T(8,128)S(1)}, f32[16,64,128]{2,1,0:T(8,128)}, u32[]{:S(2)}) copy-start(f32[16,64,128]{2,1,0:T(8,128)} %q.9) | copy-start | bytes 1572868
  0.6 6.8 %copy-start = (f32[16,64,128]{2,1,0:T(8,128)S(1)}, f32[16,64,128]{2,1,0:T(8,128)}, u32[]{:S(2)}) copy-start(f32[16,64,128]{2,1,0:T(8,128)} %p.9) | copy-start | bytes 1572868
  1.9 4.7 %collective-permute-start = (f32[24,8,128]{2,1,0:T(8,128)S(1)}, f32[24,8,128]{2,1,0:T(8,128)S(1)}, u32[]{:S(2)}, u32[]{:S(2)}) collective-permute-start(f32[24,8,128]{2,1,0:T(8,128)S(1)} %get-tuple-element.26), channel_id=1, source_target_pairs={{0,8},{8,0},{16,24},{24,16},{1,9},{9,1},{17,25},{25,17},{2,10},{10... | collective-permute-start | bytes 294920 | tf_op jit(solution)/shard_map/ppermute | solution.py:19
  2.4 5.0 %collective-permute-start.1 = (f32[24,8,128]{2,1,0:T(8,128)S(1)}, f32[24,8,128]{2,1,0:T(8,128)S(1)}, u32[]{:S(2)}, u32[]{:S(2)}) collective-permute-start(f32[24,8,128]{2,1,0:T(8,128)S(1)} %get-tuple-element.27), channel_id=1, source_target_pairs={{0,32},{8,16},{16,8},{24,56},{32,0},{40,48},{48,40},{56,24},{64,96... | collective-permute-start | bytes 294920 | tf_op jit(solution)/shard_map/ppermute | solution.py:35
  7.9 3.9 %collective-permute-start.2 = (f32[2,72,128]{2,1,0:T(8,128)S(1)}, f32[2,72,128]{2,1,0:T(8,128)S(1)}, u32[]{:S(2)}, u32[]{:S(2)}) collective-permute-start(f32[2,72,128]{2,1,0:T(8,128)S(1)} %get-tuple-element.29), channel_id=1, source_target_pairs={{0,32},{1,2},{2,1},{3,4},{4,3},{5,6},{6,5},{7,39},{32,0},{33,34},{... | collective-permute-start | bytes 221192 | tf_op jit(solution)/shard_map/ppermute | solution.py:35
  8.0 5.3 %collective-permute-start.3 = (f32[2,72,128]{2,1,0:T(8,128)S(1)}, f32[2,72,128]{2,1,0:T(8,128)S(1)}, u32[]{:S(2)}, u32[]{:S(2)}) collective-permute-start(f32[2,72,128]{2,1,0:T(8,128)S(1)} %get-tuple-element.30), channel_id=1, source_target_pairs={{0,1},{1,0},{2,3},{3,2},{4,5},{5,4},{6,7},{7,6},{8,9},{9,8},{10,11... | collective-permute-start | bytes 221192 | tf_op jit(solution)/shard_map/ppermute | solution.py:19
  11.7 9.9 %collective-permute-start.5 = (f32[7,64,128]{2,1,0:T(8,128)S(1)}, f32[7,64,128]{2,1,0:T(8,128)S(1)}, u32[]{:S(2)}, u32[]{:S(2)}) collective-permute-start(f32[7,64,128]{2,1,0:T(8,128)S(1)} %shard_map.83), channel_id=1, source_target_pairs={{0,8},{32,64},{64,32},{96,128},{128,96},{160,192},{192,160},{224,2... | collective-permute-start | bytes 688136 | tf_op jit(solution)/shard_map/ppermute | solution.py:35
  13.9 7.7 %collective-permute-start.6 = (f32[192,128]{1,0:T(8,128)S(1)}, f32[192,128]{1,0:T(8,128)S(1)}, u32[]{:S(2)}, u32[]{:S(2)}) collective-permute-start(f32[192,128]{1,0:T(8,128)S(1)} %get-tuple-element.45), channel_id=1, source_target_pairs={{0,8},{32,64},{64,32},{96,128},{128,96},{160,192},{192,160},{224,2... | collective-permute-start | bytes 294920 | tf_op jit(solution)/shard_map/ppermute | solution.py:35
  15.1 5.6 %collective-permute-start.4 = (f32[792,128]{1,0:T(8,128)S(1)}, f32[792,128]{1,0:T(8,128)S(1)}, u32[]{:S(2)}, u32[]{:S(2)}) collective-permute-start(f32[792,128]{1,0:T(8,128)S(1)} %get-tuple-element.44), channel_id=1, source_target_pairs={{0,32},{32,0},{64,96},{96,64},{128,160},{160,128},{192,224},{224,1... | collective-permute-start | bytes 1216520 | tf_op jit(solution)/shard_map/ppermute | solution.py:19
  20.7 0.9 %copy-start.3 = (f32[128,256]{1,0:T(8,128)S(1)}, f32[128,256]{1,0:T(8,128)}, u32[]{:S(2)}) copy-start(f32[128,256]{1,0:T(8,128)} %constant.5.clone.args_17_) | copy-start | bytes 393220
  20.7 1.0 %copy-start.4 = (f32[256,128]{1,0:T(8,128)S(1)}, f32[256,128]{1,0:T(8,128)}, u32[]{:S(2)}) copy-start(f32[256,128]{1,0:T(8,128)} %constant.4.clone.args_16_) | copy-start | bytes 393220

commit v6 on v5

--- a/solution.py
+++ b/solution.py
@@ -36,6 +36,7 @@
 
 
 FLOPS_Z, FLOPS_X, FLOPS_IN = 10**9, 10**9, 10**10
+FIRST = 6
 
 
 def dct_rows():
@@ -367,6 +368,10 @@
     coef[...] = jnp.dot(dy[...], along_z, precision=lax.Precision.HIGHEST, preferred_element_type=F32)
 
 
+def gather_order(place_in_group, n):
+    return (place_in_group + FIRST) % n
+
+
 def place(mine, got, inner, near, far, out, pressure, buf, sems):
     even = is_even("gx")
     near_at, far_at = jnp.where(even, X - W, 0), jnp.where(even, 0, X - W)
@@ -378,12 +383,14 @@
     for c in copies:
         c.start()
     half, rows = X // 4, Y // 2
+    n = got.shape[0]
+    source = {gather_order(i, n): i for i in range(n)}
     low = iota((rows, Z), 1) < Z // 2
     keep = jnp.concatenate([mine[...]] * (rows // 8), axis=0) > 0.5
     for h in range(half):
-        for t in range(got.shape[0] // 2):
-            a = got[2 * t, h * rows : (h + 1) * rows, :]
-            b = got[2 * t + 1, h * rows : (h + 1) * rows, :]
+        for t in range(n // 2):
+            a = got[source[2 * t], h * rows : (h + 1) * rows, :]
+            b = got[source[2 * t + 1], h * rows : (h + 1) * rows, :]
             at = slice(t * Z, (t + 1) * Z)
             buf[h, :, at] = jnp.where(keep, jnp.where(low, a, pltpu.roll(b, Z // 2, 1)), 0.0)
             buf[h + half, :, at] = jnp.where(keep, jnp.where(low, pltpu.roll(a, Z // 2, 1), b), 0.0)
@@ -448,7 +455,10 @@
     coef, far = call(
         run_far, [(2 * Y, Z), (W, Y, Z)], *ext, inner, near, xf, xb, dz, dy, scratch=halo_scratch(W - 1)
     )
-    got = lax.all_to_all(jnp.broadcast_to(coef, (n, 2 * Y, Z)), "gz", 0, 0, tiled=True)
+    group = [gather_order(i, n) for i in range(n)]
+    got = lax.all_to_all(
+        jnp.broadcast_to(coef, (n, 2 * Y, Z)), "gz", 0, 0, axis_index_groups=[group], tiled=True
+    )
     size = (X // 2, Y // 2, n * Z // 2)
     out, pressure = call(
         place, [(1, *size), (X, Y, Z)], mine, got, inner, near, far, n_far=2,

time: 41 us -> 40.4 us (0.985)
  blocking collectives: 16.1 us -> 15.3 us
    all_to_all x1, blocking collectives: 16.1 us -> 15.3 us  [per_device(): lax.all_to_all(jnp.broadcast_to(coef, (n, 2 * Y, Z)), 'gz', 0, 0, axis_in...]
where the time goes in v6:
time: 40.4 us; the launch traced here: 39.6 us
  blocking collectives  15.3 us (38%)
  starting transfers between devices  10.8 us (27%)
  Pallas kernels  7.87 us (19%)
  waiting for transfers between devices  4.11 us (10%)
  between operations  1.43 us (4%)
    all_to_all x1, blocking collectives, per_device(): lax.all_to_all(jnp.broadcast_to(coef, (n, 2 * Y, Z)), 'gz', 0, 0, axis_in...  15.3 us
    pallas_call x9, Pallas kernels, call(): pl.pallas_call(kernel, out_shape=[jax.ShapeDtypeStruct(s, F32) for s in o...  7.87 us
    ppermute x3, starting transfers between devices, swap_a(): lax.ppermute(v, axis, [(i, i ^ 1) for i in range(lax.axis_size(axis))])  6.98 us
    ppermute x4, starting transfers between devices, swap_b(): return lax.ppermute(v, names, pairs)  3.81 us
    ppermute x3, waiting for transfers between devices, swap_a(): lax.ppermute(v, axis, [(i, i ^ 1) for i in range(lax.axis_size(axis))])  3.26 us
    ppermute x4, waiting for transfers between devices, swap_b(): return lax.ppermute(v, names, pairs)  0.84 us
  transfers between devices with their start and end apart: 7, of which 3 were waited for; matrix products, arithmetic and copies ran while one was open for 0% of the time, Pallas kernels for 9%

profile of v6, /device:TPU:72, one launch (start us, length us, event | category | flops | bytes accessed | tf_op | source)
XLA Modules:
  0.0 39.6 jit_solution(16634110282180983274)
XLA Ops:
  0.7 1.2 %shard_map.77 = (f32[24,8,128]{2,1,0:T(8,128)S(1)}, f32[24,8,128]{2,1,0:T(8,128)S(1)}) custom-call(f32[16,64,128]{2,1,0:T(8,128)} %p.9, f32[16,64,128]{2,1,0:T(8,128)} %q.9, s32[16,64,128]{2,1,0:T(8,128)} %m.9), custom_call_target="tpu_custom_call" | custom-call | bytes 262144 | tf_op jit(solution)/shard_map/pallas_call | solution.py:408
  1.9 0.5 %collective-permute-start = (f32[24,8,128]{2,1,0:T(8,128)S(1)}, f32[24,8,128]{2,1,0:T(8,128)S(1)}, u32[]{:S(2)}, u32[]{:S(2)}) collective-permute-start(f32[24,8,128]{2,1,0:T(8,128)S(1)} %get-tuple-element.26), channel_id=1, source_target_pairs={{0,8},{8,0},{16,24},{24,16},{1,9},{9,1},{17,25},{25,17},{2,10},{10... | collective-permute-start | bytes 294920 | tf_op jit(solution)/shard_map/ppermute | solution.py:19
  2.4 2.4 %collective-permute-start.1 = (f32[24,8,128]{2,1,0:T(8,128)S(1)}, f32[24,8,128]{2,1,0:T(8,128)S(1)}, u32[]{:S(2)}, u32[]{:S(2)}) collective-permute-start(f32[24,8,128]{2,1,0:T(8,128)S(1)} %get-tuple-element.27), channel_id=1, source_target_pairs={{0,32},{8,16},{16,8},{24,56},{32,0},{40,48},{48,40},{56,24},{64,96... | collective-permute-start | bytes 294920 | tf_op jit(solution)/shard_map/ppermute | solution.py:35
  4.8 1.8 %collective-permute-done.ra = f32[24,8,128]{2,1,0:T(8,128)S(1)} collective-permute-done((f32[24,8,128]{2,1,0:T(8,128)S(1)}, f32[24,8,128]{2,1,0:T(8,128)S(1)}, u32[]{:S(2)}, u32[]{:S(2)}) %collective-permute-start) | collective-permute-done | bytes 98336 | tf_op jit(solution)/shard_map/ppermute | solution.py:19
  6.6 0.8 %collective-permute-done.1.rb = f32[24,8,128]{2,1,0:T(8,128)S(1)} collective-permute-done((f32[24,8,128]{2,1,0:T(8,128)S(1)}, f32[24,8,128]{2,1,0:T(8,128)S(1)}, u32[]{:S(2)}, u32[]{:S(2)}) %collective-permute-start.1) | collective-permute-done | bytes 98336 | tf_op jit(solution)/shard_map/ppermute | solution.py:35
  7.4 0.5 %shard_map.78 = (f32[2,72,128]{2,1,0:T(8,128)S(1)}, f32[2,72,128]{2,1,0:T(8,128)S(1)}, f32[48,8,128]{2,1,0:T(8,128)S(1)}) custom-call(f32[16,64,128]{2,1,0:T(8,128)S(1)} %copy-done, f32[16,64,128]{2,1,0:T(8,128)S(1)} %copy-done.1, s32[16,64,128]{2,1,0:T(8,128)S(1)} %copy-done.2, f32[24,8,128]{2,1,0:T(8,128)S(1)} %collective-permute-done.ra, ...), custom_call_target="tpu_custom_call" | custom-call | flops 1000000000 | bytes 262144 | tf_op jit(solution)/shard_map/pallas_call | solution.py:408
  7.9 0.1 collective-permute-start.2
  8.0 3.0 %collective-permute-start.3 = (f32[2,72,128]{2,1,0:T(8,128)S(1)}, f32[2,72,128]{2,1,0:T(8,128)S(1)}, u32[]{:S(2)}, u32[]{:S(2)}) collective-permute-start(f32[2,72,128]{2,1,0:T(8,128)S(1)} %get-tuple-element.30), channel_id=1, source_target_pairs={{0,1},{1,0},{2,3},{3,2},{4,5},{5,4},{6,7},{7,6},{8,9},{9,8},{10,11... | collective-permute-start | bytes 221192 | tf_op jit(solution)/shard_map/ppermute | solution.py:19
  11.7 0.1 collective-permute-start.5
  11.8 0.0 collective-permute-done.2.rb
  11.8 1.5 %collective-permute-done.3.ra = f32[2,72,128]{2,1,0:T(8,128)S(1)} collective-permute-done((f32[2,72,128]{2,1,0:T(8,128)S(1)}, f32[2,72,128]{2,1,0:T(8,128)S(1)}, u32[]{:S(2)}, u32[]{:S(2)}) %collective-permute-start.3) | collective-permute-done | bytes 73760 | tf_op jit(solution)/shard_map/ppermute | solution.py:19
  13.3 0.5 %shard_map.81 = (f32[792,128]{1,0:T(8,128)S(1)}, f32[192,128]{1,0:T(8,128)S(1)}) custom-call(f32[16,64,128]{2,1,0:T(8,128)S(1)} %copy-done, f32[16,64,128]{2,1,0:T(8,128)S(1)} %copy-done.1, s32[16,64,128]{2,1,0:T(8,128)S(1)} %copy-done.2, f32[48,8,128]{2,1,0:T(8,128)S(1)} %get-tuple-element.28._.yh, f32[2,72,128]{2,1,0:T(8,128)S(1)} %collective-permute-done.2.rb, ...), custom_call_target="tpu_custom_call" | custom-call | flops 1000000000 | bytes 262144 | tf_op jit(solution)/shard_map/pallas_call | solution.py:408
  13.9 1.2 %collective-permute-start.6 = (f32[192,128]{1,0:T(8,128)S(1)}, f32[192,128]{1,0:T(8,128)S(1)}, u32[]{:S(2)}, u32[]{:S(2)}) collective-permute-start(f32[192,128]{1,0:T(8,128)S(1)} %get-tuple-element.45), channel_id=1, source_target_pairs={{0,8},{32,64},{64,32},{96,128},{128,96},{160,192},{192,160},{224,2... | collective-permute-start | bytes 294920 | tf_op jit(solution)/shard_map/ppermute | solution.py:35
  15.1 3.5 %collective-permute-start.4 = (f32[792,128]{1,0:T(8,128)S(1)}, f32[792,128]{1,0:T(8,128)S(1)}, u32[]{:S(2)}, u32[]{:S(2)}) collective-permute-start(f32[792,128]{1,0:T(8,128)S(1)} %get-tuple-element.44), channel_id=1, source_target_pairs={{0,32},{32,0},{64,96},{96,64},{128,160},{160,128},{192,224},{224,1... | collective-permute-start | bytes 1216520 | tf_op jit(solution)/shard_map/ppermute | solution.py:19
  18.6 2.1 %shard_map.80 = (f32[16,88,128]{2,1,0:T(8,128)S(1)}, f32[16,88,128]{2,1,0:T(8,128)S(1)}, f32[16,88,128]{2,1,0:T(8,128)S(1)}, f32[16,88,128]{2,1,0:T(8,128)S(1)},...) custom-call(f32[16,64,128]{2,1,0:T(8,128)S(1)} %copy-done, ...), custom_call_target="tpu_custom_call" | custom-call | flops 10000000000 | bytes 262144 | tf_op jit(solution)/shard_map/pallas_call | solution.py:408
  20.7 0.0 copy-start.3
  20.7 0.0 copy-start.4
  20.7 0.8 %shard_map.82.args_13_.near = f32[4,64,128]{2,1,0:T(8,128)S(1)} custom-call(f32[16,88,128]{2,1,0:T(8,128)S(1)} %get-tuple-element.31.args_0_, f32[16,88,128]{2,1,0:T(8,128)S(1)} %get-tuple-element.32.args_1_, f32[16,88,128]{2,1,0:T(8,128)S(1)} %get-tuple-element.33.args_2_, f32[16,88,128]{2,1,0:T(8,128)S(1)} %get-tuple-element.34.args_3_, ...), custom_call_target="tpu_custom_call" | custom-call | bytes 262144 | tf_op jit(solution)/shard_map/pallas_call | solution.py:408
  21.6 0.0 collective-permute-done.5.args_14_
  21.6 0.0 copy-done.3
  21.6 0.1 copy-done.4
  21.7 1.6 %shard_map.84 = (f32[128,128]{1,0:T(8,128)S(1)}, f32[4,64,128]{2,1,0:T(8,128)S(1)}) custom-call(f32[16,88,128]{2,1,0:T(8,128)S(1)} %get-tuple-element.31.args_0_, f32[16,88,128]{2,1,0:T(8,128)S(1)} %get-tuple-element.32.args_1_, f32[16,88,128]{2,1,0:T(8,128)S(1)} %get-tuple-element.33.args_2_, f32[16,88,128]{2,1,0:T(8,128)S(1)} %get-tuple-element.34.args_3_, ...), custom_call_target="tpu_custom_call" | custom-call | bytes 262144 | tf_op jit(solution)/shard_map/pallas_call | solution.py:408
  23.3 15.3 %all_to_all.5.got = f32[8,128,128]{2,1,0:T(8,128)S(1)} all-to-all(f32[8,128,128]{2,1,0:T(8,128)S(1)} %broadcast_in_dim.3), channel_id=1, replica_groups={{6,7,0,1,2,3,4,5},{14,15,8,9,10,11,12,13},{22,23,16,17,18,19,20,21},{30..., dimensions={0} | all-to-all | bytes 1048576 | tf_op jit(solution)/shard_map/all_to_all | solution.py:459
  38.6 1.1 %shard_map.85 = (f32[1,8,32,512]{3,2,1,0:T(8,128)}, f32[16,64,128]{2,1,0:T(8,128)}) custom-call(f32[8,128]{1,0:T(8,128)S(1)} %shard_map.79._.mine, f32[8,128,128]{2,1,0:T(8,128)S(1)} %all_to_all.5.got, f32[8,64,128]{2,1,0:T(8,128)S(1)} %get-tuple-element.43.args_12_.inner, f32[4,64,128]{2,1,0:T(8,128)S(1)} %shard_map.82.args_13_.near, ...), custom_call_target="tpu_custom_call" | custom-call | bytes 262144 | tf_op jit(solution)/shard_map/pallas_call | solution.py:408
  (11 shorter events, 0.1 us)
Async XLA Ops:
  0.6 6.8 %copy-start.2 = (s32[16,64,128]{2,1,0:T(8,128)S(1)}, s32[16,64,128]{2,1,0:T(8,128)}, u32[]{:S(2)}) copy-start(s32[16,64,128]{2,1,0:T(8,128)} %m.9) | copy-start | bytes 1572868
  0.6 6.8 %copy-start.1 = (f32[16,64,128]{2,1,0:T(8,128)S(1)}, f32[16,64,128]{2,1,0:T(8,128)}, u32[]{:S(2)}) copy-start(f32[16,64,128]{2,1,0:T(8,128)} %q.9) | copy-start | bytes 1572868
  0.6 6.8 %copy-start = (f32[16,64,128]{2,1,0:T(8,128)S(1)}, f32[16,64,128]{2,1,0:T(8,128)}, u32[]{:S(2)}) copy-start(f32[16,64,128]{2,1,0:T(8,128)} %p.9) | copy-start | bytes 1572868
  1.9 4.7 %collective-permute-start = (f32[24,8,128]{2,1,0:T(8,128)S(1)}, f32[24,8,128]{2,1,0:T(8,128)S(1)}, u32[]{:S(2)}, u32[]{:S(2)}) collective-permute-start(f32[24,8,128]{2,1,0:T(8,128)S(1)} %get-tuple-element.26), channel_id=1, source_target_pairs={{0,8},{8,0},{16,24},{24,16},{1,9},{9,1},{17,25},{25,17},{2,10},{10... | collective-permute-start | bytes 294920 | tf_op jit(solution)/shard_map/ppermute | solution.py:19
  2.4 5.0 %collective-permute-start.1 = (f32[24,8,128]{2,1,0:T(8,128)S(1)}, f32[24,8,128]{2,1,0:T(8,128)S(1)}, u32[]{:S(2)}, u32[]{:S(2)}) collective-permute-start(f32[24,8,128]{2,1,0:T(8,128)S(1)} %get-tuple-element.27), channel_id=1, source_target_pairs={{0,32},{8,16},{16,8},{24,56},{32,0},{40,48},{48,40},{56,24},{64,96... | collective-permute-start | bytes 294920 | tf_op jit(solution)/shard_map/ppermute | solution.py:35
  7.9 3.9 %collective-permute-start.2 = (f32[2,72,128]{2,1,0:T(8,128)S(1)}, f32[2,72,128]{2,1,0:T(8,128)S(1)}, u32[]{:S(2)}, u32[]{:S(2)}) collective-permute-start(f32[2,72,128]{2,1,0:T(8,128)S(1)} %get-tuple-element.29), channel_id=1, source_target_pairs={{0,32},{1,2},{2,1},{3,4},{4,3},{5,6},{6,5},{7,39},{32,0},{33,34},{... | collective-permute-start | bytes 221192 | tf_op jit(solution)/shard_map/ppermute | solution.py:35
  8.0 5.3 %collective-permute-start.3 = (f32[2,72,128]{2,1,0:T(8,128)S(1)}, f32[2,72,128]{2,1,0:T(8,128)S(1)}, u32[]{:S(2)}, u32[]{:S(2)}) collective-permute-start(f32[2,72,128]{2,1,0:T(8,128)S(1)} %get-tuple-element.30), channel_id=1, source_target_pairs={{0,1},{1,0},{2,3},{3,2},{4,5},{5,4},{6,7},{7,6},{8,9},{9,8},{10,11... | collective-permute-start | bytes 221192 | tf_op jit(solution)/shard_map/ppermute | solution.py:19
  11.7 9.9 %collective-permute-start.5 = (f32[7,64,128]{2,1,0:T(8,128)S(1)}, f32[7,64,128]{2,1,0:T(8,128)S(1)}, u32[]{:S(2)}, u32[]{:S(2)}) collective-permute-start(f32[7,64,128]{2,1,0:T(8,128)S(1)} %shard_map.83), channel_id=1, source_target_pairs={{0,8},{32,64},{64,32},{96,128},{128,96},{160,192},{192,160},{224,2... | collective-permute-start | bytes 688136 | tf_op jit(solution)/shard_map/ppermute | solution.py:35
  13.9 7.7 %collective-permute-start.6 = (f32[192,128]{1,0:T(8,128)S(1)}, f32[192,128]{1,0:T(8,128)S(1)}, u32[]{:S(2)}, u32[]{:S(2)}) collective-permute-start(f32[192,128]{1,0:T(8,128)S(1)} %get-tuple-element.45), channel_id=1, source_target_pairs={{0,8},{32,64},{64,32},{96,128},{128,96},{160,192},{192,160},{224,2... | collective-permute-start | bytes 294920 | tf_op jit(solution)/shard_map/ppermute | solution.py:35
  15.1 5.6 %collective-permute-start.4 = (f32[792,128]{1,0:T(8,128)S(1)}, f32[792,128]{1,0:T(8,128)S(1)}, u32[]{:S(2)}, u32[]{:S(2)}) collective-permute-start(f32[792,128]{1,0:T(8,128)S(1)} %get-tuple-element.44), channel_id=1, source_target_pairs={{0,32},{32,0},{64,96},{96,64},{128,160},{160,128},{192,224},{224,1... | collective-permute-start | bytes 1216520 | tf_op jit(solution)/shard_map/ppermute | solution.py:19
  20.7 0.9 %copy-start.3 = (f32[128,256]{1,0:T(8,128)S(1)}, f32[128,256]{1,0:T(8,128)}, u32[]{:S(2)}) copy-start(f32[128,256]{1,0:T(8,128)} %constant.5.clone.args_17_) | copy-start | bytes 393220
  20.7 1.0 %copy-start.4 = (f32[256,128]{1,0:T(8,128)S(1)}, f32[256,128]{1,0:T(8,128)}, u32[]{:S(2)}) copy-start(f32[256,128]{1,0:T(8,128)} %constant.4.clone.args_16_) | copy-start | bytes 393220
